TPU v7x, 32 devices: a whole 2x2x4 slice. The times are simulated.
32 devices in a mesh: dp: 4 (over y, x), expert: 8 (over z, core).
Axes of the slice: x: 2, y: 2, z: 4, core: 2. Of those that a mesh axis runs over, the one named last changes fastest.
Arguments:
- tokens: bfloat16 [4096, 1024], P(('dp', 'expert')), may hold values from -6 to 6
- routes: int32 [4096, 8], P(('dp', 'expert')), may hold values from 0 to 15, all different within a row; in each aligned block of 128 rows (0 to 127, 128 to 255, ...) at most 96 rows name the same one
- gates: float32 [4096, 8], P(('dp', 'expert')), may hold values from 0.05 to 0.5
- cotangent: bfloat16 [4096, 1024], P(('dp', 'expert')), may hold values from -6 to 6
- partner: int32 [16], replicated, may hold values from 0 to 15, as said below
- w_gate_up: bfloat16 [16, 1024, 768], P('expert'), may hold values from -0.1875 to 0.1875
- w_down: bfloat16 [16, 1024, 384], P('expert'), may hold values from -0.3125 to 0.3125
Outputs:
- mixed: bfloat16 [4096, 1024], P(('dp', 'expert'))
- grad_tokens: bfloat16 [4096, 1024], P(('dp', 'expert'))
- grad_gate_up: float32 [16, 1024, 768], P('expert', 'dp')
- grad_down: float32 [16, 1024, 384], P('expert', 'dp')
Inputs may be any that keep to these rules, and one draw needn't show every extreme that they name: `routes`: A token names 8 different experts. In each device's block of 128 consecutive tokens no expert is named by more than 96 tokens, a bound that some block reaches. partner is a permutation that is its own inverse: each slot either keeps its expert or trades it with one slot of the device half the expert axis away (slot s lies on index s // 2 of the expert axis); each device trades at most one of its slots, and some slots trade in every draw.
All inputs are finite; a program needn't handle non-finite values.
Results may differ from a plain program's by a relative error of at most 0.01.
Values may be sent and summed in bfloat16 or wider, within the bound.
No kernel may reach another device: no remote copies, remote signals or barrier semaphores. Data moves between devices by JAX's collectives and lax.ppermute only.
A program may use at most 128 MiB of HBM per device.

v0:
```python
import jax
import jax.numpy as jnp
from jax import lax
from jax.sharding import PartitionSpec as P

grad_scale = 0.0625


def partner_2(block, axis, distance):
    count = lax.axis_size(axis)
    route = []
    for low in range(count):
        high = low | 1 << distance
        if high != low and high < count:
            route += [(low, high), (high, low)]
    return lax.ppermute(block, axis, route)


def table_lookup(table, keys):
    hits = keys[..., None] == jnp.arange(table.shape[0], dtype=jnp.int32)
    return jnp.sum(jnp.where(hits, table, 0), axis=-1)


def pick_slots(own_slots, received, moved, source_local):
    slots = own_slots.shape[0]
    index = jnp.where(moved, slots + source_local, jnp.arange(slots, dtype=jnp.int32))
    stacked = jnp.concatenate([own_slots, received], axis=0)
    return jnp.take(stacked, index, axis=0)


def local(tokens, routes, gates, cotangent, partner, w_gate_up, w_down):
    count_tokens, top_k = routes.shape
    width = tokens.shape[1]
    hidden_units = w_down.shape[2]
    n_expert = lax.axis_size("expert")
    exp_slots = w_gate_up.shape[0]
    experts_all = n_expert * exp_slots
    capacity = 3 * count_tokens * top_k // (2 * experts_all)
    pair_bit = n_expert.bit_length() - 2
    my_index = lax.axis_index("expert")
    slot_ids = my_index * exp_slots + jnp.arange(exp_slots, dtype=jnp.int32)
    partner_of = table_lookup(partner, slot_ids)
    moved = partner_of // exp_slots != my_index
    source_local = partner_of % exp_slots
    packed = jnp.concatenate([w_gate_up, w_down], axis=-1)
    target = table_lookup(partner, routes)
    received = partner_2(packed, "expert", pair_bit)
    packed = pick_slots(packed, received, moved, source_local)
    weight_gu = packed[:, :, : 2 * hidden_units]
    weight_dn = packed[:, :, 2 * hidden_units :]
    assign_total = count_tokens * top_k
    flat_slots = target.reshape(-1)
    hits = (flat_slots[:, None] == jnp.arange(experts_all, dtype=jnp.int32)).astype(jnp.int32)
    ranked = jnp.sum(jnp.cumsum(hits, axis=0) * hits, axis=1) - 1
    position = flat_slots * capacity + ranked
    filler = (
        jnp.full((experts_all * capacity,), assign_total, jnp.int32)
        .at[position]
        .set(jnp.arange(assign_total, dtype=jnp.int32))
    )
    buffer_shape = (n_expert, exp_slots, capacity, width)
    token_pad = jnp.concatenate([tokens, jnp.zeros((1, width), tokens.dtype)], axis=0)
    sending_rows = token_pad[filler // top_k].reshape(buffer_shape)
    arrived = lax.all_to_all(sending_rows, "expert", split_axis=0, concat_axis=0, tiled=True)
    pre_act = jnp.einsum("sjcd,jdf->sjcf", arrived, weight_gu, preferred_element_type=jnp.float32)
    gate_pre = pre_act[..., :hidden_units]
    up_pre = pre_act[..., hidden_units:]
    sigmoid_gate = jax.nn.sigmoid(gate_pre)
    silu_gate = gate_pre * sigmoid_gate
    hidden = (silu_gate * up_pre).astype(jnp.bfloat16)
    expert_out = jnp.einsum(
        "sjcf,jdf->sjcd", hidden, weight_dn, preferred_element_type=jnp.float32
    ).astype(jnp.bfloat16)
    returned = lax.all_to_all(expert_out, "expert", split_axis=0, concat_axis=0, tiled=True)
    picked = returned.reshape(-1, width)[position].reshape(count_tokens, top_k, width)
    mixed = jnp.einsum("tk,tkd->td", gates, picked.astype(jnp.float32)).astype(jnp.bfloat16)
    grad_out = (
        (gates[:, :, None] * cotangent[:, None, :].astype(jnp.float32))
        .astype(jnp.bfloat16)
        .reshape(assign_total, width)
    )
    grad_pad = jnp.concatenate([grad_out, jnp.zeros((1, width), jnp.bfloat16)], axis=0)
    grad_arrived = lax.all_to_all(
        grad_pad[filler].reshape(buffer_shape), "expert", split_axis=0, concat_axis=0, tiled=True
    )
    grad_hidden = jnp.einsum(
        "sjcd,jdf->sjcf", grad_arrived, weight_dn, preferred_element_type=jnp.float32
    )
    grad_down = jnp.einsum(
        "sjcf,sjcd->jdf", hidden, grad_arrived, preferred_element_type=jnp.float32
    )
    grad_gate = grad_hidden * up_pre * sigmoid_gate * (1.0 + gate_pre * (1.0 - sigmoid_gate))
    grad_up = grad_hidden * silu_gate
    grad_pre = jnp.concatenate([grad_gate, grad_up], axis=-1).astype(jnp.bfloat16)
    grad_rows = jnp.einsum(
        "sjcf,jdf->sjcd", grad_pre, weight_gu, preferred_element_type=jnp.float32
    ).astype(jnp.bfloat16)
    grad_gu = jnp.einsum("sjcd,sjcf->jdf", arrived, grad_pre, preferred_element_type=jnp.float32)
    grad_back = lax.all_to_all(grad_rows, "expert", split_axis=0, concat_axis=0, tiled=True)
    gathered = grad_back.reshape(-1, width)[position].reshape(count_tokens, top_k, width)
    grad_tokens = jnp.sum(gathered.astype(jnp.float32), axis=1).astype(jnp.bfloat16)
    terms = jnp.concatenate([grad_gu, grad_down], axis=-1) * grad_scale
    reduced = lax.psum_scatter(terms, "dp", scatter_dimension=1, tiled=True)
    return (
        mixed,
        grad_tokens,
        reduced[:, :, : 2 * hidden_units],
        reduced[:, :, 2 * hidden_units :],
    )


def solution(mesh):
    in_specs = (
        P(("dp", "expert"), None),
        P(("dp", "expert"), None),
        P(("dp", "expert"), None),
        P(("dp", "expert"), None),
        P(),
        P("expert", None, None),
        P("expert", None, None),
    )
    out_specs = (
        P(("dp", "expert"), None),
        P(("dp", "expert"), None),
        P("expert", "dp", None),
        P("expert", "dp", None),
    )
    return jax.shard_map(local, mesh=mesh, in_specs=in_specs, out_specs=out_specs, check_vma=False)
```

profile of v0, /device:TPU:0, one launch (start us, length us, event | category | flops | bytes accessed | tf_op | source)
XLA Modules:
  0.0 572.0 jit_solution(12115314040941407603)
XLA Ops:
  8.5 4.5 reduce-window.6
  13.5 4.3 scatter_custom_fusion
  18.8 5.8 %gather_fusion = bf16[1536,1024]{1,0:T(8,128)(2,1)} fusion(bf16[129,1024]{1,0:T(8,128)(2,1)S(1)} %concatenate.21, s32[2048]{0:T(1024)S(1)} %get-tuple-element.26), kind=kCustom, calls=%fused_computation | custom fusion | bytes 6297600 | tf_op jit(solution)/shard_map/gather | solution.py:63
  24.6 6.6 %all-to-all-start = ((bf16[8,2,96,1024]{3,2,1,0:T(8,128)(2,1)}), bf16[8,2,96,1024]{3,2,1,0:T(8,128)(2,1)}, u32[]{:S(2)}, u32[]{:S(2)}) async-start(bf16[8,2,96,1024]{3,2,1,0:T(8,128)(2,1)} %bitcast.10), calls=%async_computation | async-start | bytes 6291456 | tf_op jit(solution)/shard_map/all_to_all | solution.py:64
  38.3 5.8 %gather_fusion.2 = bf16[1536,1024]{1,0:T(8,128)(2,1)} fusion(bf16[1025,1024]{1,0:T(8,128)(2,1)S(1)} %concatenate.22, s32[2048]{0:T(1024)S(1)} %get-tuple-element.25), kind=kCustom, calls=%fused_computation.2 | custom fusion | bytes 6297600 | tf_op jit(solution)/shard_map/gather | solution.py:84
  44.1 160.4 %all-to-all-done = bf16[8,2,96,1024]{3,2,1,0:T(8,128)(2,1)} async-done(((bf16[8,2,96,1024]{3,2,1,0:T(8,128)(2,1)}), bf16[8,2,96,1024]{3,2,1,0:T(8,128)(2,1)}, u32[]{:S(2)}, u32[]{:S(2)}) %all-to-all-start) | async-done | bytes 3145760 | tf_op jit(solution)/shard_map/all_to_all | solution.py:64
  204.5 3.8 all-to-all-start.2
  208.7 130.6 %collective-permute-done = bf16[2,1024,1152]{2,1,0:T(8,128)(2,1)} collective-permute-done((bf16[2,1024,1152]{2,1,0:T(8,128)(2,1)}, bf16[2,1024,1152]{2,1,0:T(8,128)(2,1)}, u32[]{:S(2)}, u32[]{:S(2)}) %collective-permute-start) | collective-permute-done | bytes 4718624 | tf_op jit(solution)/shard_map/ppermute | solution.py:16
  339.4 4.5 pad_maximum_fusion
  343.9 4.2 gather_fusion.5
  348.0 5.8 %fusion = bf16[4,1024,640]{2,1,0:T(8,128)(2,1)} fusion(bf16[2,1024,1152]{2,1,0:T(8,128)(2,1)} %constant_dynamic-update-slice_fusion, bf16[2,1024,1152]{2,1,0:T(8,128)(2,1)} %collective-permute-done), kind=kLoop, calls=%fused_computation.10 | loop fusion | flops 2621440 | bytes 14680064 | tf_op jit(solution)/shard_map/concatenate | solution.py:27
  353.9 4.9 gather_fusion.4
  358.8 3.4 maximum_select_fusion
  364.3 6.8 %fusion.13 = f32[8,2,96,768]{3,2,0,1:T(8,128)} fusion(bf16[8,2,96,1024]{3,2,1,0:T(8,128)(2,1)} %all-to-all-done, bf16[2,1024,1152]{2,1,0:T(8,128)(2,1)S(1)} %maximum_select_fusion), kind=kOutput, calls=%fused_computation.35 | convolution fusion | flops 2415919104 | bytes 11010048 | tf_op jit(solution)/shard_map/sjcd,jdf->sjcf/dot_general | solution.py:65
  372.5 4.7 fusion.9
  379.0 6.5 %convolution_bitcast_fusion = f32[2,1024,768]{1,2,0:T(8,128)} fusion(bf16[8,2,96,1024]{3,2,1,0:T(8,128)(2,1)} %all-to-all-done, bf16[8,2,96,384]{3,2,0,1:T(8,128)(2,1)S(1)} %get-tuple-element.21, bf16[8,2,96,384]{3,2,0,1:T(8,128)(2,1)S(1)} %get-tuple-element.20), kind=kOutput, calls=%fused_computation.22 | convolution fusion | flops 2420637696 | bytes 11796480 | tf_op jit(solution)/shard_map/sjcd,sjcf->jdf/dot_general | solution.py:98
  385.6 8.3 %maximum_multiply_fusion = f32[2,1024,1152]{1,2,0:T(8,128)} fusion(f32[2,1024,384]{1,2,0:T(8,128)S(1)} %convolution_bitcast_fusion.1, f32[2,1024,768]{1,2,0:T(8,128)} %convolution_bitcast_fusion), kind=kLoop, calls=%fused_computation.9 | loop fusion | flops 4718592 | bytes 18874368 | tf_op jit(solution)/shard_map/mul | solution.py:102
  400.4 3.9 all-to-all-start.1
  404.3 5.4 convert_bitcast_fusion
  412.0 63.6 %all-to-all-done.1 = bf16[8,2,96,1024]{3,2,1,0:T(8,128)(2,1)S(1)} async-done(((bf16[8,2,96,1024]{3,2,1,0:T(8,128)(2,1)}), bf16[8,2,96,1024]{3,2,1,0:T(8,128)(2,1)S(1)}, u32[]{:S(2)}, u32[]{:S(2)}) %all-to-all-start.1) | async-done | bytes 3145760 | tf_op jit(solution)/shard_map/all_to_all | solution.py:74
  475.5 4.5 all-to-all-start.3
  480.2 5.3 gather_fusion.1
  488.6 63.0 %all-to-all-done.3 = bf16[8,2,96,1024]{3,2,1,0:T(8,128)(2,1)} async-done(((bf16[8,2,96,1024]{3,2,1,0:T(8,128)(2,1)}), bf16[8,2,96,1024]{3,2,1,0:T(8,128)(2,1)}, u32[]{:S(2)}, u32[]{:S(2)}) %all-to-all-start.3) | async-done | bytes 3145760 | tf_op jit(solution)/shard_map/all_to_all | solution.py:99
  551.5 7.3 %gather_fusion.3 = bf16[1024,1024]{1,0:T(8,128)(2,1)S(1)} fusion(bf16[1536,1024]{1,0:T(8,128)(2,1)} %bitcast.23, s32[1024]{0:T(1024)S(1)} %broadcast_clamp_fusion), kind=kCustom, calls=%fused_computation.3 | custom fusion | bytes 4198400 | tf_op jit(solution)/shard_map/gather | solution.py:100
  (73 shorter events, 33.7 us)
Async XLA Ops:
  24.6 6.6 %copy-start.1 = (bf16[2,1024,768]{2,1,0:T(8,128)(2,1)S(1)}, bf16[2,1024,768]{2,1,0:T(8,128)(2,1)}, u32[]{:S(2)}) copy-start(bf16[2,1024,768]{2,1,0:T(8,128)(2,1)} %param.12) | copy-start | bytes 9437188
  24.6 179.8 %all-to-all-start = ((bf16[8,2,96,1024]{3,2,1,0:T(8,128)(2,1)}), bf16[8,2,96,1024]{3,2,1,0:T(8,128)(2,1)}, u32[]{:S(2)}, u32[]{:S(2)}) async-start(bf16[8,2,96,1024]{3,2,1,0:T(8,128)(2,1)} %bitcast.10), calls=%async_computation | async-start | bytes 6291456 | tf_op jit(solution)/shard_map/all_to_all | solution.py:64
  31.2 2.0 copy-start.2
  33.2 4.3 copy-start.5
  33.3 4.3 copy-start.6
  34.6 304.7 %collective-permute-start = (bf16[2,1024,1152]{2,1,0:T(8,128)(2,1)}, bf16[2,1024,1152]{2,1,0:T(8,128)(2,1)}, u32[]{:S(2)}, u32[]{:S(2)}) collective-permute-start(bf16[2,1024,1152]{2,1,0:T(8,128)(2,1)} %constant_dynamic-update-slice_fusion), channel_id=1, source_target_pairs={{0,4},{4,0},{1,5},{5,1},{2,6},{6,2},{3,7},{7,3},{8,12},{12,8},{9,1... | collective-permute-start | bytes 14155784 | tf_op jit(solution)/shard_map/ppermute | solution.py:16
  204.4 4.0 copy-start.7
  204.5 168.0 %all-to-all-start.2 = ((bf16[8,2,96,1024]{3,2,1,0:T(8,128)(2,1)}), bf16[8,2,96,1024]{3,2,1,0:T(8,128)(2,1)S(1)}, u32[]{:S(2)}, u32[]{:S(2)}) async-start(bf16[8,2,96,1024]{3,2,1,0:T(8,128)(2,1)} %bitcast.94), calls=%async_computation.2 | async-start | bytes 6291456 | tf_op jit(solution)/shard_map/all_to_all | solution.py:83
  208.2 352.7 %reduce-scatter.2.cloned.1.call-start = ((), (), s32[]{:S(2)}) async-start(), calls=%async_computation.5 | async-start | bytes 11796480 | tf_op jit(solution)/shard_map/reduce_scatter | solution.py:103
  362.2 2.1 copy-start
  377.2 1.5 copy-start.3
  377.2 1.5 copy-start.8
  377.2 1.8 copy-start.9
  393.8 1.3 copy-start.4
  400.4 75.1 %all-to-all-start.1 = ((bf16[8,2,96,1024]{3,2,1,0:T(8,128)(2,1)}), bf16[8,2,96,1024]{3,2,1,0:T(8,128)(2,1)S(1)}, u32[]{:S(2)}, u32[]{:S(2)}) async-start(bf16[8,2,96,1024]{3,2,1,0:T(8,128)(2,1)} %copy.44), calls=%async_computation.1 | async-start | bytes 6291456 | tf_op jit(solution)/shard_map/all_to_all | solution.py:74
  475.5 76.0 %all-to-all-start.3 = ((bf16[8,2,96,1024]{3,2,1,0:T(8,128)(2,1)}), bf16[8,2,96,1024]{3,2,1,0:T(8,128)(2,1)}, u32[]{:S(2)}, u32[]{:S(2)}) async-start(bf16[8,2,96,1024]{3,2,1,0:T(8,128)(2,1)} %copy.47), calls=%async_computation.3 | async-start | bytes 6291456 | tf_op jit(solution)/shard_map/all_to_all | solution.py:99
  560.9 1.4 slice-start
  562.4 1.6 slice-start.1
Sparse Core Ops, SparseCore 0:
  394.0 93.8 reduce-scatter.1
where the time goes:
time: 573 us; the launch traced here: 572 us
  waiting for transfers between devices  419 us (73%)
  local copies, waits for them, and re-layouts  56.2 us (10%)
  matrix products  30.5 us (5%)
  other arithmetic  30.2 us (5%)
  starting transfers between devices  21.8 us (4%)
  between operations  14.3 us (2%)
    all_to_all x1, waiting for transfers between devices, local(): lax.all_to_all(sending_rows, 'expert', split_axis=0, concat_axis=0, tiled...  160 us
    ppermute x1, waiting for transfers between devices, partner_2(): return lax.ppermute(block, axis, route)  131 us
    all_to_all x1, waiting for transfers between devices, local(): lax.all_to_all(expert_out, 'expert', split_axis=0, concat_axis=0, tiled=T...  63.6 us
    all_to_all x1, waiting for transfers between devices, local(): lax.all_to_all(grad_rows, 'expert', split_axis=0, concat_axis=0, tiled=True)  63 us
  transfers between devices with their start and end apart: 6, of which 5 were waited for; matrix products, arithmetic and copies ran while one was open for 12% of the time, Pallas kernels for 0%

commit v1 on v0

--- a/solution.py
+++ b/solution.py
@@ -28,7 +28,7 @@
     return jnp.take(stacked, index, axis=0)
 
 
-def local(tokens, routes, gates, cotangent, partner, w_gate_up, w_down):
+def routed(tokens, routes, gates, cotangent, partner, w_gate_up, w_down):
     count_tokens, top_k = routes.shape
     width = tokens.shape[1]
     hidden_units = w_down.shape[2]
@@ -109,6 +109,138 @@
     )
 
 
+def swap_with(block, axis, mask):
+    return lax.ppermute(block, axis, [(i, i ^ mask) for i in range(lax.axis_size(axis))])
+
+
+def gather_relative(block):
+    n_expert = lax.axis_size("expert")
+    column = [block] + [swap_with(block, "expert", mask) for mask in range(2, n_expert, 2)]
+    column = jnp.stack(column)
+    return jnp.stack([column, swap_with(column, "expert", 1)], axis=1).reshape(-1, block.shape[-1])
+
+
+def reduce_relative(partial, count_tokens):
+    n_expert = lax.axis_size("expert")
+    terms = partial.reshape(n_expert // 2, 2, count_tokens, -1)
+    other = swap_with(terms[:, 1].astype(jnp.bfloat16), "expert", 1)
+    pair = terms[:, 0].astype(jnp.float32) + other.astype(jnp.float32)
+    total = pair[0]
+    for step in range(1, n_expert // 2):
+        sent = swap_with(pair[step].astype(jnp.bfloat16), "expert", 2 * step)
+        total = total + sent.astype(jnp.float32)
+    return total.astype(jnp.bfloat16)
+
+
+def relative(array, index):
+    count = array.shape[0]
+    for bit in range(count.bit_length() - 1):
+        parts = array.reshape((count >> bit + 1, 2, 1 << bit) + array.shape[1:])
+        array = jnp.where((index >> bit) & 1 == 1, parts[:, ::-1], parts).reshape(array.shape)
+    return array
+
+
+def scatter_sum(terms):
+    me = lax.axis_index("dp")
+    low = me & 1
+    high = me >> 1
+    by = terms.reshape((2, 2) + terms.shape[1:])
+    pick = lambda array, axis, at: lax.dynamic_index_in_dim(array, at, axis, keepdims=False)
+    first, second = by[:, :, 0], by[:, :, 1]
+    f32 = jnp.float32
+    got_low = swap_with(pick(first, 1, 1 - low), "dp", 1)
+    got_high = swap_with(pick(second, 0, 1 - high), "dp", 2)
+    pair_low = pick(first, 1, low).astype(f32) + got_low.astype(f32)
+    pair_high = pick(second, 0, high).astype(f32) + got_high.astype(f32)
+    end_low = swap_with(pick(pair_low, 0, 1 - high).astype(jnp.bfloat16), "dp", 2)
+    end_high = swap_with(pick(pair_high, 0, 1 - low).astype(jnp.bfloat16), "dp", 1)
+    sum_low = pick(pair_low, 0, high) + end_low.astype(f32)
+    sum_high = pick(pair_high, 0, low) + end_high.astype(f32)
+    return jnp.concatenate([sum_low, sum_high], axis=0)
+
+
+def dense(tokens, routes, gates, cotangent, partner, w_gate_up, w_down):
+    count_tokens, _ = routes.shape
+    width = tokens.shape[1]
+    units = w_down.shape[2]
+    n_expert = lax.axis_size("expert")
+    n_dp = lax.axis_size("dp")
+    experts_all = n_expert * 2
+    bf16, f32 = jnp.bfloat16, jnp.float32
+    me = lax.axis_index("expert")
+    partner_of = table_lookup(partner, me * 2 + jnp.arange(2, dtype=jnp.int32))
+    moved = partner_of // 2 != me
+    flip = moved[1]
+
+    slot_gates = jnp.sum(
+        jnp.where(
+            routes[None] == jnp.arange(experts_all, dtype=jnp.int32)[:, None, None], gates[None], 0.0
+        ),
+        axis=-1,
+    )
+    all_gates = lax.all_to_all(
+        slot_gates.reshape(n_expert, 2, count_tokens), "expert", 0, 0, tiled=True
+    )
+    all_gates = relative(all_gates, me)
+    all_gates = jnp.where(flip, all_gates[:, ::-1], all_gates)
+    gate_of = [all_gates[:, i].reshape(-1, 1) for i in range(2)]
+
+    rows = gather_relative(tokens)
+    cots = gather_relative(cotangent)
+    ordered = lambda w: jnp.concatenate(
+        [jnp.where(flip, w[1], w[0]), jnp.where(flip, w[0], w[1])], axis=1
+    )
+    up = ordered(w_gate_up)
+    down = ordered(w_down)
+
+    pre_act = jnp.dot(rows, up, preferred_element_type=f32)
+    weighted, factors = [], []
+    for i in range(2):
+        gate_pre = pre_act[:, 2 * i * units : (2 * i + 1) * units]
+        up_pre = pre_act[:, (2 * i + 1) * units : (2 * i + 2) * units]
+        sigmoid_gate = jax.nn.sigmoid(gate_pre)
+        silu_gate = gate_pre * sigmoid_gate
+        weighted.append((gate_of[i] * silu_gate * up_pre).astype(bf16))
+        factors.append(
+            gate_of[i] * up_pre * sigmoid_gate * (1.0 + gate_pre * (1.0 - sigmoid_gate))
+        )
+        factors.append(gate_of[i] * silu_gate)
+    weighted = jnp.concatenate(weighted, axis=1)
+    contract = lambda a, b, i, j: lax.dot_general(
+        a, b, (((i,), (j,)), ((), ())), preferred_element_type=f32
+    )
+    mixed_part = contract(weighted, down, 1, 1)
+    mixed = reduce_relative(mixed_part, count_tokens)
+
+    back = jnp.dot(cots, down, preferred_element_type=f32)
+    grad_pre = [
+        (back[:, i // 2 * units : (i // 2 + 1) * units] * factors[i]).astype(bf16) for i in range(4)
+    ]
+    sums = []
+    for i in range(2):
+        grad_gu = contract(rows, jnp.concatenate(grad_pre[2 * i : 2 * i + 2], axis=1), 0, 0)
+        grad_dn = contract(cots, weighted[:, i * units : (i + 1) * units], 0, 0)
+        terms = jnp.concatenate([grad_gu, grad_dn], axis=1).astype(bf16)
+        terms = terms.reshape(n_dp, 2, width // (2 * n_dp), 3 * units)
+        sums.append(scatter_sum(terms) * grad_scale)
+    traded = swap_with(sums[0].astype(bf16), "expert", n_expert // 2).astype(f32)
+    lead = jnp.where(moved[0] | moved[1], traded, sums[0])
+    out = jnp.where(flip, jnp.stack([sums[1], lead]), jnp.stack([lead, sums[1]]))
+
+    grad_part = contract(jnp.concatenate(grad_pre, axis=1), up, 1, 1)
+    grad_tokens = reduce_relative(grad_part, count_tokens)
+    return mixed, grad_tokens, out[:, :, : 2 * units], out[:, :, 2 * units :]
+
+
+def local(tokens, routes, gates, cotangent, partner, w_gate_up, w_down):
+    count_tokens, top_k = routes.shape
+    slots = w_gate_up.shape[0]
+    experts_all = lax.axis_size("expert") * slots
+    few = experts_all <= 4 * top_k and slots == 2 and lax.axis_size("dp") == 4
+    step = dense if few else routed
+    return step(tokens, routes, gates, cotangent, partner, w_gate_up, w_down)
+
+
 def solution(mesh):
     in_specs = (
         P(("dp", "expert"), None),

time: 573 us -> 212 us (0.37)
  waiting for transfers between devices: 419 us -> 109 us
  local copies, waits for them, and re-layouts: 56.2 us -> 13.2 us
  starting transfers between devices: 21.8 us -> 42.3 us
  matrix products: 30.5 us -> 18.6 us
  between operations: 14.3 us -> 2.46 us
  other arithmetic: 30.2 us -> 23.7 us
    all_to_all x4 -> x1, waiting for transfers between devices: 288 us -> 16 us  [dense(): lax.all_to_all(slot_gates.reshape(n_expert, 2, count_tokens), 'expert', 0...]
    ppermute x1 -> x25, waiting for transfers between devices: 131 us -> 93.3 us  [swap_with(): lax.ppermute(block, axis, [(i, i ^ mask) for i in range(lax.axis_size(axi...]
    ppermute x1 -> x25, starting transfers between devices: 2.92 us -> 39 us  [swap_with(): lax.ppermute(block, axis, [(i, i ^ mask) for i in range(lax.axis_size(axi...]
    gather x6 -> x0, local copies, waits for them, and re-layouts: 33.3 us -> none  [the longest x2 9.06 us: pick_slots(): return jnp.take(stacked, index, axis=0)]
    all_to_all x4 -> x1, starting transfers between devices: 18.7 us -> 3.33 us  [dense(): lax.all_to_all(slot_gates.reshape(n_expert, 2, count_tokens), 'expert', 0...]
    dot_general x7 -> x8, matrix products: 30.5 us -> 18.6 us  [the longest x6 11.3 us: dense(): lax.dot_general(a, b, (((i,), (j,)), ((), ())), preferred_element_type=f32)]
    concatenate x2 -> x4, other arithmetic: 10.3 us -> 0.3 us  [the longest x2 0.2 us: dense(): terms = jnp.concatenate([grad_gu, grad_dn], axis=1).astype(bf16)]
    mul x2 -> x1, other arithmetic: 8.27 us -> 0.08 us  [dense(): sums.append(scatter_sum(terms) * grad_scale)]
  transfers between devices with their start and end apart: 6 -> 26, of which waited for: 5 -> 11; matrix products, arithmetic and copies ran while one was open for 12% -> 11% of each run, Pallas kernels for 0% -> 0%
where the time goes in v1:
time: 212 us; the launch traced here: 209 us
  waiting for transfers between devices  109 us (51%)
  starting transfers between devices  42.3 us (20%)
  other arithmetic  23.7 us (11%)
  matrix products  18.6 us (9%)
  local copies, waits for them, and re-layouts  13.2 us (6%)
  between operations  2.46 us (1%)
    ppermute x25, waiting for transfers between devices, swap_with(): lax.ppermute(block, axis, [(i, i ^ mask) for i in range(lax.axis_size(axi...  93.3 us
    ppermute x25, starting transfers between devices, swap_with(): lax.ppermute(block, axis, [(i, i ^ mask) for i in range(lax.axis_size(axi...  39 us
    all_to_all x1, waiting for transfers between devices, dense(): lax.all_to_all(slot_gates.reshape(n_expert, 2, count_tokens), 'expert', 0...  16 us
    dot_general x6, matrix products, dense(): lax.dot_general(a, b, (((i,), (j,)), ((), ())), preferred_element_type=f32)  11.3 us
    another operation x4, other arithmetic, gather_relative(): jnp.stack([column, swap_with(column, 'expert', 1)], axis=1)  6.93 us
    select_n x2, other arithmetic, dense(): jnp.where(flip, w[1], w[0])  6.65 us
    dot_general x2, local copies, waits for them, and re-layouts, dense(): lax.dot_general(a, b, (((i,), (j,)), ((), ())), preferred_element_type=f32)  6.54 us
    dot_general x1, matrix products, dense(): pre_act = jnp.dot(rows, up, preferred_element_type=f32)  5.44 us
  transfers between devices with their start and end apart: 26, of which 11 were waited for; matrix products, arithmetic and copies ran while one was open for 11% of the time, Pallas kernels for 0%

profile of v1, /device:TPU:0, one launch (start us, length us, event | category | flops | bytes accessed | tf_op | source)
XLA Modules:
  0.0 209.5 jit_solution(16887365691189374137)
XLA Ops:
  0.6 5.1 %collective-permute-start.2 = (bf16[128,1024]{1,0:T(8,128)(2,1)}, bf16[128,1024]{1,0:T(8,128)(2,1)S(1)}, u32[]{:S(2)}, u32[]{:S(2)}) collective-permute-start(bf16[128,1024]{1,0:T(8,128)(2,1)} %param.7), channel_id=1, source_target_pairs={{0,6},{1,7},{2,4},{3,5},{4,2},{5,3},{6,0},{7,1},{8,14},{9,15},{10,... | collective-permute-start | bytes 786440 | tf_op jit(solution)/shard_map/ppermute | solution.py:113
  7.8 2.9 %collective-permute-start.9 = (bf16[128,1024]{1,0:T(8,128)(2,1)}, bf16[128,1024]{1,0:T(8,128)(2,1)}, u32[]{:S(2)}, u32[]{:S(2)}) collective-permute-start(bf16[128,1024]{1,0:T(8,128)(2,1)} %param.10), channel_id=1, source_target_pairs={{0,4},{1,5},{2,6},{3,7},{4,0},{5,1},{6,2},{7,3},{8,12},{9,13},{10,... | collective-permute-start | bytes 786440 | tf_op jit(solution)/shard_map/ppermute | solution.py:113
  12.0 3.3 %all-to-all-start = ((f32[8,2,128]{2,1,0:T(2,128)}), f32[8,2,128]{2,1,0:T(2,128)S(1)}, u32[]{:S(2)}, u32[]{:S(2)}) async-start(f32[8,2,128]{2,1,0:T(2,128)} %bitcast.1), calls=%async_computation | async-start | bytes 16384 | tf_op jit(solution)/shard_map/all_to_all | solution.py:181
  16.9 4.6 %select_bitcast_fusion.1 = (bf16[1024,768]{1,0:T(8,128)(2,1)}, bf16[1024,768]{1,0:T(8,128)(2,1)}) fusion(pred[]{:T(512)} %bitcast, bf16[2,1024,768]{2,1,0:T(8,128)(2,1)} %param.12), kind=kLoop, calls=%fused_computation.51 | loop fusion | flops 1572864 | bytes 6291457 | tf_op jit(solution)/shard_map/jit(_where)/select_n | solution.py:191
  24.9 3.7 %collective-permute-start.10 = (bf16[128,1024]{1,0:T(8,128)(2,1)S(1)}, bf16[128,1024]{1,0:T(8,128)(2,1)}, u32[]{:S(2)}, u32[]{:S(2)}) collective-permute-start(bf16[128,1024]{1,0:T(8,128)(2,1)S(1)} %copy-done.11), channel_id=1, source_target_pairs={{0,6},{1,7},{2,4},{3,5},{4,2},{5,3},{6,0},{7,1},{8,14},{9,15},{10,... | collective-permute-start | bytes 786440 | tf_op jit(solution)/shard_map/ppermute | solution.py:113
  30.4 16.0 %all-to-all-done = f32[8,2,128]{2,1,0:T(2,128)S(1)} async-done(((f32[8,2,128]{2,1,0:T(2,128)}), f32[8,2,128]{2,1,0:T(2,128)S(1)}, u32[]{:S(2)}, u32[]{:S(2)}) %all-to-all-start) | async-done | bytes 8224 | tf_op jit(solution)/shard_map/all_to_all | solution.py:181
  46.4 2.6 %fusion.67 = (bf16[4,1,128,1024]{3,2,1,0:T(8,128)(2,1)}, bf16[4,128,1024]{2,1,0:T(8,128)(2,1)}) fusion(bf16[1,128,1024]{2,1,0:T(8,128)(2,1)} %bitcast.30, bf16[1,128,1024]{2,1,0:T(8,128)(2,1)} %bitcast.29, bf16[1,128,1024]{2,1,0:T(8,128)(2,1)} %bitcast.28, bf16[1,128,1024]{2,1,0:T(8,128)(2,1)S(1)} %bitcast.184), kind=kLoop, calls=%fused_computation.141 | loop fusion | flops 1572864 | bytes 3145728 | tf_op jit(solution)/shard_map/stack | solution.py:120
  52.3 2.6 %copy.45 = bf16[1024,1024]{1,0:T(8,128)(2,1)} copy(bf16[1024,1024]{0,1:T(8,128)(2,1)S(1)} %bitcast.170) | data formatting | bytes 4194304 | tf_op jit(solution)/shard_map/dot_general | solution.py:209
  54.9 2.7 %pad_maximum_fusion.2 = bf16[4,2,128,1024]{3,2,1,0:T(8,128)(2,1)} fusion(bf16[4,1,128,1024]{3,2,1,0:T(8,128)(2,1)} %bitcast.33, bf16[4,1,128,1024]{3,2,1,0:T(8,128)(2,1)S(1)} %copy-done.1), kind=kLoop, calls=%fused_computation.21 | loop fusion | flops 1048576 | bytes 4194304 | tf_op jit(solution)/shard_map/stack | solution.py:120
  57.6 3.9 %copy.46 = bf16[1024,1024]{1,0:T(8,128)(2,1)} copy(bf16[1024,1024]{0,1:T(8,128)(2,1)} %bitcast.172) | data formatting | bytes 4194304 | tf_op jit(solution)/shard_map/dot_general | solution.py:209
  61.6 5.4 %fusion.14 = f32[1024,1536]{1,0:T(8,128)S(1)} fusion(bf16[1024,1024]{1,0:T(8,128)(2,1)S(1)} %bitcast.171, bf16[1024,768]{1,0:T(8,128)(2,1)} %get-tuple-element.17, bf16[1024,768]{1,0:T(8,128)(2,1)} %get-tuple-element.16), kind=kOutput, calls=%fused_computation.26 | convolution fusion | flops 3227516928 | bytes 11534336 | tf_op jit(solution)/shard_map/dot_general | solution.py:196
  68.8 2.4 %multiply_convert_fusion.3 = (bf16[1024,384]{1,0:T(8,128)(2,1)S(1)}, bf16[1024,384]{1,0:T(8,128)(2,1)S(1)}, bf16[1024,384]{1,0:T(8,128)(2,1)S(1)}, bf16[1024,384...) fusion(f32[1024,768]{1,0:T(8,128)S(1)} %fusion.33, f32[1024,1536]{1,0:T(8,128)S(1)} %fusion.14, ...), kind=kLoop, calls=%fused_computation.43 | loop fusion | flops 13369344 | bytes 14163968 | tf_op jit(solution)/shard_map/convert_element_type | solution.py:217
  79.8 3.4 %fusion = f32[1024,1024]{1,0:T(8,128)S(1)} fusion(bf16[1024,384]{1,0:T(8,128)(2,1)S(1)} %get-tuple-element.12, bf16[1024,384]{1,0:T(8,128)(2,1)S(1)} %get-tuple-element.13, bf16[1024,384]{1,0:T(8,128)(2,1)S(1)} %get-tuple-element.9, bf16[1024,384]{1,0:T(8,128)(2,1)S(1)} %get-tuple-element.8, bf16[1024,768]{1,0:T(8,128)(2,1)S(1)} %copy-done.6, ...), kind=kOutput, calls=%fused_computation.1 | convolution fusion | flops 3240099840 | bytes 10485760 | tf_op jit(solution)/shard_map/dot_general | solution.py:209
  89.8 9.7 %collective-permute-done.16 = bf16[2,128,1152]{2,1,0:T(8,128)(2,1)S(1)} collective-permute-done((bf16[2,128,1152]{2,1,0:T(8,128)(2,1)S(1)}, bf16[2,128,1152]{2,1,0:T(8,128)(2,1)S(1)}, u32[]{:S(2)}, u32[]{:S(2)}) %collective-permute-start.16) | collective-permute-done | bytes 589856 | tf_op jit(solution)/shard_map/ppermute | solution.py:113
  102.7 8.9 %collective-permute-done.20 = bf16[2,128,1152]{2,1,0:T(8,128)(2,1)S(1)} collective-permute-done((bf16[2,128,1152]{2,1,0:T(8,128)(2,1)S(1)}, bf16[2,128,1152]{2,1,0:T(8,128)(2,1)S(1)}, u32[]{:S(2)}, u32[]{:S(2)}) %collective-permute-start.20) | collective-permute-done | bytes 589856 | tf_op jit(solution)/shard_map/ppermute | solution.py:113
  115.4 10.2 %collective-permute-done.21 = bf16[128,1152]{1,0:T(8,128)(2,1)S(1)} collective-permute-done((bf16[128,1152]{1,0:T(8,128)(2,1)S(1)}, bf16[128,1152]{1,0:T(8,128)(2,1)S(1)}, u32[]{:S(2)}, u32[]{:S(2)}) %collective-permute-start.21) | collective-permute-done | bytes 294944 | tf_op jit(solution)/shard_map/ppermute | solution.py:113
  126.1 7.6 %collective-permute-done.23 = bf16[128,1152]{1,0:T(8,128)(2,1)S(1)} collective-permute-done((bf16[128,1152]{1,0:T(8,128)(2,1)S(1)}, bf16[128,1152]{1,0:T(8,128)(2,1)S(1)}, u32[]{:S(2)}, u32[]{:S(2)}) %collective-permute-start.23) | collective-permute-done | bytes 294944 | tf_op jit(solution)/shard_map/ppermute | solution.py:113
  133.9 6.4 %collective-permute-start.24 = (bf16[256,1152]{1,0:T(8,128)(2,1)S(1)}, bf16[256,1152]{1,0:T(8,128)(2,1)S(1)}, u32[]{:S(2)}, u32[]{:S(2)}) collective-permute-start(bf16[256,1152]{1,0:T(8,128)(2,1)S(1)} %fusion.34), channel_id=1, source_target_pairs={{0,4},{1,5},{2,6},{3,7},{4,0},{5,1},{6,2},{7,3},{8,12},{9,13},{10,... | collective-permute-start | bytes 1769480 | tf_op jit(solution)/shard_map/ppermute | solution.py:113
  143.0 2.5 %collective-permute-start.15 = (bf16[128,1024]{1,0:T(8,128)(2,1)S(1)}, bf16[128,1024]{1,0:T(8,128)(2,1)S(1)}, u32[]{:S(2)}, u32[]{:S(2)}) collective-permute-start(bf16[128,1024]{1,0:T(8,128)(2,1)S(1)} %get-tuple-element.21), channel_id=1, source_target_pairs={{0,6},{1,7},{2,4},{3,5},{4,2},{5,3},{6,0},{7,1},{8,14},{9,15},{10,... | collective-permute-start | bytes 786440 | tf_op jit(solution)/shard_map/ppermute | solution.py:113
  146.2 13.5 %collective-permute-done.13 = bf16[128,1024]{1,0:T(8,128)(2,1)S(1)} collective-permute-done((bf16[128,1024]{1,0:T(8,128)(2,1)S(1)}, bf16[128,1024]{1,0:T(8,128)(2,1)S(1)}, u32[]{:S(2)}, u32[]{:S(2)}) %collective-permute-start.13) | collective-permute-done | bytes 262176 | tf_op jit(solution)/shard_map/ppermute | solution.py:113
  159.7 2.4 %collective-permute-start.6 = (bf16[128,1024]{1,0:T(8,128)(2,1)S(1)}, bf16[128,1024]{1,0:T(8,128)(2,1)S(1)}, u32[]{:S(2)}, u32[]{:S(2)}) collective-permute-start(bf16[128,1024]{1,0:T(8,128)(2,1)S(1)} %get-tuple-element.27), channel_id=1, source_target_pairs={{0,4},{1,5},{2,6},{3,7},{4,0},{5,1},{6,2},{7,3},{8,12},{9,13},{10,... | collective-permute-start | bytes 786440 | tf_op jit(solution)/shard_map/ppermute | solution.py:113
  162.1 26.5 %collective-permute-done.14 = bf16[128,1024]{1,0:T(8,128)(2,1)S(1)} collective-permute-done((bf16[128,1024]{1,0:T(8,128)(2,1)S(1)}, bf16[128,1024]{1,0:T(8,128)(2,1)S(1)}, u32[]{:S(2)}, u32[]{:S(2)}) %collective-permute-start.14) | collective-permute-done | bytes 262176 | tf_op jit(solution)/shard_map/ppermute | solution.py:113
  188.6 2.4 %collective-permute-start.7 = (bf16[128,1024]{1,0:T(8,128)(2,1)S(1)}, bf16[128,1024]{1,0:T(8,128)(2,1)S(1)}, u32[]{:S(2)}, u32[]{:S(2)}) collective-permute-start(bf16[128,1024]{1,0:T(8,128)(2,1)S(1)} %get-tuple-element.26), channel_id=1, source_target_pairs={{0,6},{1,7},{2,4},{3,5},{4,2},{5,3},{6,0},{7,1},{8,14},{9,15},{10,... | collective-permute-start | bytes 786440 | tf_op jit(solution)/shard_map/ppermute | solution.py:113
  191.9 13.6 %collective-permute-done.6 = bf16[128,1024]{1,0:T(8,128)(2,1)S(1)} collective-permute-done((bf16[128,1024]{1,0:T(8,128)(2,1)S(1)}, bf16[128,1024]{1,0:T(8,128)(2,1)S(1)}, u32[]{:S(2)}, u32[]{:S(2)}) %collective-permute-start.6) | collective-permute-done | bytes 262176 | tf_op jit(solution)/shard_map/ppermute | solution.py:113
  (112 shorter events, 44.5 us)
Async XLA Ops:
  0.6 24.3 %collective-permute-start.2 = (bf16[128,1024]{1,0:T(8,128)(2,1)}, bf16[128,1024]{1,0:T(8,128)(2,1)S(1)}, u32[]{:S(2)}, u32[]{:S(2)}) collective-permute-start(bf16[128,1024]{1,0:T(8,128)(2,1)} %param.7), channel_id=1, source_target_pairs={{0,6},{1,7},{2,4},{3,5},{4,2},{5,3},{6,0},{7,1},{8,14},{9,15},{10,... | collective-permute-start | bytes 786440 | tf_op jit(solution)/shard_map/ppermute | solution.py:113
  5.7 22.9 %collective-permute-start = (bf16[128,1024]{1,0:T(8,128)(2,1)}, bf16[128,1024]{1,0:T(8,128)(2,1)S(1)}, u32[]{:S(2)}, u32[]{:S(2)}) collective-permute-start(bf16[128,1024]{1,0:T(8,128)(2,1)} %param.7), channel_id=1, source_target_pairs={{0,2},{1,3},{2,0},{3,1},{4,6},{5,7},{6,4},{7,5},{8,10},{9,11},{10,... | collective-permute-start | bytes 786440 | tf_op jit(solution)/shard_map/ppermute | solution.py:113
  5.7 24.4 %collective-permute-start.1 = (bf16[128,1024]{1,0:T(8,128)(2,1)}, bf16[128,1024]{1,0:T(8,128)(2,1)S(1)}, u32[]{:S(2)}, u32[]{:S(2)}) collective-permute-start(bf16[128,1024]{1,0:T(8,128)(2,1)} %param.7), channel_id=1, source_target_pairs={{0,4},{1,5},{2,6},{3,7},{4,0},{5,1},{6,2},{7,3},{8,12},{9,13},{10,... | collective-permute-start | bytes 786440 | tf_op jit(solution)/shard_map/ppermute | solution.py:113
  6.4 40.0 %collective-permute-start.8 = (bf16[128,1024]{1,0:T(8,128)(2,1)}, bf16[128,1024]{1,0:T(8,128)(2,1)}, u32[]{:S(2)}, u32[]{:S(2)}) collective-permute-start(bf16[128,1024]{1,0:T(8,128)(2,1)} %param.10), channel_id=1, source_target_pairs={{0,2},{1,3},{2,0},{3,1},{4,6},{5,7},{6,4},{7,5},{8,10},{9,11},{10,... | collective-permute-start | bytes 786440 | tf_op jit(solution)/shard_map/ppermute | solution.py:113
  7.8 38.6 %collective-permute-start.9 = (bf16[128,1024]{1,0:T(8,128)(2,1)}, bf16[128,1024]{1,0:T(8,128)(2,1)}, u32[]{:S(2)}, u32[]{:S(2)}) collective-permute-start(bf16[128,1024]{1,0:T(8,128)(2,1)} %param.10), channel_id=1, source_target_pairs={{0,4},{1,5},{2,6},{3,7},{4,0},{5,1},{6,2},{7,3},{8,12},{9,13},{10,... | collective-permute-start | bytes 786440 | tf_op jit(solution)/shard_map/ppermute | solution.py:113
  12.0 34.3 %all-to-all-start = ((f32[8,2,128]{2,1,0:T(2,128)}), f32[8,2,128]{2,1,0:T(2,128)S(1)}, u32[]{:S(2)}, u32[]{:S(2)}) async-start(f32[8,2,128]{2,1,0:T(2,128)} %bitcast.1), calls=%async_computation | async-start | bytes 16384 | tf_op jit(solution)/shard_map/all_to_all | solution.py:181
  24.9 21.5 %collective-permute-start.10 = (bf16[128,1024]{1,0:T(8,128)(2,1)S(1)}, bf16[128,1024]{1,0:T(8,128)(2,1)}, u32[]{:S(2)}, u32[]{:S(2)}) collective-permute-start(bf16[128,1024]{1,0:T(8,128)(2,1)S(1)} %copy-done.11), channel_id=1, source_target_pairs={{0,6},{1,7},{2,4},{3,5},{4,2},{5,3},{6,0},{7,1},{8,14},{9,15},{10,... | collective-permute-start | bytes 786440 | tf_op jit(solution)/shard_map/ppermute | solution.py:113
  30.3 19.5 %collective-permute-start.3 = (bf16[4,128,1024]{2,1,0:T(8,128)(2,1)S(1)}, bf16[4,128,1024]{2,1,0:T(8,128)(2,1)S(1)}, u32[]{:S(2)}, u32[]{:S(2)}) collective-permute-start(bf16[4,128,1024]{2,1,0:T(8,128)(2,1)S(1)} %get-tuple-element.29), channel_id=1, source_target_pairs={{0,1},{1,0},{2,3},{3,2},{4,5},{5,4},{6,7},{7,6},{8,9},{9,8},{10,11... | collective-permute-start | bytes 3145736 | tf_op jit(solution)/shard_map/ppermute | solution.py:113
  83.3 16.2 %collective-permute-start.16 = (bf16[2,128,1152]{2,1,0:T(8,128)(2,1)S(1)}, bf16[2,128,1152]{2,1,0:T(8,128)(2,1)S(1)}, u32[]{:S(2)}, u32[]{:S(2)}) collective-permute-start(bf16[2,128,1152]{2,1,0:T(8,128)(2,1)S(1)} %dynamic-slice_bitcast_fusion.1), channel_id=1, source_target_pairs={{0,8},{8,0},{16,24},{24,16},{1,9},{9,1},{17,25},{25,17},{2,10},{10... | collective-permute-start | bytes 1769480 | tf_op jit(solution)/shard_map/ppermute | solution.py:113
  84.9 16.2 %collective-permute-start.18 = (bf16[2,128,1152]{2,1,0:T(8,128)(2,1)S(1)}, bf16[2,128,1152]{2,1,0:T(8,128)(2,1)S(1)}, u32[]{:S(2)}, u32[]{:S(2)}) collective-permute-start(bf16[2,128,1152]{2,1,0:T(8,128)(2,1)S(1)} %fusion.38), channel_id=1, source_target_pairs={{0,16},{8,24},{16,0},{24,8},{1,17},{9,25},{17,1},{25,9},{2,18},{10... | collective-permute-start | bytes 1769480 | tf_op jit(solution)/shard_map/ppermute | solution.py:113
  86.4 25.2 %collective-permute-start.20 = (bf16[2,128,1152]{2,1,0:T(8,128)(2,1)S(1)}, bf16[2,128,1152]{2,1,0:T(8,128)(2,1)S(1)}, u32[]{:S(2)}, u32[]{:S(2)}) collective-permute-start(bf16[2,128,1152]{2,1,0:T(8,128)(2,1)S(1)} %dynamic-slice_bitcast_fusion), channel_id=1, source_target_pairs={{0,8},{8,0},{16,24},{24,16},{1,9},{9,1},{17,25},{25,17},{2,10},{10... | collective-permute-start | bytes 1769480 | tf_op jit(solution)/shard_map/ppermute | solution.py:113
  87.0 26.6 %collective-permute-start.22 = (bf16[2,128,1152]{2,1,0:T(8,128)(2,1)S(1)}, bf16[2,128,1152]{2,1,0:T(8,128)(2,1)S(1)}, u32[]{:S(2)}, u32[]{:S(2)}) collective-permute-start(bf16[2,128,1152]{2,1,0:T(8,128)(2,1)S(1)} %fusion.42), channel_id=1, source_target_pairs={{0,16},{8,24},{16,0},{24,8},{1,17},{9,25},{17,1},{25,9},{2,18},{10... | collective-permute-start | bytes 1769480 | tf_op jit(solution)/shard_map/ppermute | solution.py:113
  87.7 52.8 %collective-permute-start.12 = (bf16[4,128,1024]{2,1,0:T(8,128)(2,1)S(1)}, bf16[4,128,1024]{2,1,0:T(8,128)(2,1)S(1)}, u32[]{:S(2)}, u32[]{:S(2)}) collective-permute-start(bf16[4,128,1024]{2,1,0:T(8,128)(2,1)S(1)} %fusion.32), channel_id=1, source_target_pairs={{0,1},{1,0},{2,3},{3,2},{4,5},{5,4},{6,7},{7,6},{8,9},{9,8},{10,11... | collective-permute-start | bytes 3145736 | tf_op jit(solution)/shard_map/ppermute | solution.py:113
  99.5 46.0 %collective-permute-start.4 = (bf16[4,128,1024]{2,1,0:T(8,128)(2,1)S(1)}, bf16[4,128,1024]{2,1,0:T(8,128)(2,1)S(1)}, u32[]{:S(2)}, u32[]{:S(2)}) collective-permute-start(bf16[4,128,1024]{2,1,0:T(8,128)(2,1)S(1)} %fusion.31), channel_id=1, source_target_pairs={{0,1},{1,0},{2,3},{3,2},{4,5},{5,4},{6,7},{7,6},{8,9},{9,8},{10,11... | collective-permute-start | bytes 3145736 | tf_op jit(solution)/shard_map/ppermute | solution.py:113
  101.1 39.3 %collective-permute-start.17 = (bf16[128,1152]{1,0:T(8,128)(2,1)S(1)}, bf16[128,1152]{1,0:T(8,128)(2,1)S(1)}, u32[]{:S(2)}, u32[]{:S(2)}) collective-permute-start(bf16[128,1152]{1,0:T(8,128)(2,1)S(1)} %fusion.55), channel_id=1, source_target_pairs={{0,16},{8,24},{16,0},{24,8},{1,17},{9,25},{17,1},{25,9},{2,18},{10... | collective-permute-start | bytes 884744 | tf_op jit(solution)/shard_map/ppermute | solution.py:113
  111.7 28.7 %collective-permute-start.19 = (bf16[128,1152]{1,0:T(8,128)(2,1)S(1)}, bf16[128,1152]{1,0:T(8,128)(2,1)S(1)}, u32[]{:S(2)}, u32[]{:S(2)}) collective-permute-start(bf16[128,1152]{1,0:T(8,128)(2,1)S(1)} %fusion.56), channel_id=1, source_target_pairs={{0,8},{8,0},{16,24},{24,16},{1,9},{9,1},{17,25},{25,17},{2,10},{10... | collective-permute-start | bytes 884744 | tf_op jit(solution)/shard_map/ppermute | solution.py:113
  113.7 11.8 %collective-permute-start.21 = (bf16[128,1152]{1,0:T(8,128)(2,1)S(1)}, bf16[128,1152]{1,0:T(8,128)(2,1)S(1)}, u32[]{:S(2)}, u32[]{:S(2)}) collective-permute-start(bf16[128,1152]{1,0:T(8,128)(2,1)S(1)} %fusion.57), channel_id=1, source_target_pairs={{0,16},{8,24},{16,0},{24,8},{1,17},{9,25},{17,1},{25,9},{2,18},{10... | collective-permute-start | bytes 884744 | tf_op jit(solution)/shard_map/ppermute | solution.py:113
  133.9 72.4 %collective-permute-start.24 = (bf16[256,1152]{1,0:T(8,128)(2,1)S(1)}, bf16[256,1152]{1,0:T(8,128)(2,1)S(1)}, u32[]{:S(2)}, u32[]{:S(2)}) collective-permute-start(bf16[256,1152]{1,0:T(8,128)(2,1)S(1)} %fusion.34), channel_id=1, source_target_pairs={{0,4},{1,5},{2,6},{3,7},{4,0},{5,1},{6,2},{7,3},{8,12},{9,13},{10,... | collective-permute-start | bytes 1769480 | tf_op jit(solution)/shard_map/ppermute | solution.py:113
  141.0 18.7 %collective-permute-start.13 = (bf16[128,1024]{1,0:T(8,128)(2,1)S(1)}, bf16[128,1024]{1,0:T(8,128)(2,1)S(1)}, u32[]{:S(2)}, u32[]{:S(2)}) collective-permute-start(bf16[128,1024]{1,0:T(8,128)(2,1)S(1)} %get-tuple-element.20), channel_id=1, source_target_pairs={{0,2},{1,3},{2,0},{3,1},{4,6},{5,7},{6,4},{7,5},{8,10},{9,11},{10,... | collective-permute-start | bytes 786440 | tf_op jit(solution)/shard_map/ppermute | solution.py:113
  141.1 47.5 %collective-permute-start.14 = (bf16[128,1024]{1,0:T(8,128)(2,1)S(1)}, bf16[128,1024]{1,0:T(8,128)(2,1)S(1)}, u32[]{:S(2)}, u32[]{:S(2)}) collective-permute-start(bf16[128,1024]{1,0:T(8,128)(2,1)S(1)} %get-tuple-element.22), channel_id=1, source_target_pairs={{0,4},{1,5},{2,6},{3,7},{4,0},{5,1},{6,2},{7,3},{8,12},{9,13},{10,... | collective-permute-start | bytes 786440 | tf_op jit(solution)/shard_map/ppermute | solution.py:113
  143.0 48.0 %collective-permute-start.15 = (bf16[128,1024]{1,0:T(8,128)(2,1)S(1)}, bf16[128,1024]{1,0:T(8,128)(2,1)S(1)}, u32[]{:S(2)}, u32[]{:S(2)}) collective-permute-start(bf16[128,1024]{1,0:T(8,128)(2,1)S(1)} %get-tuple-element.21), channel_id=1, source_target_pairs={{0,6},{1,7},{2,4},{3,5},{4,2},{5,3},{6,0},{7,1},{8,14},{9,15},{10,... | collective-permute-start | bytes 786440 | tf_op jit(solution)/shard_map/ppermute | solution.py:113
  146.1 45.7 %collective-permute-start.5 = (bf16[128,1024]{1,0:T(8,128)(2,1)S(1)}, bf16[128,1024]{1,0:T(8,128)(2,1)S(1)}, u32[]{:S(2)}, u32[]{:S(2)}) collective-permute-start(bf16[128,1024]{1,0:T(8,128)(2,1)S(1)} %get-tuple-element.25), channel_id=1, source_target_pairs={{0,2},{1,3},{2,0},{3,1},{4,6},{5,7},{6,4},{7,5},{8,10},{9,11},{10,... | collective-permute-start | bytes 786440 | tf_op jit(solution)/shard_map/ppermute | solution.py:113
  159.7 45.7 %collective-permute-start.6 = (bf16[128,1024]{1,0:T(8,128)(2,1)S(1)}, bf16[128,1024]{1,0:T(8,128)(2,1)S(1)}, u32[]{:S(2)}, u32[]{:S(2)}) collective-permute-start(bf16[128,1024]{1,0:T(8,128)(2,1)S(1)} %get-tuple-element.27), channel_id=1, source_target_pairs={{0,4},{1,5},{2,6},{3,7},{4,0},{5,1},{6,2},{7,3},{8,12},{9,13},{10,... | collective-permute-start | bytes 786440 | tf_op jit(solution)/shard_map/ppermute | solution.py:113
  188.6 16.9 %collective-permute-start.7 = (bf16[128,1024]{1,0:T(8,128)(2,1)S(1)}, bf16[128,1024]{1,0:T(8,128)(2,1)S(1)}, u32[]{:S(2)}, u32[]{:S(2)}) collective-permute-start(bf16[128,1024]{1,0:T(8,128)(2,1)S(1)} %get-tuple-element.26), channel_id=1, source_target_pairs={{0,6},{1,7},{2,4},{3,5},{4,2},{5,3},{6,0},{7,1},{8,14},{9,15},{10,... | collective-permute-start | bytes 786440 | tf_op jit(solution)/shard_map/ppermute | solution.py:113
  (14 other events, 56.7 us)

commit v2 on v0

--- a/solution.py
+++ b/solution.py
@@ -1,9 +1,14 @@
+import functools
+
 import jax
 import jax.numpy as jnp
 from jax import lax
+from jax.experimental import pallas as pl
+from jax.experimental.pallas import tpu as pltpu
 from jax.sharding import PartitionSpec as P
 
 grad_scale = 0.0625
+vmem = 20 << 20
 
 
 def partner_2(block, axis, distance):
@@ -28,7 +33,7 @@
     return jnp.take(stacked, index, axis=0)
 
 
-def local(tokens, routes, gates, cotangent, partner, w_gate_up, w_down):
+def routed(tokens, routes, gates, cotangent, partner, w_gate_up, w_down):
     count_tokens, top_k = routes.shape
     width = tokens.shape[1]
     hidden_units = w_down.shape[2]
@@ -109,6 +114,306 @@
     )
 
 
+def swap_with(block, axis, mask):
+    return lax.ppermute(block, axis, [(i, i ^ mask) for i in range(lax.axis_size(axis))])
+
+
+def send(block, pairs):
+    return lax.ppermute(block, "expert", [(2 * a + c, 2 * b + c) for a, b in pairs for c in range(2)])
+
+
+def after(value, *earlier):
+    return lax.optimization_barrier((value,) + earlier)[0]
+
+
+def near_blocks(block, inner):
+    two = swap_with(block, "expert", 4)
+    one = swap_with(block, "expert", 2)
+    middle = send(block, [(1, 2), (2, 1)])
+    ends = send(two, [(1, 0), (2, 3)])
+    return [block, one, two, jnp.where(inner, middle, ends)]
+
+
+def direct_blocks(block):
+    return [block] + [swap_with(block, "expert", mask) for mask in (2, 4, 6)]
+
+
+def both_cores(blocks):
+    return [(block, swap_with(block, "expert", 1)) for block in blocks]
+
+
+def reduce_relative(kept, other):
+    f32, bf16 = jnp.float32, jnp.bfloat16
+    pair = [(kept[k].astype(f32) + other[k].astype(f32)) for k in range(4)]
+    far = pair[3].astype(bf16)
+    passed = send(far, [(0, 1), (3, 2)])
+    one = swap_with(pair[1].astype(bf16), "expert", 2)
+    middle = send(far, [(1, 2), (2, 1)])
+    two = swap_with((pair[2] + passed.astype(f32)).astype(bf16), "expert", 4)
+    total = pair[0] + one.astype(f32) + middle.astype(f32) + two.astype(f32)
+    return total.astype(bf16), passed
+
+
+def relative(array, index):
+    count = array.shape[0]
+    for bit in range(count.bit_length() - 1):
+        parts = array.reshape((count >> bit + 1, 2, 1 << bit) + array.shape[1:])
+        array = jnp.where((index >> bit) & 1 == 1, parts[:, ::-1], parts).reshape(array.shape)
+    return array
+
+
+def contract(a, b, i, j):
+    return lax.dot_general(a, b, (((i,), (j,)), ((), ())), preferred_element_type=jnp.float32)
+
+
+def message_kernel(tokens_ref, routes_ref, gates_ref, out_ref, *, experts):
+    rows, width = tokens_ref.shape
+    lanes = out_ref.shape[1] - width
+    out_ref[:, :width] = tokens_ref[...]
+    lane = lax.broadcasted_iota(jnp.int32, (rows, lanes), 1)
+    expert = lane % experts
+    gate = jnp.zeros((rows, lanes), jnp.float32)
+    for k in range(routes_ref.shape[1]):
+        gate = gate + jnp.where(routes_ref[:, k : k + 1] == expert, gates_ref[:, k : k + 1], 0.0)
+    high = gate.astype(jnp.bfloat16).astype(jnp.float32)
+    middle = (gate - high).astype(jnp.bfloat16).astype(jnp.float32)
+    low = gate - high - middle
+    third = lane // experts
+    value = jnp.where(third == 0, high, jnp.where(third == 1, middle, jnp.where(third == 2, low, 0.0)))
+    out_ref[:, width:] = value.astype(out_ref.dtype)
+
+
+def message(tokens, routes, gates, experts):
+    rows, width = tokens.shape
+    return pl.pallas_call(
+        functools.partial(message_kernel, experts=experts),
+        out_shape=jax.ShapeDtypeStruct((rows, width + 128), tokens.dtype),
+        cost_estimate=pl.CostEstimate(flops=0, bytes_accessed=1 << 20, transcendentals=0),
+        name="message",
+    )(tokens, routes, gates)
+
+
+def gate_of(ref, width, expert, experts):
+    values = ref[:, width:].astype(jnp.float32)
+    lane = lax.broadcasted_iota(jnp.int32, values.shape, 1)
+    chosen = jnp.logical_and(lane % experts == expert, lane < 3 * experts)
+    return jnp.sum(jnp.where(chosen, values, 0.0), axis=1, keepdims=True)
+
+
+def forward_kernel(at, x_ref, y_ref, up_ref, down_ref, h_ref, f_ref, kept_ref, sent_ref, *, experts):
+    units = down_ref.shape[2]
+    half = kept_ref.shape[0]
+    width = up_ref.shape[1]
+    x = jnp.concatenate([x_ref[:, :width], y_ref[:, :width]], axis=0)
+    total = None
+    for i in range(2):
+        slot = jnp.bitwise_xor(at[1], i)
+        pre = jnp.dot(x, up_ref[slot], preferred_element_type=jnp.float32)
+        gate_pre, up_pre = pre[:, :units], pre[:, units:]
+        expert = 2 * at[2] + slot
+        gate = [gate_of(ref, width, expert, experts) for ref in (x_ref, y_ref)]
+        gate = jnp.concatenate(gate, axis=0)
+        sig = 0.5 * jnp.tanh(0.5 * gate_pre) + 0.5
+        scaled = gate * sig
+        silu = scaled * gate_pre
+        hidden = (silu * up_pre).astype(jnp.bfloat16)
+        h_ref[i] = hidden
+        f_ref[i, :, :units] = (up_pre * (scaled + silu * (1.0 - sig))).astype(f_ref.dtype)
+        f_ref[i, :, units:] = silu.astype(f_ref.dtype)
+        part = contract(hidden, down_ref[slot], 1, 1)
+        total = part if total is None else total + part
+    kept_ref[...] = total[:half].astype(kept_ref.dtype)
+    sent_ref[...] = total[half:].astype(sent_ref.dtype)
+
+
+def call(kernel, name, scalars, operands, outs, flops, places=None, scratch=()):
+    places = places or [pltpu.VMEM] * len(outs)
+    return pl.pallas_call(
+        kernel,
+        in_specs=[pl.BlockSpec(memory_space=pltpu.SMEM)]
+        + [pl.BlockSpec(memory_space=pltpu.VMEM)] * len(operands),
+        out_specs=[pl.BlockSpec(memory_space=place) for place in places],
+        scratch_shapes=list(scratch),
+        out_shape=[jax.ShapeDtypeStruct(shape, dtype) for shape, dtype in outs],
+        compiler_params=pltpu.CompilerParams(vmem_limit_bytes=vmem),
+        cost_estimate=pl.CostEstimate(flops=2 * flops, bytes_accessed=0, transcendentals=0),
+        name=name,
+    )(scalars, *operands)
+
+
+def forward(at, pair, w_gate_up, w_down, experts):
+    count_tokens = pair[0].shape[0]
+    width = w_gate_up.shape[1]
+    n = 2 * count_tokens
+    units = w_down.shape[2]
+    bf16 = jnp.bfloat16
+    outs = [((2, n, units), bf16), ((2, n, 2 * units), bf16)] + [((count_tokens, width), bf16)] * 2
+    kernel = functools.partial(forward_kernel, experts=experts)
+    flops = 12 * n * width * units
+    return call(kernel, "forward", at, (*pair, w_gate_up, w_down), outs, flops)
+
+
+def weight_kernel(at, *refs):
+    xs, cs, fs, hs = refs[:8], refs[8:16], refs[16:20], refs[20:24]
+    down_ref, *outs = refs[24:35]
+    held, sems = refs[35:41], refs[41]
+    copies = [
+        pltpu.make_async_copy(source, target, sems.at[i])
+        for i, (source, target) in enumerate(zip(held, (outs[0], *outs[5:])))
+    ]
+    outs = [held[0], *outs[1:5], *held[1:]]
+    units = down_ref.shape[2]
+    block = xs[0].shape[0]
+    for order in range(2):
+        p_ref, send_a, send_b, keep_a, keep_b = outs[5 * order : 5 * order + 5]
+        rows = send_a.shape[1]
+        down = down_ref[jnp.bitwise_xor(at[1], order)]
+        for k in range(4):
+            c = jnp.concatenate([cs[2 * k][...], cs[2 * k + 1][...]], axis=0)
+            back = jnp.dot(c, down, preferred_element_type=jnp.float32)
+            here = slice(2 * k * block, 2 * (k + 1) * block)
+            factor = fs[k][order].astype(jnp.float32)
+            p_ref[here, :units] = (back * factor[:, :units]).astype(p_ref.dtype)
+            p_ref[here, units:] = (back * factor[:, units:]).astype(p_ref.dtype)
+        for i in range(4):
+            start = pl.multiple_of(jnp.bitwise_xor(at[0], i) * 2 * rows, 2 * rows)
+            column = pl.ds(start, 2 * rows)
+            x = jnp.concatenate([ref[:, column] for ref in xs], axis=0)
+            c = jnp.concatenate([ref[:, column] for ref in cs], axis=0)
+            h = jnp.concatenate([ref[order] for ref in hs], axis=0)
+            first = (contract(x, p_ref[...], 0, 0) * grad_scale).astype(send_a.dtype)
+            last = (contract(c, h, 0, 0) * grad_scale).astype(send_a.dtype)
+            ref_a = send_a if i & 1 else keep_a
+            ref_b = send_b if i & 2 else keep_b
+            ref_a[i >> 1, :, : 2 * units] = first[:rows]
+            ref_a[i >> 1, :, 2 * units :] = last[:rows]
+            ref_b[i & 1, :, : 2 * units] = first[rows:]
+            ref_b[i & 1, :, 2 * units :] = last[rows:]
+        for copy in copies[:1] if order == 0 else copies[1:]:
+            copy.start()
+    for copy in copies:
+        copy.wait()
+
+
+def weight_terms(at, rows, cots, factors, hidden, w_down):
+    count_tokens, width = cots[0][0].shape
+    n = 8 * count_tokens
+    units = w_down.shape[2]
+    bf16 = jnp.bfloat16
+    flat = lambda pairs: [block for pair in pairs for block in pair]
+    outs = [((n, 2 * units), bf16)] + [((2, width // 8, 3 * units), bf16)] * 4
+    operands = (*flat(rows), *flat(cots), *factors, *hidden, w_down)
+    flops = 16 * n * width * units
+    far = [outs[0], *outs]
+    scratch = [pltpu.VMEM(*out) for out in far] + [pltpu.SemaphoreType.DMA((len(far),))]
+    places = [pltpu.HBM] + [pltpu.VMEM] * 4 + [pltpu.HBM] * 5
+    result = call(weight_kernel, "weight_terms", at, operands, outs * 2, flops, places, scratch)
+    return result[:5], result[5:]
+
+
+def backward_kernel(at, p_ref, q_ref, up_ref, kept_ref, sent_ref):
+    half = kept_ref.shape[1]
+    for k in range(kept_ref.shape[0]):
+        here = slice(2 * k * half, 2 * (k + 1) * half)
+        total = contract(p_ref[here], up_ref[at[1]], 1, 1)
+        total = total + contract(q_ref[here], up_ref[1 - at[1]], 1, 1)
+        kept_ref[k] = total[:half].astype(kept_ref.dtype)
+        sent_ref[k] = total[half:].astype(sent_ref.dtype)
+
+
+def backward(at, first, second, w_gate_up, count_tokens):
+    width = w_gate_up.shape[1]
+    outs = [((first.shape[0] // (2 * count_tokens), count_tokens, width), jnp.bfloat16)] * 2
+    flops = 4 * first.size * width
+    return call(backward_kernel, "backward", at, (first, second, w_gate_up), outs, flops)
+
+
+def finish_kernel(at, a0, a1, b0, b1, ta, tb, gu_ref, dn_ref):
+    columns = gu_ref.shape[2]
+    rows = a0.shape[0]
+    for h, (own, other, traded) in enumerate(((a0, a1, ta), (b0, b1, tb))):
+        lead = jnp.where(at[1] == 1, traded[...].astype(jnp.float32), own[...])
+        for slot, value in ((at[0], lead), (1 - at[0], other[...])):
+            gu_ref[slot, h * rows : (h + 1) * rows, :] = value[:, :columns]
+            dn_ref[slot, h * rows : (h + 1) * rows, :] = value[:, columns:]
+
+
+def finish(at, sums, traded, units):
+    rows = traded[0].shape[0]
+    full = pl.BlockSpec(memory_space=pltpu.VMEM)
+    return pl.pallas_call(
+        finish_kernel,
+        in_specs=[pl.BlockSpec(memory_space=pltpu.SMEM)] + [full] * 6,
+        out_specs=[full, full],
+        out_shape=[
+            jax.ShapeDtypeStruct((2, 2 * rows, 2 * units), jnp.float32),
+            jax.ShapeDtypeStruct((2, 2 * rows, units), jnp.float32),
+        ],
+        compiler_params=pltpu.CompilerParams(vmem_limit_bytes=vmem),
+        cost_estimate=pl.CostEstimate(flops=0, bytes_accessed=0, transcendentals=0),
+        name="finish",
+    )(at, sums[0][0], sums[1][0], sums[0][1], sums[1][1], traded[0], traded[1])
+
+
+def pair_sum(send_a, send_b, keep_a, keep_b):
+    f32 = jnp.float32
+    got_a = swap_with(send_a, "dp", 1)
+    got_b = swap_with(send_b, "dp", 2)
+    return keep_a.astype(f32) + got_a.astype(f32), keep_b.astype(f32) + got_b.astype(f32)
+
+
+def quarter_sum(pair_a, pair_b):
+    f32, bf16 = jnp.float32, jnp.bfloat16
+    end_a = swap_with(pair_a[1].astype(bf16), "dp", 2)
+    end_b = swap_with(pair_b[1].astype(bf16), "dp", 1)
+    return pair_a[0] + end_a.astype(f32), pair_b[0] + end_b.astype(f32)
+
+
+def dense(tokens, routes, gates, cotangent, partner, w_gate_up, w_down):
+    count_tokens, _ = routes.shape
+    units = w_down.shape[2]
+    n_expert = lax.axis_size("expert")
+    bf16, f32, i32 = jnp.bfloat16, jnp.float32, jnp.int32
+    me = lax.axis_index("expert")
+    partner_of = table_lookup(partner, me * 2 + jnp.arange(2, dtype=i32))
+    moved = partner_of // 2 != me
+    flip = moved[1].astype(i32)
+    trades = jnp.any(moved).astype(i32)
+    inner = (me // 2 == 1) | (me // 2 == 2)
+
+    line = near_blocks(message(tokens, routes, gates, 2 * n_expert), inner)
+    rows = both_cores(line)
+    cots = both_cores(direct_blocks(after(cotangent, line[0])))
+
+    at = jnp.stack([lax.axis_index("dp"), flip, me])
+    passes = [forward(at, rows[k], w_gate_up, w_down, 2 * n_expert) for k in range(4)]
+    hidden, factors, kept, sent = zip(*passes)
+
+    (first, *terms), (second, *later) = weight_terms(at, rows, cots, factors, hidden, w_down)
+    pair = pair_sum(*terms)
+    other = [swap_with(block, "expert", 1) for block in sent]
+    mixed, passed = reduce_relative(kept, other)
+    sums = [quarter_sum(*pair)]
+    later[:2] = after(later[:2], *pair)
+    second = after(second, passed)
+    kept, sent = backward(at, first, second, w_gate_up, count_tokens)
+    sums.append(quarter_sum(*pair_sum(*later)))
+    grad_tokens, _ = reduce_relative(kept, swap_with(sent, "expert", 1))
+    traded = [swap_with(half.astype(bf16), "expert", n_expert // 2) for half in sums[0]]
+    grad_gu, grad_dn = finish(jnp.stack([flip, trades]), sums, traded, units)
+    return mixed, grad_tokens, grad_gu, grad_dn
+
+
+def local(tokens, routes, gates, cotangent, partner, w_gate_up, w_down):
+    count_tokens, top_k = routes.shape
+    slots = w_gate_up.shape[0]
+    experts_all = lax.axis_size("expert") * slots
+    line = lax.axis_size("dp") == 4 and lax.axis_size("expert") == 8
+    few = experts_all <= 4 * top_k and slots == 2
+    step = dense if few and line else routed
+    return step(tokens, routes, gates, cotangent, partner, w_gate_up, w_down)
+
+
 def solution(mesh):
     in_specs = (
         P(("dp", "expert"), None),

time: 573 us -> 153 us (0.27)
  waiting for transfers between devices: 419 us -> 57.6 us
  local copies, waits for them, and re-layouts: 56.2 us -> 6.55 us
  starting transfers between devices: 21.8 us -> 55.2 us
  matrix products: 30.5 us -> 0 us
  Pallas kernels: 0 us -> 26.6 us
  other arithmetic: 30.2 us -> 4.78 us
  between operations: 14.3 us -> 2.35 us
    all_to_all x4 -> x0, waiting for transfers between devices: 288 us -> none  [the longest x1 160 us: local(): lax.all_to_all(sending_rows, 'expert', split_axis=0, concat_axis=0, tiled...]
    ppermute x1 -> x38, waiting for transfers between devices: 131 us -> 57.6 us  [the longest x32 50.5 us: swap_with(): lax.ppermute(block, axis, [(i, i ^ mask) for i in range(lax.axis_size(axi...]
    ppermute x1 -> x38, starting transfers between devices: 2.92 us -> 55.2 us  [the longest x32 45.8 us: swap_with(): lax.ppermute(block, axis, [(i, i ^ mask) for i in range(lax.axis_size(axi...]
    gather x6 -> x0, local copies, waits for them, and re-layouts: 33.3 us -> none  [the longest x2 9.06 us: pick_slots(): return jnp.take(stacked, index, axis=0)]
    dot_general x7 -> x0, matrix products: 30.5 us -> none  [the longest x1 6.81 us: local(): jnp.einsum('sjcd,jdf->sjcf', arrived, weight_gu, preferred_element_type=j...]
    pallas_call x0 -> x8, Pallas kernels: none -> 26.6 us  [the longest x6 22.4 us: call(): pl.pallas_call(kernel, in_specs=[pl.BlockSpec(memory_space=pltpu.SMEM)] +...]
    all_to_all x4 -> x0, starting transfers between devices: 18.7 us -> none  [the longest x1 6.59 us: local(): lax.all_to_all(sending_rows, 'expert', split_axis=0, concat_axis=0, tiled...]
    concatenate x2 -> x0, other arithmetic: 10.3 us -> none  [pick_slots(): stacked = jnp.concatenate([own_slots, received], axis=0)]
  transfers between devices with their start and end apart: 6 -> 38, of which waited for: 5 -> 9; matrix products, arithmetic and copies ran while one was open for 12% -> 3% of each run, Pallas kernels for 0% -> 16%
where the time goes in v2:
time: 153 us
  waiting for transfers between devices  57.6 us (38%)
  starting transfers between devices  55.2 us (36%)
  Pallas kernels  26.6 us (17%)
  local copies, waits for them, and re-layouts  6.55 us (4%)
  other arithmetic  4.78 us (3%)
  between operations  2.35 us (2%)
    ppermute x32, waiting for transfers between devices, swap_with(): lax.ppermute(block, axis, [(i, i ^ mask) for i in range(lax.axis_size(axi...  50.5 us
    ppermute x32, starting transfers between devices, swap_with(): lax.ppermute(block, axis, [(i, i ^ mask) for i in range(lax.axis_size(axi...  45.8 us
    pallas_call x6, Pallas kernels, call(): pl.pallas_call(kernel, in_specs=[pl.BlockSpec(memory_space=pltpu.SMEM)] +...  22.4 us
    ppermute x6, starting transfers between devices, send(): lax.ppermute(block, 'expert', [(2 * a + c, 2 * b + c) for a, b in pairs f...  9.35 us
    ppermute x6, waiting for transfers between devices, send(): lax.ppermute(block, 'expert', [(2 * a + c, 2 * b + c) for a, b in pairs f...  7.03 us
    unnamed x14, local copies, waits for them, and re-layouts  5.82 us
  transfers between devices with their start and end apart: 38, of which 9 were waited for; matrix products, arithmetic and copies ran while one was open for 3% of the time, Pallas kernels for 16%

profile of v2, /device:TPU:0, one launch (start us, length us, event | category | flops | bytes accessed | tf_op | source)
XLA Modules:
  0.0 153.0 jit_solution(13432604952883065217)
XLA Ops:
  5.7 4.0 %collective-permute-start.7 = (bf16[128,1152]{1,0:T(8,128)(2,1)}, bf16[128,1152]{1,0:T(8,128)(2,1)S(1)}, u32[]{:S(2)}, u32[]{:S(2)}) collective-permute-start(bf16[128,1152]{1,0:T(8,128)(2,1)} %message.1.x_ref.refs_0_), channel_id=1, source_target_pairs={{0,4},{1,5},{2,6},{3,7},{4,0},{5,1},{6,2},{7,3},{8,12},{9,13},{10,... | collective-permute-start | bytes 884744 | tf_op jit(solution)/shard_map/ppermute | solution.py:118
  10.4 2.9 %collective-permute-start.2 = (bf16[128,1152]{1,0:T(8,128)(2,1)}, bf16[128,1152]{1,0:T(8,128)(2,1)S(1)}, u32[]{:S(2)}, u32[]{:S(2)}) collective-permute-start(bf16[128,1152]{1,0:T(8,128)(2,1)} %message.1.x_ref.refs_0_), channel_id=1, source_target_pairs={{0,2},{1,3},{2,0},{3,1},{4,6},{5,7},{6,4},{7,5},{8,10},{9,11},{10,... | collective-permute-start | bytes 884744 | tf_op jit(solution)/shard_map/ppermute | solution.py:118
  14.2 9.9 %collective-permute-done.7.x_ref.refs_4_ = bf16[128,1152]{1,0:T(8,128)(2,1)S(1)} collective-permute-done((bf16[128,1152]{1,0:T(8,128)(2,1)}, bf16[128,1152]{1,0:T(8,128)(2,1)S(1)}, u32[]{:S(2)}, u32[]{:S(2)}) %collective-permute-start.7) | collective-permute-done | bytes 294944 | tf_op jit(solution)/shard_map/ppermute | solution.py:118
  28.1 4.1 %collective-permute-start.19 = (bf16[128,1024]{1,0:T(8,128)(2,1)}, bf16[128,1024]{1,0:T(8,128)(2,1)S(1)}, u32[]{:S(2)}, u32[]{:S(2)}) collective-permute-start(bf16[128,1024]{1,0:T(8,128)(2,1)} %refs_8_), channel_id=1, source_target_pairs={{0,4},{1,5},{2,6},{3,7},{4,0},{5,1},{6,2},{7,3},{8,12},{9,13},{10,... | collective-permute-start | bytes 786440 | tf_op jit(solution)/shard_map/ppermute | solution.py:118
  33.1 4.5 %collective-permute-done.8 = bf16[128,1152]{1,0:T(8,128)(2,1)S(1)} collective-permute-done((bf16[128,1152]{1,0:T(8,128)(2,1)S(1)}, bf16[128,1152]{1,0:T(8,128)(2,1)S(1)}, u32[]{:S(2)}, u32[]{:S(2)}) %collective-permute-start.8) | collective-permute-done | bytes 294944 | tf_op jit(solution)/shard_map/ppermute | solution.py:122
  41.1 2.2 %forward.4 = (bf16[2,256,384]{2,1,0:T(8,128)(2,1)S(1)}, bf16[2,256,768]{2,1,0:T(8,128)(2,1)S(1)}, bf16[128,1024]{1,0:T(8,128)(2,1)S(1)}, bf16[128,1024]{1,0:T(8,128)(2,1)S(1)}) custom-call(s32[3]{0:T(128)S(1)} %pad_add_fusion.at, bf16[128,1152]{1,0:T(8,128)(2,1)S(1)} %copy-done, bf16[128,1152]{1,0:T(8,128)(2,1)S(1)} %collective-permute-done.y_ref.refs_1_, ...), custom_call_target="tpu_custom_call" | custom-call | flops 2415919104 | tf_op jit(solution)/shard_map/forward/pallas_call | solution.py:231
  43.5 2.2 %forward.5 = (bf16[2,256,384]{2,1,0:T(8,128)(2,1)S(1)}, bf16[2,256,768]{2,1,0:T(8,128)(2,1)S(1)}, bf16[128,1024]{1,0:T(8,128)(2,1)S(1)}, bf16[128,1024]{1,0:T(8,128)(2,1)S(1)}) custom-call(s32[3]{0:T(128)S(1)} %pad_add_fusion.at, bf16[128,1152]{1,0:T(8,128)(2,1)S(1)} %collective-permute-done.2.x_ref.refs_2_, ...), custom_call_target="tpu_custom_call" | custom-call | flops 2415919104 | tf_op jit(solution)/shard_map/forward/pallas_call | solution.py:231
  46.3 2.2 %forward.6 = (bf16[2,256,384]{2,1,0:T(8,128)(2,1)S(1)}, bf16[2,256,768]{2,1,0:T(8,128)(2,1)S(1)}, bf16[128,1024]{1,0:T(8,128)(2,1)S(1)}, bf16[128,1024]{1,0:T(8,128)(2,1)S(1)}) custom-call(s32[3]{0:T(128)S(1)} %pad_add_fusion.at, bf16[128,1152]{1,0:T(8,128)(2,1)S(1)} %broadcast_select_fusion.x_ref.refs_6_, ...), custom_call_target="tpu_custom_call" | custom-call | flops 2415919104 | tf_op jit(solution)/shard_map/forward/pallas_call | solution.py:231
  48.6 2.2 %forward.7 = (bf16[2,256,384]{2,1,0:T(8,128)(2,1)S(1)}, bf16[2,256,768]{2,1,0:T(8,128)(2,1)S(1)}, bf16[128,1024]{1,0:T(8,128)(2,1)S(1)}, bf16[128,1024]{1,0:T(8,128)(2,1)S(1)}) custom-call(s32[3]{0:T(128)S(1)} %pad_add_fusion.at, bf16[128,1152]{1,0:T(8,128)(2,1)S(1)} %collective-permute-done.7.x_ref.refs_4_, ...), custom_call_target="tpu_custom_call" | custom-call | flops 2415919104 | tf_op jit(solution)/shard_map/forward/pallas_call | solution.py:231
  52.9 4.7 %collective-permute-start.5 = (bf16[128,1024]{1,0:T(8,128)(2,1)S(1)}, bf16[128,1024]{1,0:T(8,128)(2,1)S(1)}, u32[]{:S(2)}, u32[]{:S(2)}) collective-permute-start(bf16[128,1024]{1,0:T(8,128)(2,1)S(1)} %add_convert_fusion.5), channel_id=1, source_target_pairs={{0,2},{1,3},{2,0},{3,1},{4,6},{5,7},{6,4},{7,5},{8,10},{9,11},{10,... | collective-permute-start | bytes 786440 | tf_op jit(solution)/shard_map/ppermute | solution.py:118
  57.7 2.3 %collective-permute-start.14 = (bf16[128,1024]{1,0:T(8,128)(2,1)S(1)}, bf16[128,1024]{1,0:T(8,128)(2,1)S(1)}, u32[]{:S(2)}, u32[]{:S(2)}) collective-permute-start(bf16[128,1024]{1,0:T(8,128)(2,1)S(1)} %add_convert_fusion.4), channel_id=1, source_target_pairs={{0,2},{1,3},{6,4},{7,5},{8,10},{9,11},{14,12},{15,13},{16,18},{17,... | collective-permute-start | bytes 786440 | tf_op jit(solution)/shard_map/ppermute | solution.py:122
  60.0 9.5 %weight_terms.1 = (bf16[1024,768]{1,0:T(8,128)(2,1)S(1)}, bf16[2,128,1152]{2,1,0:T(8,128)(2,1)S(1)}, bf16[2,128,1152]{2,1,0:T(8,128)(2,1)S(1)}, bf16[2,128,1152]...) custom-call(s32[3]{0:T(128)S(1)} %pad_add_fusion.at, ...), custom_call_target="tpu_custom_call" | custom-call | flops 12884901888 | tf_op jit(solution)/shard_map/weight_terms/pallas_call | solution.py:231
  73.7 4.0 %backward.1 = (bf16[4,128,1024]{2,1,0:T(8,128)(2,1)S(1)}, bf16[4,128,1024]{2,1,0:T(8,128)(2,1)S(1)}) custom-call(s32[3]{0:T(128)S(1)} %pad_add_fusion.at, bf16[1024,768]{1,0:T(8,128)(2,1)S(1)} %get-tuple-element.55.p_ref, bf16[1024,768]{1,0:T(8,128)(2,1)S(1)} %get-tuple-element.57.q_ref, bf16[2,1024,768]{2,1,0:T(8,128)(2,1)S(1)} %copy-done.3), custom_call_target="tpu_custom_call" | custom-call | flops 6442450944 | tf_op jit(solution)/shard_map/backward/pallas_call | solution.py:231
  77.7 7.0 %collective-permute-done.28 = bf16[2,128,1152]{2,1,0:T(8,128)(2,1)S(1)} collective-permute-done((bf16[2,128,1152]{2,1,0:T(8,128)(2,1)S(1)}, bf16[2,128,1152]{2,1,0:T(8,128)(2,1)S(1)}, u32[]{:S(2)}, u32[]{:S(2)}) %collective-permute-start.28) | collective-permute-done | bytes 589856 | tf_op jit(solution)/shard_map/ppermute | solution.py:118
  84.7 9.5 %collective-permute-start.15 = (bf16[128,1024]{1,0:T(8,128)(2,1)S(1)}, bf16[128,1024]{1,0:T(8,128)(2,1)S(1)}, u32[]{:S(2)}, u32[]{:S(2)}) collective-permute-start(bf16[128,1024]{1,0:T(8,128)(2,1)S(1)} %add_convert_fusion.3), channel_id=1, source_target_pairs={{0,4},{1,5},{2,6},{3,7},{4,0},{5,1},{6,2},{7,3},{8,12},{9,13},{10,... | collective-permute-start | bytes 786440 | tf_op jit(solution)/shard_map/ppermute | solution.py:118
  98.4 7.2 %collective-permute-done.15 = bf16[128,1024]{1,0:T(8,128)(2,1)S(1)} collective-permute-done((bf16[128,1024]{1,0:T(8,128)(2,1)S(1)}, bf16[128,1024]{1,0:T(8,128)(2,1)S(1)}, u32[]{:S(2)}, u32[]{:S(2)}) %collective-permute-start.15) | collective-permute-done | bytes 262176 | tf_op jit(solution)/shard_map/ppermute | solution.py:118
  108.2 10.2 %collective-permute-done.33 = bf16[128,1152]{1,0:T(8,128)(2,1)S(1)} collective-permute-done((bf16[128,1152]{1,0:T(8,128)(2,1)S(1)}, bf16[128,1152]{1,0:T(8,128)(2,1)S(1)}, u32[]{:S(2)}, u32[]{:S(2)}) %collective-permute-start.33) | collective-permute-done | bytes 294944 | tf_op jit(solution)/shard_map/ppermute | solution.py:118
  121.9 3.5 %collective-permute-start.26 = (bf16[128,1024]{1,0:T(8,128)(2,1)S(1)}, bf16[128,1024]{1,0:T(8,128)(2,1)S(1)}, u32[]{:S(2)}, u32[]{:S(2)}) collective-permute-start(bf16[128,1024]{1,0:T(8,128)(2,1)S(1)} %get-tuple-element.79), channel_id=1, source_target_pairs={{0,2},{1,3},{6,4},{7,5},{8,10},{9,11},{14,12},{15,13},{16,18},{17,... | collective-permute-start | bytes 786440 | tf_op jit(solution)/shard_map/ppermute | solution.py:122
  125.5 2.5 %collective-permute-done.32 = bf16[128,1152]{1,0:T(8,128)(2,1)S(1)} collective-permute-done((bf16[128,1152]{1,0:T(8,128)(2,1)S(1)}, bf16[128,1152]{1,0:T(8,128)(2,1)S(1)}, u32[]{:S(2)}, u32[]{:S(2)}) %collective-permute-start.32) | collective-permute-done | bytes 294944 | tf_op jit(solution)/shard_map/ppermute | solution.py:118
  128.7 2.5 %collective-permute-done.26 = bf16[128,1024]{1,0:T(8,128)(2,1)S(1)} collective-permute-done((bf16[128,1024]{1,0:T(8,128)(2,1)S(1)}, bf16[128,1024]{1,0:T(8,128)(2,1)S(1)}, u32[]{:S(2)}, u32[]{:S(2)}) %collective-permute-start.26) | collective-permute-done | bytes 262176 | tf_op jit(solution)/shard_map/ppermute | solution.py:122
  131.2 2.5 %collective-permute-start.24 = (bf16[128,1024]{1,0:T(8,128)(2,1)S(1)}, bf16[128,1024]{1,0:T(8,128)(2,1)S(1)}, u32[]{:S(2)}, u32[]{:S(2)}) collective-permute-start(bf16[128,1024]{1,0:T(8,128)(2,1)S(1)} %get-tuple-element.78), channel_id=1, source_target_pairs={{0,2},{1,3},{2,0},{3,1},{4,6},{5,7},{6,4},{7,5},{8,10},{9,11},{10,... | collective-permute-start | bytes 786440 | tf_op jit(solution)/shard_map/ppermute | solution.py:118
  133.8 2.4 %collective-permute-start.27 = (bf16[128,1024]{1,0:T(8,128)(2,1)S(1)}, bf16[128,1024]{1,0:T(8,128)(2,1)S(1)}, u32[]{:S(2)}, u32[]{:S(2)}) collective-permute-start(bf16[128,1024]{1,0:T(8,128)(2,1)S(1)} %fusion.4), channel_id=1, source_target_pairs={{0,4},{1,5},{2,6},{3,7},{4,0},{5,1},{6,2},{7,3},{8,12},{9,13},{10,... | collective-permute-start | bytes 786440 | tf_op jit(solution)/shard_map/ppermute | solution.py:118
  138.4 2.9 %collective-permute-done.24 = bf16[128,1024]{1,0:T(8,128)(2,1)S(1)} collective-permute-done((bf16[128,1024]{1,0:T(8,128)(2,1)S(1)}, bf16[128,1024]{1,0:T(8,128)(2,1)S(1)}, u32[]{:S(2)}, u32[]{:S(2)}) %collective-permute-start.24) | collective-permute-done | bytes 262176 | tf_op jit(solution)/shard_map/ppermute | solution.py:118
  141.3 10.8 %collective-permute-done.27 = bf16[128,1024]{1,0:T(8,128)(2,1)S(1)} collective-permute-done((bf16[128,1024]{1,0:T(8,128)(2,1)S(1)}, bf16[128,1024]{1,0:T(8,128)(2,1)S(1)}, u32[]{:S(2)}, u32[]{:S(2)}) %collective-permute-start.27) | collective-permute-done | bytes 262176 | tf_op jit(solution)/shard_map/ppermute | solution.py:118
  (100 shorter events, 34.8 us)
Async XLA Ops:
  5.7 18.4 %collective-permute-start.7 = (bf16[128,1152]{1,0:T(8,128)(2,1)}, bf16[128,1152]{1,0:T(8,128)(2,1)S(1)}, u32[]{:S(2)}, u32[]{:S(2)}) collective-permute-start(bf16[128,1152]{1,0:T(8,128)(2,1)} %message.1.x_ref.refs_0_), channel_id=1, source_target_pairs={{0,4},{1,5},{2,6},{3,7},{4,0},{5,1},{6,2},{7,3},{8,12},{9,13},{10,... | collective-permute-start | bytes 884744 | tf_op jit(solution)/shard_map/ppermute | solution.py:118
  9.7 18.4 %collective-permute-start.6 = (bf16[128,1152]{1,0:T(8,128)(2,1)}, bf16[128,1152]{1,0:T(8,128)(2,1)S(1)}, u32[]{:S(2)}, u32[]{:S(2)}) collective-permute-start(bf16[128,1152]{1,0:T(8,128)(2,1)} %message.1.x_ref.refs_0_), channel_id=1, source_target_pairs={{2,4},{3,5},{4,2},{5,3},{10,12},{11,13},{12,10},{13,11},{18,20},{1... | collective-permute-start | bytes 884744 | tf_op jit(solution)/shard_map/ppermute | solution.py:122
  10.4 21.9 %collective-permute-start.2 = (bf16[128,1152]{1,0:T(8,128)(2,1)}, bf16[128,1152]{1,0:T(8,128)(2,1)S(1)}, u32[]{:S(2)}, u32[]{:S(2)}) collective-permute-start(bf16[128,1152]{1,0:T(8,128)(2,1)} %message.1.x_ref.refs_0_), channel_id=1, source_target_pairs={{0,2},{1,3},{2,0},{3,1},{4,6},{5,7},{6,4},{7,5},{8,10},{9,11},{10,... | collective-permute-start | bytes 884744 | tf_op jit(solution)/shard_map/ppermute | solution.py:118
  13.3 24.4 %collective-permute-start = (bf16[128,1152]{1,0:T(8,128)(2,1)}, bf16[128,1152]{1,0:T(8,128)(2,1)S(1)}, u32[]{:S(2)}, u32[]{:S(2)}) collective-permute-start(bf16[128,1152]{1,0:T(8,128)(2,1)} %message.1.x_ref.refs_0_), channel_id=1, source_target_pairs={{0,1},{1,0},{2,3},{3,2},{4,5},{5,4},{6,7},{7,6},{8,9},{9,8},{10,11... | collective-permute-start | bytes 884744 | tf_op jit(solution)/shard_map/ppermute | solution.py:118
  13.3 37.6 %collective-permute-start.17 = (bf16[128,1024]{1,0:T(8,128)(2,1)}, bf16[128,1024]{1,0:T(8,128)(2,1)S(1)}, u32[]{:S(2)}, u32[]{:S(2)}) collective-permute-start(bf16[128,1024]{1,0:T(8,128)(2,1)} %refs_8_), channel_id=1, source_target_pairs={{0,2},{1,3},{2,0},{3,1},{4,6},{5,7},{6,4},{7,5},{8,10},{9,11},{10,... | collective-permute-start | bytes 786440 | tf_op jit(solution)/shard_map/ppermute | solution.py:118
  24.1 13.5 %collective-permute-start.8 = (bf16[128,1152]{1,0:T(8,128)(2,1)S(1)}, bf16[128,1152]{1,0:T(8,128)(2,1)S(1)}, u32[]{:S(2)}, u32[]{:S(2)}) collective-permute-start(bf16[128,1152]{1,0:T(8,128)(2,1)S(1)} %collective-permute-done.7.x_ref.refs_4_), channel_id=1, source_target_pairs={{2,0},{3,1},{4,6},{5,7},{10,8},{11,9},{12,14},{13,15},{18,16},{19,... | collective-permute-start | bytes 884744 | tf_op jit(solution)/shard_map/ppermute | solution.py:122
  28.1 23.3 %collective-permute-start.19 = (bf16[128,1024]{1,0:T(8,128)(2,1)}, bf16[128,1024]{1,0:T(8,128)(2,1)S(1)}, u32[]{:S(2)}, u32[]{:S(2)}) collective-permute-start(bf16[128,1024]{1,0:T(8,128)(2,1)} %refs_8_), channel_id=1, source_target_pairs={{0,4},{1,5},{2,6},{3,7},{4,0},{5,1},{6,2},{7,3},{8,12},{9,13},{10,... | collective-permute-start | bytes 786440 | tf_op jit(solution)/shard_map/ppermute | solution.py:118
  32.2 19.3 %collective-permute-start.21 = (bf16[128,1024]{1,0:T(8,128)(2,1)}, bf16[128,1024]{1,0:T(8,128)(2,1)S(1)}, u32[]{:S(2)}, u32[]{:S(2)}) collective-permute-start(bf16[128,1024]{1,0:T(8,128)(2,1)} %refs_8_), channel_id=1, source_target_pairs={{0,6},{1,7},{2,4},{3,5},{4,2},{5,3},{6,0},{7,1},{8,14},{9,15},{10,... | collective-permute-start | bytes 786440 | tf_op jit(solution)/shard_map/ppermute | solution.py:118
  52.1 44.1 %collective-permute-start.1 = (bf16[128,1024]{1,0:T(8,128)(2,1)S(1)}, bf16[128,1024]{1,0:T(8,128)(2,1)S(1)}, u32[]{:S(2)}, u32[]{:S(2)}) collective-permute-start(bf16[128,1024]{1,0:T(8,128)(2,1)S(1)} %get-tuple-element.39), channel_id=1, source_target_pairs={{0,1},{1,0},{2,3},{3,2},{4,5},{5,4},{6,7},{7,6},{8,9},{9,8},{10,11... | collective-permute-start | bytes 786440 | tf_op jit(solution)/shard_map/ppermute | solution.py:118
  52.7 20.0 %collective-permute-start.13 = (bf16[128,1024]{1,0:T(8,128)(2,1)S(1)}, bf16[128,1024]{1,0:T(8,128)(2,1)S(1)}, u32[]{:S(2)}, u32[]{:S(2)}) collective-permute-start(bf16[128,1024]{1,0:T(8,128)(2,1)S(1)} %get-tuple-element.45), channel_id=1, source_target_pairs={{0,1},{1,0},{2,3},{3,2},{4,5},{5,4},{6,7},{7,6},{8,9},{9,8},{10,11... | collective-permute-start | bytes 786440 | tf_op jit(solution)/shard_map/ppermute | solution.py:118
  52.9 43.3 %collective-permute-start.5 = (bf16[128,1024]{1,0:T(8,128)(2,1)S(1)}, bf16[128,1024]{1,0:T(8,128)(2,1)S(1)}, u32[]{:S(2)}, u32[]{:S(2)}) collective-permute-start(bf16[128,1024]{1,0:T(8,128)(2,1)S(1)} %add_convert_fusion.5), channel_id=1, source_target_pairs={{0,2},{1,3},{2,0},{3,1},{4,6},{5,7},{6,4},{7,5},{8,10},{9,11},{10,... | collective-permute-start | bytes 786440 | tf_op jit(solution)/shard_map/ppermute | solution.py:118
  57.7 13.5 %collective-permute-start.14 = (bf16[128,1024]{1,0:T(8,128)(2,1)S(1)}, bf16[128,1024]{1,0:T(8,128)(2,1)S(1)}, u32[]{:S(2)}, u32[]{:S(2)}) collective-permute-start(bf16[128,1024]{1,0:T(8,128)(2,1)S(1)} %add_convert_fusion.4), channel_id=1, source_target_pairs={{0,2},{1,3},{6,4},{7,5},{8,10},{9,11},{14,12},{15,13},{16,18},{17,... | collective-permute-start | bytes 786440 | tf_op jit(solution)/shard_map/ppermute | solution.py:122
  69.6 15.2 %collective-permute-start.28 = (bf16[2,128,1152]{2,1,0:T(8,128)(2,1)S(1)}, bf16[2,128,1152]{2,1,0:T(8,128)(2,1)S(1)}, u32[]{:S(2)}, u32[]{:S(2)}) collective-permute-start(bf16[2,128,1152]{2,1,0:T(8,128)(2,1)S(1)} %get-tuple-element.61), channel_id=1, source_target_pairs={{0,8},{8,0},{16,24},{24,16},{1,9},{9,1},{17,25},{25,17},{2,10},{10... | collective-permute-start | bytes 1769480 | tf_op jit(solution)/shard_map/ppermute | solution.py:118
  71.1 23.3 %collective-permute-start.30 = (bf16[2,128,1152]{2,1,0:T(8,128)(2,1)S(1)}, bf16[2,128,1152]{2,1,0:T(8,128)(2,1)S(1)}, u32[]{:S(2)}, u32[]{:S(2)}) collective-permute-start(bf16[2,128,1152]{2,1,0:T(8,128)(2,1)S(1)} %get-tuple-element.66), channel_id=1, source_target_pairs={{0,16},{8,24},{16,0},{24,8},{1,17},{9,25},{17,1},{25,9},{2,18},{10... | collective-permute-start | bytes 1769480 | tf_op jit(solution)/shard_map/ppermute | solution.py:118
  72.7 25.2 %collective-permute-start.11 = (bf16[128,1024]{1,0:T(8,128)(2,1)S(1)}, bf16[128,1024]{1,0:T(8,128)(2,1)S(1)}, u32[]{:S(2)}, u32[]{:S(2)}) collective-permute-start(bf16[128,1024]{1,0:T(8,128)(2,1)S(1)} %add_convert_fusion.4), channel_id=1, source_target_pairs={{2,4},{3,5},{4,2},{5,3},{10,12},{11,13},{12,10},{13,11},{18,20},{1... | collective-permute-start | bytes 786440 | tf_op jit(solution)/shard_map/ppermute | solution.py:122
  84.7 20.8 %collective-permute-start.15 = (bf16[128,1024]{1,0:T(8,128)(2,1)S(1)}, bf16[128,1024]{1,0:T(8,128)(2,1)S(1)}, u32[]{:S(2)}, u32[]{:S(2)}) collective-permute-start(bf16[128,1024]{1,0:T(8,128)(2,1)S(1)} %add_convert_fusion.3), channel_id=1, source_target_pairs={{0,4},{1,5},{2,6},{3,7},{4,0},{5,1},{6,2},{7,3},{8,12},{9,13},{10,... | collective-permute-start | bytes 786440 | tf_op jit(solution)/shard_map/ppermute | solution.py:118
  94.4 13.6 %collective-permute-start.29 = (bf16[128,1152]{1,0:T(8,128)(2,1)S(1)}, bf16[128,1152]{1,0:T(8,128)(2,1)S(1)}, u32[]{:S(2)}, u32[]{:S(2)}) collective-permute-start(bf16[128,1152]{1,0:T(8,128)(2,1)S(1)} %fusion.8), channel_id=1, source_target_pairs={{0,16},{8,24},{16,0},{24,8},{1,17},{9,25},{17,1},{25,9},{2,18},{10... | collective-permute-start | bytes 884744 | tf_op jit(solution)/shard_map/ppermute | solution.py:118
  96.2 25.5 %collective-permute-start.23 = (bf16[4,128,1024]{2,1,0:T(8,128)(2,1)S(1)}, bf16[4,128,1024]{2,1,0:T(8,128)(2,1)S(1)}, u32[]{:S(2)}, u32[]{:S(2)}) collective-permute-start(bf16[4,128,1024]{2,1,0:T(8,128)(2,1)S(1)} %get-tuple-element.59), channel_id=1, source_target_pairs={{0,1},{1,0},{2,3},{3,2},{4,5},{5,4},{6,7},{7,6},{8,9},{9,8},{10,11... | collective-permute-start | bytes 3145736 | tf_op jit(solution)/shard_map/ppermute | solution.py:118
  96.3 23.2 %collective-permute-start.31 = (bf16[2,128,1152]{2,1,0:T(8,128)(2,1)S(1)}, bf16[2,128,1152]{2,1,0:T(8,128)(2,1)S(1)}, u32[]{:S(2)}, u32[]{:S(2)}) collective-permute-start(bf16[2,128,1152]{2,1,0:T(8,128)(2,1)S(1)} %get-tuple-element.67), channel_id=1, source_target_pairs={{0,8},{8,0},{16,24},{24,16},{1,9},{9,1},{17,25},{25,17},{2,10},{10... | collective-permute-start | bytes 1769480 | tf_op jit(solution)/shard_map/ppermute | solution.py:118
  97.9 20.5 %collective-permute-start.33 = (bf16[128,1152]{1,0:T(8,128)(2,1)S(1)}, bf16[128,1152]{1,0:T(8,128)(2,1)S(1)}, u32[]{:S(2)}, u32[]{:S(2)}) collective-permute-start(bf16[128,1152]{1,0:T(8,128)(2,1)S(1)} %fusion.10), channel_id=1, source_target_pairs={{0,8},{8,0},{16,24},{24,16},{1,9},{9,1},{17,25},{25,17},{2,10},{10... | collective-permute-start | bytes 884744 | tf_op jit(solution)/shard_map/ppermute | solution.py:118
  105.6 14.6 %collective-permute-start.34 = (bf16[2,128,1152]{2,1,0:T(8,128)(2,1)S(1)}, bf16[2,128,1152]{2,1,0:T(8,128)(2,1)S(1)}, u32[]{:S(2)}, u32[]{:S(2)}) collective-permute-start(bf16[2,128,1152]{2,1,0:T(8,128)(2,1)S(1)} %get-tuple-element.69), channel_id=1, source_target_pairs={{0,16},{8,24},{16,0},{24,8},{1,17},{9,25},{17,1},{25,9},{2,18},{10... | collective-permute-start | bytes 1769480 | tf_op jit(solution)/shard_map/ppermute | solution.py:118
  108.1 28.1 %collective-permute-start.36 = (bf16[128,1152]{1,0:T(8,128)(2,1)S(1)}, bf16[128,1152]{1,0:T(8,128)(2,1)S(1)}, u32[]{:S(2)}, u32[]{:S(2)}) collective-permute-start(bf16[128,1152]{1,0:T(8,128)(2,1)S(1)} %get-tuple-element.74), channel_id=1, source_target_pairs={{0,4},{1,5},{2,6},{3,7},{4,0},{5,1},{6,2},{7,3},{8,12},{9,13},{10,... | collective-permute-start | bytes 884744 | tf_op jit(solution)/shard_map/ppermute | solution.py:118
  118.4 17.8 %collective-permute-start.37 = (bf16[128,1152]{1,0:T(8,128)(2,1)S(1)}, bf16[128,1152]{1,0:T(8,128)(2,1)S(1)}, u32[]{:S(2)}, u32[]{:S(2)}) collective-permute-start(bf16[128,1152]{1,0:T(8,128)(2,1)S(1)} %get-tuple-element.72), channel_id=1, source_target_pairs={{0,4},{1,5},{2,6},{3,7},{4,0},{5,1},{6,2},{7,3},{8,12},{9,13},{10,... | collective-permute-start | bytes 884744 | tf_op jit(solution)/shard_map/ppermute | solution.py:118
  133.8 18.3 %collective-permute-start.27 = (bf16[128,1024]{1,0:T(8,128)(2,1)S(1)}, bf16[128,1024]{1,0:T(8,128)(2,1)S(1)}, u32[]{:S(2)}, u32[]{:S(2)}) collective-permute-start(bf16[128,1024]{1,0:T(8,128)(2,1)S(1)} %fusion.4), channel_id=1, source_target_pairs={{0,4},{1,5},{2,6},{3,7},{4,0},{5,1},{6,2},{7,3},{8,12},{9,13},{10,... | collective-permute-start | bytes 786440 | tf_op jit(solution)/shard_map/ppermute | solution.py:118
  (20 other events, 163.4 us)

commit v3 on v0

--- a/solution.py
+++ b/solution.py
@@ -1,9 +1,14 @@
+import functools
+
 import jax
 import jax.numpy as jnp
 from jax import lax
+from jax.experimental import pallas as pl
+from jax.experimental.pallas import tpu as pltpu
 from jax.sharding import PartitionSpec as P
 
 grad_scale = 0.0625
+vmem = 12 << 20
 
 
 def partner_2(block, axis, distance):
@@ -28,7 +33,7 @@
     return jnp.take(stacked, index, axis=0)
 
 
-def local(tokens, routes, gates, cotangent, partner, w_gate_up, w_down):
+def routed(tokens, routes, gates, cotangent, partner, w_gate_up, w_down):
     count_tokens, top_k = routes.shape
     width = tokens.shape[1]
     hidden_units = w_down.shape[2]
@@ -109,6 +114,335 @@
     )
 
 
+def swap_with(block, axis, mask):
+    return lax.ppermute(block, axis, [(i, i ^ mask) for i in range(lax.axis_size(axis))])
+
+
+def send(block, pairs):
+    return lax.ppermute(block, "expert", [(2 * a + c, 2 * b + c) for a, b in pairs for c in range(2)])
+
+
+def both_cores(block):
+    return block, swap_with(block, "expert", 1)
+
+
+def contract(a, b, i, j):
+    return lax.dot_general(a, b, (((i,), (j,)), ((), ())), preferred_element_type=jnp.float32)
+
+
+def message_kernel(tokens_ref, cotangent_ref, routes_ref, gates_ref, out_ref, again_ref, *, experts):
+    rows, width = tokens_ref.shape
+    lanes = out_ref.shape[1] - 2 * width
+    out_ref[:, :width] = tokens_ref[...]
+    out_ref[:, width : 2 * width] = cotangent_ref[...]
+    lane = lax.broadcasted_iota(jnp.int32, (rows, lanes), 1)
+    expert = lane % experts
+    gate = jnp.zeros((rows, lanes), jnp.float32)
+    routes, gates = routes_ref[...].T, gates_ref[...].T
+    for k in range(routes.shape[1]):
+        gate = gate + jnp.where(routes[:, k : k + 1] == expert, gates[:, k : k + 1], 0.0)
+    high = gate.astype(jnp.bfloat16).astype(jnp.float32)
+    middle = (gate - high).astype(jnp.bfloat16).astype(jnp.float32)
+    low = gate - high - middle
+    third = lane // experts
+    value = jnp.where(third == 0, high, jnp.where(third == 1, middle, jnp.where(third == 2, low, 0.0)))
+    out_ref[:, 2 * width :] = value.astype(out_ref.dtype)
+    again_ref[...] = out_ref[...]
+
+
+def message(tokens, cotangent, routes, gates, experts):
+    rows, width = tokens.shape
+    return pl.pallas_call(
+        functools.partial(message_kernel, experts=experts),
+        out_shape=[jax.ShapeDtypeStruct((n, 2 * width + 128), tokens.dtype) for n in (rows, rows)],
+        cost_estimate=pl.CostEstimate(flops=0, bytes_accessed=1 << 20, transcendentals=0),
+        name="message",
+    )(tokens, cotangent, routes.T, gates.T)
+
+
+def gate_of(ref, width, expert, experts):
+    values = ref[:, 2 * width :].astype(jnp.float32)
+    lane = lax.broadcasted_iota(jnp.int32, values.shape, 1)
+    chosen = jnp.logical_and(lane % experts == expert, lane < 3 * experts)
+    return jnp.sum(jnp.where(chosen, values, 0.0), axis=1, keepdims=True)
+
+
+def marked(kernel, count, *refs):
+    refs[count - 1][...] = jnp.zeros_like(refs[count - 1])
+    kernel(*refs[: count - 1], *refs[count:])
+
+
+def call(kernel, name, scalars, operands, outs, flops, places=None, scratch=()):
+    outs = [*outs, ((8, 128), jnp.float32)]
+    places = [*(places or [pltpu.VMEM] * (len(outs) - 1)), pltpu.VMEM]
+    return pl.pallas_call(
+        functools.partial(marked, kernel, 1 + len(operands) + len(outs)),
+        in_specs=[pl.BlockSpec(memory_space=pltpu.SMEM)]
+        + [pl.BlockSpec(memory_space=pltpu.VMEM)] * len(operands),
+        out_specs=[pl.BlockSpec(memory_space=place) for place in places],
+        out_shape=[jax.ShapeDtypeStruct(shape, dtype) for shape, dtype in outs],
+        scratch_shapes=list(scratch),
+        compiler_params=pltpu.CompilerParams(vmem_limit_bytes=vmem),
+        cost_estimate=pl.CostEstimate(flops=int(flops), bytes_accessed=0, transcendentals=0),
+        name=name,
+    )(scalars, *operands)
+
+
+def hold_kernel(*refs):
+    del refs
+
+
+def hold(values, *earlier):
+    anywhere = pl.BlockSpec(memory_space=pl.ANY)
+    n = len(values)
+    return pl.pallas_call(
+        hold_kernel,
+        in_specs=[anywhere] * (n + len(earlier)),
+        out_specs=[anywhere] * n,
+        out_shape=[jax.ShapeDtypeStruct(x.shape, x.dtype) for x in values],
+        input_output_aliases={i: i for i in range(n)},
+        compiler_params=pltpu.CompilerParams(vmem_limit_bytes=vmem),
+        cost_estimate=pl.CostEstimate(flops=0, bytes_accessed=0, transcendentals=0),
+        name="hold",
+    )(*values, *earlier)
+
+
+def inner_kernel(at, xs, up_ref, down_ref, h_ref, p_ref, experts):
+    width, units = up_ref.shape[1], down_ref.shape[2]
+    x = jnp.concatenate([ref[:, :width] for ref in xs], axis=0)
+    c = jnp.concatenate([ref[:, width : 2 * width] for ref in xs], axis=0)
+    for i in range(2):
+        slot = jnp.bitwise_xor(at[1], i)
+        pre = jnp.dot(x, up_ref[slot], preferred_element_type=jnp.float32)
+        back = jnp.dot(c, down_ref[slot], preferred_element_type=jnp.float32)
+        gate_pre, up_pre = pre[:, :units], pre[:, units:]
+        expert = 2 * at[2] + slot
+        gate = [gate_of(ref, width, expert, experts) for ref in xs]
+        gate = jnp.concatenate(gate, axis=0)
+        sig = 0.5 * jnp.tanh(0.5 * gate_pre) + 0.5
+        scaled = gate * sig
+        silu = scaled * gate_pre
+        h_ref[i] = (silu * up_pre).astype(h_ref.dtype)
+        p_ref[i, :, :units] = (back * up_pre * (scaled + silu * (1.0 - sig))).astype(p_ref.dtype)
+        p_ref[i, :, units:] = (back * silu).astype(p_ref.dtype)
+
+
+def outer_kernel(at, h_ref, p_ref, up_ref, down_ref, *outs):
+    kept_ref, sent_ref = outs[-2:]
+    width = up_ref.shape[1]
+    half = kept_ref.shape[0]
+    slots = [jnp.bitwise_xor(at[1], i) for i in range(2)]
+    out = sum(contract(h_ref[i], down_ref[slots[i]], 1, 1) for i in range(2))
+    kept_ref[:, :width] = out[:half].astype(kept_ref.dtype)
+    sent_ref[:, :width] = out[half:].astype(sent_ref.dtype)
+    out = sum(contract(p_ref[i], up_ref[slots[i]], 1, 1) for i in range(2))
+    kept_ref[:, width:] = out[:half].astype(kept_ref.dtype)
+    sent_ref[:, width:] = out[half:].astype(sent_ref.dtype)
+
+
+def near_kernel(at, *refs, pieces, experts):
+    xs, (up_ref, down_ref, h_ref, p_ref, kept_ref, sent_ref) = refs[:pieces], refs[pieces:]
+    inner_kernel(at, xs, up_ref, down_ref, h_ref, p_ref, experts)
+    outer_kernel(at, h_ref, p_ref, up_ref, down_ref, kept_ref, sent_ref)
+
+
+def far_kernel(at, *refs, pieces, experts):
+    inner_kernel(at, refs[:pieces], *refs[pieces:], experts)
+
+
+def term(xs, ps, hs, order, column, width):
+    units = hs[0].shape[2]
+    x = jnp.concatenate([ref[:, pl.ds(column, width // 4)] for ref in xs], axis=0)
+    c = jnp.concatenate([ref[:, pl.ds(width + column, width // 4)] for ref in xs], axis=0)
+    p = jnp.concatenate([ref[order] for ref in ps], axis=0)
+    h = jnp.concatenate([ref[order] for ref in hs], axis=0)
+    return contract(x, p, 0, 0), contract(c, h, 0, 0)
+
+
+def early_kernel(at, *refs, pieces):
+    xs, ps, hs, outs = refs[:pieces], refs[pieces : pieces + 3], refs[pieces + 3 : pieces + 6], refs[pieces + 6 :]
+    units = hs[0].shape[2]
+    quarter = outs[0].shape[1]
+    for order in range(2):
+        for i in range(4):
+            column = pl.multiple_of(jnp.bitwise_xor(at[0], i) * quarter, quarter)
+            first, last = term(xs, ps, hs, order, column, 4 * quarter)
+            outs[order][i, :, : 2 * units] = first.astype(outs[order].dtype)
+            outs[order][i, :, 2 * units :] = last.astype(outs[order].dtype)
+
+
+def late_kernel(at, *refs, pieces, order):
+    xs, (p_ref, h_ref, sum_ref), outs = refs[:pieces], refs[pieces : pieces + 3], refs[-4:]
+    send_a, send_b, keep_a, keep_b = outs
+    units = h_ref.shape[2]
+    quarter = sum_ref.shape[1]
+    rows = quarter // 2
+    for i in (1, 3, 2, 0):
+        column = pl.multiple_of(jnp.bitwise_xor(at[0], i) * quarter, quarter)
+        first, last = term(xs, (p_ref,), (h_ref,), order, column, 4 * quarter)
+        first = ((first + sum_ref[i, :, : 2 * units]) * grad_scale).astype(send_a.dtype)
+        last = ((last + sum_ref[i, :, 2 * units :]) * grad_scale).astype(send_a.dtype)
+        ref_a = send_a if i & 1 else keep_a
+        ref_b = send_b if i & 2 else keep_b
+        ref_a[i >> 1, :, : 2 * units] = first[:rows]
+        ref_a[i >> 1, :, 2 * units :] = last[:rows]
+        ref_b[i & 1, :, : 2 * units] = first[rows:]
+        ref_b[i & 1, :, 2 * units :] = last[rows:]
+
+
+def far_block_kernel(at, middle, ends, *refs):
+    refs[-1][...] = jnp.where(at[4] == 1, middle[...], ends[...])
+
+
+def line_kernel(at, kept, other, *outs):
+    out = outs[-1]
+    out[...] = (kept[...].astype(jnp.float32) + other[...].astype(jnp.float32)).astype(out.dtype)
+
+
+def pair_kernel(at, got_a, got_b, keep_a, keep_b, *refs):
+    f32 = jnp.float32
+    more, results = refs[: (len(refs) - 3) * 5 // 7], refs[-2:]
+    end_a, end_b, own = refs[len(more) : len(more) + 3]
+    for half, (got, keep, out) in enumerate(((got_a, keep_a, end_a), (got_b, keep_b, end_b))):
+        out[...] = (keep[1].astype(f32) + got[1].astype(f32)).astype(out.dtype)
+        own[half] = keep[0].astype(f32) + got[0].astype(f32)
+    if more:
+        value = sum(ref[...].astype(f32) for ref in more).astype(results[0].dtype)
+        for i, ref in enumerate(results):
+            ref[...] = value[:, i * ref.shape[1] : (i + 1) * ref.shape[1]]
+
+
+def lead_kernel(at, end_a, end_b, own, done, sent_a, sent_b, first):
+    del done
+    for half, (end, sent) in enumerate(((end_a, sent_a), (end_b, sent_b))):
+        value = own[half] + end[...].astype(jnp.float32)
+        first[half] = value
+        sent[...] = value.astype(sent.dtype)
+
+
+def finish_kernel(at, first, second, end_a, end_b, traded_a, traded_b, gu_ref, dn_ref):
+    columns = gu_ref.shape[2]
+    rows = end_a.shape[0]
+    for half, (end, traded) in enumerate(((end_a, traded_a), (end_b, traded_b))):
+        here = slice(half * rows, (half + 1) * rows)
+        lead = jnp.where(at[3] == 1, traded[...].astype(jnp.float32), first[half])
+        for slot, value in ((at[1], lead), (1 - at[1], second[half] + end[...].astype(jnp.float32))):
+            gu_ref[slot, here, :] = value[:, :columns]
+            dn_ref[slot, here, :] = value[:, columns:]
+
+
+def dense(tokens, routes, gates, cotangent, partner, w_gate_up, w_down):
+    count_tokens, _ = routes.shape
+    units = w_down.shape[2]
+    n_expert = lax.axis_size("expert")
+    bf16, f32, i32 = jnp.bfloat16, jnp.float32, jnp.int32
+    me = lax.axis_index("expert")
+    partner_of = table_lookup(partner, me * 2 + jnp.arange(2, dtype=i32))
+    moved = partner_of // 2 != me
+    flip = moved[1].astype(i32)
+    trades = jnp.any(moved).astype(i32)
+    inner = (me // 2 == 1) | (me // 2 == 2)
+
+    experts = 2 * n_expert
+    width = tokens.shape[1]
+    n = 2 * count_tokens
+    at = jnp.stack([lax.axis_index("dp"), flip, me, trades, inner.astype(i32)])
+    flops = 4 * n * width * units
+    weights = (w_gate_up, w_down)
+    inner_outs = [((2, n, units), bf16), ((2, n, 2 * units), bf16)]
+    outer_outs = [((count_tokens, 2 * width), bf16)] * 2
+
+    rows, columns = width // 8, 3 * units
+    part = [((2, rows, columns), bf16)] * 4
+    one_block = ((rows, columns), bf16)
+    both = ((2, rows, columns), f32)
+
+    block, again = message(tokens, cotangent, routes, gates, experts)
+    two = swap_with(block, "expert", 4)
+    one = swap_with(block, "expert", 2)
+
+    def near(pieces, cost):
+        kernel = functools.partial(near_kernel, pieces=len(pieces), experts=experts)
+        outs = inner_outs + outer_outs
+        return call(kernel, "near_block", at, (*pieces, *weights), outs, cost * flops)
+
+    ends = send(two, [(1, 0), (2, 3)])
+    (again,) = hold([again], two)
+    middle = send(again, [(1, 2), (2, 1)])
+    pieces = [both_cores(block)]
+    passes = [near(pieces[0], 12)]
+    (one,) = hold([one], passes[0][4])
+    pieces += [both_cores(one), both_cores(two)]
+    passes += [near(pieces[1], 12), near(pieces[2], 15)]
+    hidden, grads, kept, sent, _ = map(list, zip(*passes))
+    flat = [piece for block in pieces for piece in block]
+    *sums, done = call(
+        functools.partial(early_kernel, pieces=len(flat)),
+        "early_terms",
+        at,
+        (*flat, *grads, *hidden),
+        [((4, width // 4, 3 * units), f32)] * 2,
+        27 * flops,
+    )
+    other = [swap_with(block, "expert", 1) for block in sent]
+
+    def line(k, *earlier):
+        operands = (kept[k], other[k], *earlier)
+        going, done = call(line_kernel, "line_terms", at, operands, outer_outs[:1], 0)
+        return swap_with(going, "expert", 2 * k), done
+
+    (got_one, mark_one), (got_two, mark_two) = line(1), line(2)
+
+    far, _ = call(far_block_kernel, "far_block", at, (middle, ends, done, mark_one, mark_two), [(block.shape, bf16)], 0)
+    far = both_cores(far)
+    kernel = functools.partial(far_kernel, pieces=2, experts=experts)
+    h, p, _ = call(kernel, "far_hidden", at, (*far, *weights), inner_outs, 12 * flops)
+
+    def late(i, *earlier):
+        kernel = functools.partial(late_kernel, pieces=2, order=i)
+        return call(kernel, "late_terms", at, (*far, p, h, sums[i], *earlier), part, 6 * flops)
+
+    def halves(send_a, send_b, keep_a, keep_b, more):
+        got_a, got_b = swap_with(send_a, "dp", 1), swap_with(send_b, "dp", 2)
+        operands = (got_a, got_b, keep_a, keep_b, *more)
+        outs = [one_block, one_block, both] + [((count_tokens, width), bf16)] * (2 if more else 0)
+        end_a, end_b, own, *results, _ = call(pair_kernel, "pair_terms", at, operands, outs, 0)
+        return swap_with(end_a, "dp", 2), swap_with(end_b, "dp", 1), own, results
+
+    *first, done = late(0)
+    *second, done = late(1, done)
+    k, s, _ = call(outer_kernel, "far_results", at, (h, p, *weights, done), outer_outs, 12 * flops)
+    kept.append(k)
+    other.append(swap_with(s, "expert", 1))
+    got_three, done = line(3, got_one, got_two)
+    end_a, end_b, own, _ = halves(*first, [])
+    *leading, head, _ = call(
+        lead_kernel, "lead_terms", at, (end_a, end_b, own, done), [one_block, one_block, both], 0
+    )
+    traded = [swap_with(half, "expert", n_expert // 2) for half in leading]
+    more = [kept[0], other[0], got_one, got_two, got_three]
+    end_a, end_b, tail, (mixed, grad_tokens) = halves(*second, more)
+    grad_gu, grad_dn, _ = call(
+        finish_kernel,
+        "finish",
+        at,
+        (head, tail, end_a, end_b, *traded),
+        [((2, 2 * rows, 2 * units), f32), ((2, 2 * rows, units), f32)],
+        0,
+    )
+    return mixed, grad_tokens, grad_gu, grad_dn
+
+
+def local(tokens, routes, gates, cotangent, partner, w_gate_up, w_down):
+    count_tokens, top_k = routes.shape
+    slots = w_gate_up.shape[0]
+    experts_all = lax.axis_size("expert") * slots
+    line = lax.axis_size("dp") == 4 and lax.axis_size("expert") == 8
+    few = experts_all <= 4 * top_k and slots == 2
+    step = dense if few and line else routed
+    return step(tokens, routes, gates, cotangent, partner, w_gate_up, w_down)
+
+
 def solution(mesh):
     in_specs = (
         P(("dp", "expert"), None),

time: 573 us -> 136 us (0.24)
  waiting for transfers between devices: 419 us -> 66 us
  local copies, waits for them, and re-layouts: 56.2 us -> 5.1 us
  Pallas kernels: 0 us -> 36.6 us
  matrix products: 30.5 us -> 0 us
  other arithmetic: 30.2 us -> 1.48 us
  between operations: 14.3 us -> 2.06 us
    all_to_all x4 -> x0, waiting for transfers between devices: 288 us -> none  [the longest x1 160 us: local(): lax.all_to_all(sending_rows, 'expert', split_axis=0, concat_axis=0, tiled...]
    ppermute x1 -> x25, waiting for transfers between devices: 131 us -> 66 us  [the longest x23 65.4 us: swap_with(): lax.ppermute(block, axis, [(i, i ^ mask) for i in range(lax.axis_size(axi...]
    pallas_call x0 -> x19, Pallas kernels: none -> 36.6 us  [the longest x16 34.1 us: call(): pl.pallas_call(functools.partial(marked, kernel, 1 + len(operands) + len(...]
    gather x6 -> x0, local copies, waits for them, and re-layouts: 33.3 us -> none  [the longest x2 9.06 us: pick_slots(): return jnp.take(stacked, index, axis=0)]
    dot_general x7 -> x0, matrix products: 30.5 us -> none  [the longest x1 6.81 us: local(): jnp.einsum('sjcd,jdf->sjcf', arrived, weight_gu, preferred_element_type=j...]
    ppermute x1 -> x25, starting transfers between devices: 2.92 us -> 24.3 us  [the longest x23 22.1 us: swap_with(): lax.ppermute(block, axis, [(i, i ^ mask) for i in range(lax.axis_size(axi...]
    all_to_all x4 -> x0, starting transfers between devices: 18.7 us -> none  [the longest x1 6.59 us: local(): lax.all_to_all(sending_rows, 'expert', split_axis=0, concat_axis=0, tiled...]
    concatenate x2 -> x0, other arithmetic: 10.3 us -> none  [pick_slots(): stacked = jnp.concatenate([own_slots, received], axis=0)]
  transfers between devices with their start and end apart: 6 -> 25, of which waited for: 5 -> 10; matrix products, arithmetic and copies ran while one was open for 12% -> 2% of each run, Pallas kernels for 0% -> 23%
where the time goes in v3:
time: 136 us
  waiting for transfers between devices  66 us (49%)
  Pallas kernels  36.6 us (27%)
  starting transfers between devices  24.3 us (18%)
  local copies, waits for them, and re-layouts  5.1 us (4%)
  between operations  2.06 us (2%)
  other arithmetic  1.48 us (1%)
    ppermute x23, waiting for transfers between devices, swap_with(): lax.ppermute(block, axis, [(i, i ^ mask) for i in range(lax.axis_size(axi...  65.4 us
    pallas_call x16, Pallas kernels, call(): pl.pallas_call(functools.partial(marked, kernel, 1 + len(operands) + len(...  34.1 us
    ppermute x23, starting transfers between devices, swap_with(): lax.ppermute(block, axis, [(i, i ^ mask) for i in range(lax.axis_size(axi...  22.1 us
    unnamed x12, local copies, waits for them, and re-layouts  4.42 us
  transfers between devices with their start and end apart: 25, of which 10 were waited for; matrix products, arithmetic and copies ran while one was open for 2% of the time, Pallas kernels for 23%

profile of v3, /device:TPU:0, one launch (start us, length us, event | category | flops | bytes accessed | tf_op | source)
XLA Modules:
  0.0 135.6 jit_solution(14044134031939370041)
XLA Ops:
  0.6 2.6 %message.1 = (bf16[128,2176]{1,0:T(8,128)(2,1)}, bf16[128,2176]{1,0:T(8,128)(2,1)}) custom-call(bf16[128,1024]{1,0:T(8,128)(2,1)} %tokens_ref.1, bf16[128,1024]{1,0:T(8,128)(2,1)} %cotangent_ref.1, s32[8,128]{1,0:T(8,128)} %bitcast.6, f32[8,128]{1,0:T(8,128)} %bitcast.7), custom_call_target="tpu_custom_call" | custom-call | bytes 1048576 | tf_op jit(solution)/shard_map/message/pallas_call | solution.py:155
  3.7 2.6 %collective-permute-start.4 = (bf16[128,2176]{1,0:T(8,128)(2,1)}, bf16[128,2176]{1,0:T(8,128)(2,1)S(1)}, u32[]{:S(2)}, u32[]{:S(2)}) collective-permute-start(bf16[128,2176]{1,0:T(8,128)(2,1)} %get-tuple-element.57.refs_1_), channel_id=1, source_target_pairs={{0,2},{1,3},{2,0},{3,1},{4,6},{5,7},{6,4},{7,5},{8,10},{9,11},{10,... | collective-permute-start | bytes 1671176 | tf_op jit(solution)/shard_map/ppermute | solution.py:118
  6.2 2.6 %collective-permute-start = (bf16[128,2176]{1,0:T(8,128)(2,1)}, bf16[128,2176]{1,0:T(8,128)(2,1)S(1)}, u32[]{:S(2)}, u32[]{:S(2)}) collective-permute-start(bf16[128,2176]{1,0:T(8,128)(2,1)} %get-tuple-element.57.refs_1_), channel_id=1, source_target_pairs={{0,4},{1,5},{2,6},{3,7},{4,0},{5,1},{6,2},{7,3},{8,12},{9,13},{10,... | collective-permute-start | bytes 1671176 | tf_op jit(solution)/shard_map/ppermute | solution.py:118
  12.3 1.9 %copy-done.1 = bf16[2,1024,768]{2,1,0:T(8,128)(2,1)S(1)} copy-done((bf16[2,1024,768]{2,1,0:T(8,128)(2,1)S(1)}, bf16[2,1024,768]{2,1,0:T(8,128)(2,1)}, u32[]{:S(2)}) %copy-start.1) | copy-done | bytes 3145752
  16.7 3.6 %near_block.3 = (bf16[2,256,384]{2,1,0:T(8,128)(2,1)S(1)}, bf16[2,256,768]{2,1,0:T(8,128)(2,1)S(1)}, bf16[128,2048]{1,0:T(8,128)(2,1)S(1)}, bf16[128,2048]{1,0:T(8,128)(2,1)S(1)}, f32[8,128]{1,0:T(8,128)S(1)}) custom-call(s32[5]{0:T(128)S(1)} %stack.28.refs_0_, bf16[128,2176]{1,0:T(8,128)(2,1)S(1)} %copy-done.5, ...), custom_call_target="tpu_custom_call" | custom-call | flops 4831838208 | tf_op jit(solution)/shard_map/near_block/pallas_call | solution.py:178
  20.3 11.3 %collective-permute-done.4.refs_0_ = bf16[128,2176]{1,0:T(8,128)(2,1)S(1)} collective-permute-done((bf16[128,2176]{1,0:T(8,128)(2,1)}, bf16[128,2176]{1,0:T(8,128)(2,1)S(1)}, u32[]{:S(2)}, u32[]{:S(2)}) %collective-permute-start.4) | collective-permute-done | bytes 557088 | tf_op jit(solution)/shard_map/ppermute | solution.py:118
  31.5 2.6 %collective-permute-done.refs_1_.refs_5_ = bf16[128,2176]{1,0:T(8,128)(2,1)S(1)} collective-permute-done((bf16[128,2176]{1,0:T(8,128)(2,1)}, bf16[128,2176]{1,0:T(8,128)(2,1)S(1)}, u32[]{:S(2)}, u32[]{:S(2)}) %collective-permute-start) | collective-permute-done | bytes 557088 | tf_op jit(solution)/shard_map/ppermute | solution.py:118
  36.3 4.0 %near_block.4 = (bf16[2,256,384]{2,1,0:T(8,128)(2,1)S(1)}, bf16[2,256,768]{2,1,0:T(8,128)(2,1)S(1)}, bf16[128,2048]{1,0:T(8,128)(2,1)S(1)}, bf16[128,2048]{1,0:T(8,128)(2,1)S(1)}, f32[8,128]{1,0:T(8,128)}) custom-call(s32[5]{0:T(128)S(1)} %stack.28.refs_0_, bf16[128,2176]{1,0:T(8,128)(2,1)S(1)} %hold.3.refs_1_.refs_3_, ...), custom_call_target="tpu_custom_call" | custom-call | flops 4831838208 | tf_op jit(solution)/shard_map/near_block/pallas_call | solution.py:178
  40.8 4.0 %near_block.5 = (bf16[2,256,384]{2,1,0:T(8,128)(2,1)S(1)}, bf16[2,256,768]{2,1,0:T(8,128)(2,1)S(1)}, bf16[128,2048]{1,0:T(8,128)(2,1)S(1)}, bf16[128,2048]{1,0:T(8,128)(2,1)S(1)}, f32[8,128]{1,0:T(8,128)}) custom-call(s32[5]{0:T(128)S(1)} %stack.28.refs_0_, bf16[128,2176]{1,0:T(8,128)(2,1)S(1)} %collective-permute-done.refs_1_.refs_5_, ...), custom_call_target="tpu_custom_call" | custom-call | flops 6039797760 | tf_op jit(solution)/shard_map/near_block/pallas_call | solution.py:178
  44.8 4.9 %early_terms.1 = (f32[4,256,1152]{2,1,0:T(8,128)S(1)}, f32[4,256,1152]{2,1,0:T(8,128)S(1)}, f32[8,128]{1,0:T(8,128)S(1)}) custom-call(s32[5]{0:T(128)S(1)} %stack.28.refs_0_, bf16[128,2176]{1,0:T(8,128)(2,1)S(1)} %copy-done.5, bf16[128,2176]{1,0:T(8,128)(2,1)S(1)} %collective-permute-done.3.refs_2_, bf16[128,2176]{1,0:T(8,128)(2,1)S(1)} %hold.3.refs_1_.refs_3_, ...), custom_call_target="tpu_custom_call" | custom-call | flops 10871635968 | tf_op jit(solution)/shard_map/early_terms/pallas_call | solution.py:178
  52.9 2.3 %collective-permute-start.13 = (bf16[128,2048]{1,0:T(8,128)(2,1)S(1)}, bf16[128,2048]{1,0:T(8,128)(2,1)S(1)}, u32[]{:S(2)}, u32[]{:S(2)}) collective-permute-start(bf16[128,2048]{1,0:T(8,128)(2,1)S(1)} %get-tuple-element.84), channel_id=1, source_target_pairs={{0,2},{1,3},{2,0},{3,1},{4,6},{5,7},{6,4},{7,5},{8,10},{9,11},{10,... | collective-permute-start | bytes 1572872 | tf_op jit(solution)/shard_map/ppermute | solution.py:118
  56.2 2.8 %far_hidden.1 = (bf16[2,256,384]{2,1,0:T(8,128)(2,1)S(1)}, bf16[2,256,768]{2,1,0:T(8,128)(2,1)S(1)}, f32[8,128]{1,0:T(8,128)}) custom-call(s32[5]{0:T(128)S(1)} %stack.28.refs_0_, bf16[128,2176]{1,0:T(8,128)(2,1)S(1)} %get-tuple-element.72.refs_1_, bf16[128,2176]{1,0:T(8,128)(2,1)S(1)} %collective-permute-done.9.refs_2_, ...), custom_call_target="tpu_custom_call" | custom-call | flops 4831838208 | tf_op jit(solution)/shard_map/far_hidden/pallas_call | solution.py:178
  60.4 1.5 %collective-permute-start.17 = (bf16[2,128,1152]{2,1,0:T(8,128)(2,1)S(1)}, bf16[2,128,1152]{2,1,0:T(8,128)(2,1)S(1)}, u32[]{:S(2)}, u32[]{:S(2)}) collective-permute-start(bf16[2,128,1152]{2,1,0:T(8,128)(2,1)S(1)} %get-tuple-element.92), channel_id=1, source_target_pairs={{0,8},{8,0},{16,24},{24,16},{1,9},{9,1},{17,25},{25,17},{2,10},{10... | collective-permute-start | bytes 1769480 | tf_op jit(solution)/shard_map/ppermute | solution.py:118
  63.4 1.7 %late_terms.3 = (bf16[2,128,1152]{2,1,0:T(8,128)(2,1)S(1)}, bf16[2,128,1152]{2,1,0:T(8,128)(2,1)S(1)}, bf16[2,128,1152]{2,1,0:T(8,128)(2,1)S(1)}, bf16[2,128,1152]{2,1,0:T(8,128)(2,1)S(1)}, f32[8,128]{1,0:T(8,128)S(1)}) custom-call(s32[5]{0:T(128)S(1)} %stack.28.refs_0_, bf16[128,2176]{1,0:T(8,128)(2,1)S(1)} %get-tuple-element.72.refs_1_, ...), custom_call_target="tpu_custom_call" | custom-call | flops 2415919104 | tf_op jit(solution)/shard_map/late_terms/pallas_call | solution.py:178
  65.2 2.5 %far_results.1 = (bf16[128,2048]{1,0:T(8,128)(2,1)S(1)}, bf16[128,2048]{1,0:T(8,128)(2,1)S(1)}, f32[8,128]{1,0:T(8,128)}) custom-call(s32[5]{0:T(128)S(1)} %stack.28.refs_0_, bf16[2,256,384]{2,1,0:T(8,128)(2,1)S(1)} %get-tuple-element.74.refs_4_.refs_1_, bf16[2,256,768]{2,1,0:T(8,128)(2,1)S(1)} %get-tuple-element.73.refs_3_.refs_2_, ...), custom_call_target="tpu_custom_call" | custom-call | flops 4831838208 | tf_op jit(solution)/shard_map/far_results/pallas_call | solution.py:178
  67.6 8.0 %collective-permute-done.17.refs_1_ = bf16[2,128,1152]{2,1,0:T(8,128)(2,1)S(1)} collective-permute-done((bf16[2,128,1152]{2,1,0:T(8,128)(2,1)S(1)}, bf16[2,128,1152]{2,1,0:T(8,128)(2,1)S(1)}, u32[]{:S(2)}, u32[]{:S(2)}) %collective-permute-start.17) | collective-permute-done | bytes 589856 | tf_op jit(solution)/shard_map/ppermute | solution.py:118
  81.8 2.5 %collective-permute-start.16 = (bf16[128,2048]{1,0:T(8,128)(2,1)S(1)}, bf16[128,2048]{1,0:T(8,128)(2,1)S(1)}, u32[]{:S(2)}, u32[]{:S(2)}) collective-permute-start(bf16[128,2048]{1,0:T(8,128)(2,1)S(1)} %get-tuple-element.89), channel_id=1, source_target_pairs={{0,6},{1,7},{2,4},{3,5},{4,2},{5,3},{6,0},{7,1},{8,14},{9,15},{10,... | collective-permute-start | bytes 1572872 | tf_op jit(solution)/shard_map/ppermute | solution.py:118
  84.4 3.6 %collective-permute-done.19.refs_1_ = bf16[128,1152]{1,0:T(8,128)(2,1)S(1)} collective-permute-done((bf16[128,1152]{1,0:T(8,128)(2,1)S(1)}, bf16[128,1152]{1,0:T(8,128)(2,1)S(1)}, u32[]{:S(2)}, u32[]{:S(2)}) %collective-permute-start.19) | collective-permute-done | bytes 294944 | tf_op jit(solution)/shard_map/ppermute | solution.py:118
  88.5 11.2 %collective-permute-done.20.refs_2_ = bf16[128,1152]{1,0:T(8,128)(2,1)S(1)} collective-permute-done((bf16[128,1152]{1,0:T(8,128)(2,1)S(1)}, bf16[128,1152]{1,0:T(8,128)(2,1)S(1)}, u32[]{:S(2)}, u32[]{:S(2)}) %collective-permute-start.20) | collective-permute-done | bytes 294944 | tf_op jit(solution)/shard_map/ppermute | solution.py:118
  100.8 1.9 %collective-permute-start.23 = (bf16[128,1152]{1,0:T(8,128)(2,1)S(1)}, bf16[128,1152]{1,0:T(8,128)(2,1)S(1)}, u32[]{:S(2)}, u32[]{:S(2)}) collective-permute-start(bf16[128,1152]{1,0:T(8,128)(2,1)S(1)} %get-tuple-element.104), channel_id=1, source_target_pairs={{0,4},{1,5},{2,6},{3,7},{4,0},{5,1},{6,2},{7,3},{8,12},{9,13},{10,... | collective-permute-start | bytes 884744 | tf_op jit(solution)/shard_map/ppermute | solution.py:118
  103.8 1.6 %pair_terms.2 = (bf16[128,1152]{1,0:T(8,128)(2,1)S(1)}, bf16[128,1152]{1,0:T(8,128)(2,1)S(1)}, f32[2,128,1152]{2,1,0:T(8,128)S(1)}, bf16[128,1024]{1,0:T(8,128)(...) custom-call(s32[5]{0:T(128)S(1)} %stack.28.refs_0_, bf16[2,128,1152]{2,1,0:T(8,128)(2,1)S(1)} %collective-permute-done.10.refs_1_, ...), custom_call_target="tpu_custom_call" | custom-call | tf_op jit(solution)/shard_map/pair_terms/pallas_call | solution.py:178
  106.5 21.0 %collective-permute-done.23.refs_5_ = bf16[128,1152]{1,0:T(8,128)(2,1)S(1)} collective-permute-done((bf16[128,1152]{1,0:T(8,128)(2,1)S(1)}, bf16[128,1152]{1,0:T(8,128)(2,1)S(1)}, u32[]{:S(2)}, u32[]{:S(2)}) %collective-permute-start.23) | collective-permute-done | bytes 294944 | tf_op jit(solution)/shard_map/ppermute | solution.py:118
  127.4 5.9 %collective-permute-done.24.refs_6_ = bf16[128,1152]{1,0:T(8,128)(2,1)S(1)} collective-permute-done((bf16[128,1152]{1,0:T(8,128)(2,1)S(1)}, bf16[128,1152]{1,0:T(8,128)(2,1)S(1)}, u32[]{:S(2)}, u32[]{:S(2)}) %collective-permute-start.24) | collective-permute-done | bytes 294944 | tf_op jit(solution)/shard_map/ppermute | solution.py:118
  133.4 2.2 %finish.1 = (f32[2,256,768]{2,1,0:T(8,128)}, f32[2,256,384]{2,1,0:T(8,128)}, f32[8,128]{1,0:T(8,128)}) custom-call(s32[5]{0:T(128)S(1)} %stack.28.refs_0_, f32[2,128,1152]{2,1,0:T(8,128)S(1)} %get-tuple-element.100.refs_1_, f32[2,128,1152]{2,1,0:T(8,128)S(1)} %get-tuple-element.101.refs_2_, bf16[128,1152]{1,0:T(8,128)(2,1)S(1)} %collective-permute-done.21.refs_3_, ...), custom_call_target="tpu_custom_call" | custom-call | tf_op jit(solution)/shard_map/finish/pallas_call | solution.py:178
  (62 shorter events, 24.8 us)
Async XLA Ops:
  3.2 9.1 %collective-permute-start.3 = (bf16[128,2176]{1,0:T(8,128)(2,1)}, bf16[128,2176]{1,0:T(8,128)(2,1)S(1)}, u32[]{:S(2)}, u32[]{:S(2)}) collective-permute-start(bf16[128,2176]{1,0:T(8,128)(2,1)} %get-tuple-element.57.refs_1_), channel_id=1, source_target_pairs={{0,1},{1,0},{2,3},{3,2},{4,5},{5,4},{6,7},{7,6},{8,9},{9,8},{10,11... | collective-permute-start | bytes 1671176 | tf_op jit(solution)/shard_map/ppermute | solution.py:118
  3.7 27.9 %collective-permute-start.4 = (bf16[128,2176]{1,0:T(8,128)(2,1)}, bf16[128,2176]{1,0:T(8,128)(2,1)S(1)}, u32[]{:S(2)}, u32[]{:S(2)}) collective-permute-start(bf16[128,2176]{1,0:T(8,128)(2,1)} %get-tuple-element.57.refs_1_), channel_id=1, source_target_pairs={{0,2},{1,3},{2,0},{3,1},{4,6},{5,7},{6,4},{7,5},{8,10},{9,11},{10,... | collective-permute-start | bytes 1671176 | tf_op jit(solution)/shard_map/ppermute | solution.py:118
  6.2 27.9 %collective-permute-start = (bf16[128,2176]{1,0:T(8,128)(2,1)}, bf16[128,2176]{1,0:T(8,128)(2,1)S(1)}, u32[]{:S(2)}, u32[]{:S(2)}) collective-permute-start(bf16[128,2176]{1,0:T(8,128)(2,1)} %get-tuple-element.57.refs_1_), channel_id=1, source_target_pairs={{0,4},{1,5},{2,6},{3,7},{4,0},{5,1},{6,2},{7,3},{8,12},{9,13},{10,... | collective-permute-start | bytes 1671176 | tf_op jit(solution)/shard_map/ppermute | solution.py:118
  31.5 4.7 %collective-permute-start.5 = (bf16[128,2176]{1,0:T(8,128)(2,1)S(1)}, bf16[128,2176]{1,0:T(8,128)(2,1)S(1)}, u32[]{:S(2)}, u32[]{:S(2)}) collective-permute-start(bf16[128,2176]{1,0:T(8,128)(2,1)S(1)} %hold.3.refs_1_.refs_3_), channel_id=1, source_target_pairs={{0,1},{1,0},{2,3},{3,2},{4,5},{5,4},{6,7},{7,6},{8,9},{9,8},{10,11... | collective-permute-start | bytes 1671176 | tf_op jit(solution)/shard_map/ppermute | solution.py:118
  34.1 6.7 %collective-permute-start.6 = (bf16[128,2176]{1,0:T(8,128)(2,1)S(1)}, bf16[128,2176]{1,0:T(8,128)(2,1)S(1)}, u32[]{:S(2)}, u32[]{:S(2)}) collective-permute-start(bf16[128,2176]{1,0:T(8,128)(2,1)S(1)} %collective-permute-done.refs_1_.refs_5_), channel_id=1, source_target_pairs={{0,1},{1,0},{2,3},{3,2},{4,5},{5,4},{6,7},{7,6},{8,9},{9,8},{10,11... | collective-permute-start | bytes 1671176 | tf_op jit(solution)/shard_map/ppermute | solution.py:118
  34.1 17.0 %collective-permute-start.1 = (bf16[128,2176]{1,0:T(8,128)(2,1)S(1)}, bf16[128,2176]{1,0:T(8,128)(2,1)S(1)}, u32[]{:S(2)}, u32[]{:S(2)}) collective-permute-start(bf16[128,2176]{1,0:T(8,128)(2,1)S(1)} %hold.2), channel_id=1, source_target_pairs={{2,4},{3,5},{4,2},{5,3},{10,12},{11,13},{12,10},{13,11},{18,20},{1... | collective-permute-start | bytes 1671176 | tf_op jit(solution)/shard_map/ppermute | solution.py:122
  34.8 16.9 %collective-permute-start.2 = (bf16[128,2176]{1,0:T(8,128)(2,1)S(1)}, bf16[128,2176]{1,0:T(8,128)(2,1)S(1)}, u32[]{:S(2)}, u32[]{:S(2)}) collective-permute-start(bf16[128,2176]{1,0:T(8,128)(2,1)S(1)} %collective-permute-done.refs_1_.refs_5_), channel_id=1, source_target_pairs={{2,0},{3,1},{4,6},{5,7},{10,8},{11,9},{12,14},{13,15},{18,16},{19,... | collective-permute-start | bytes 1671176 | tf_op jit(solution)/shard_map/ppermute | solution.py:122
  40.3 9.5 %collective-permute-start.7 = (bf16[128,2048]{1,0:T(8,128)(2,1)S(1)}, bf16[128,2048]{1,0:T(8,128)(2,1)S(1)}, u32[]{:S(2)}, u32[]{:S(2)}) collective-permute-start(bf16[128,2048]{1,0:T(8,128)(2,1)S(1)} %get-tuple-element.67), channel_id=1, source_target_pairs={{0,1},{1,0},{2,3},{3,2},{4,5},{5,4},{6,7},{7,6},{8,9},{9,8},{10,11... | collective-permute-start | bytes 1572872 | tf_op jit(solution)/shard_map/ppermute | solution.py:118
  44.8 5.6 %collective-permute-start.8 = (bf16[128,2048]{1,0:T(8,128)(2,1)S(1)}, bf16[128,2048]{1,0:T(8,128)(2,1)S(1)}, u32[]{:S(2)}, u32[]{:S(2)}) collective-permute-start(bf16[128,2048]{1,0:T(8,128)(2,1)S(1)} %get-tuple-element.70), channel_id=1, source_target_pairs={{0,1},{1,0},{2,3},{3,2},{4,5},{5,4},{6,7},{7,6},{8,9},{9,8},{10,11... | collective-permute-start | bytes 1572872 | tf_op jit(solution)/shard_map/ppermute | solution.py:118
  52.9 27.2 %collective-permute-start.13 = (bf16[128,2048]{1,0:T(8,128)(2,1)S(1)}, bf16[128,2048]{1,0:T(8,128)(2,1)S(1)}, u32[]{:S(2)}, u32[]{:S(2)}) collective-permute-start(bf16[128,2048]{1,0:T(8,128)(2,1)S(1)} %get-tuple-element.84), channel_id=1, source_target_pairs={{0,2},{1,3},{2,0},{3,1},{4,6},{5,7},{6,4},{7,5},{8,10},{9,11},{10,... | collective-permute-start | bytes 1572872 | tf_op jit(solution)/shard_map/ppermute | solution.py:118
  55.2 26.0 %collective-permute-start.14 = (bf16[128,2048]{1,0:T(8,128)(2,1)S(1)}, bf16[128,2048]{1,0:T(8,128)(2,1)S(1)}, u32[]{:S(2)}, u32[]{:S(2)}) collective-permute-start(bf16[128,2048]{1,0:T(8,128)(2,1)S(1)} %get-tuple-element.85), channel_id=1, source_target_pairs={{0,4},{1,5},{2,6},{3,7},{4,0},{5,1},{6,2},{7,3},{8,12},{9,13},{10,... | collective-permute-start | bytes 1572872 | tf_op jit(solution)/shard_map/ppermute | solution.py:118
  60.4 15.3 %collective-permute-start.17 = (bf16[2,128,1152]{2,1,0:T(8,128)(2,1)S(1)}, bf16[2,128,1152]{2,1,0:T(8,128)(2,1)S(1)}, u32[]{:S(2)}, u32[]{:S(2)}) collective-permute-start(bf16[2,128,1152]{2,1,0:T(8,128)(2,1)S(1)} %get-tuple-element.92), channel_id=1, source_target_pairs={{0,8},{8,0},{16,24},{24,16},{1,9},{9,1},{17,25},{25,17},{2,10},{10... | collective-permute-start | bytes 1769480 | tf_op jit(solution)/shard_map/ppermute | solution.py:118
  61.9 15.0 %collective-permute-start.18 = (bf16[2,128,1152]{2,1,0:T(8,128)(2,1)S(1)}, bf16[2,128,1152]{2,1,0:T(8,128)(2,1)S(1)}, u32[]{:S(2)}, u32[]{:S(2)}) collective-permute-start(bf16[2,128,1152]{2,1,0:T(8,128)(2,1)S(1)} %get-tuple-element.93), channel_id=1, source_target_pairs={{0,16},{8,24},{16,0},{24,8},{1,17},{9,25},{17,1},{25,9},{2,18},{10... | collective-permute-start | bytes 1769480 | tf_op jit(solution)/shard_map/ppermute | solution.py:118
  67.6 13.5 %collective-permute-start.15 = (bf16[128,2048]{1,0:T(8,128)(2,1)S(1)}, bf16[128,2048]{1,0:T(8,128)(2,1)S(1)}, u32[]{:S(2)}, u32[]{:S(2)}) collective-permute-start(bf16[128,2048]{1,0:T(8,128)(2,1)S(1)} %get-tuple-element.88), channel_id=1, source_target_pairs={{0,1},{1,0},{2,3},{3,2},{4,5},{5,4},{6,7},{7,6},{8,9},{9,8},{10,11... | collective-permute-start | bytes 1572872 | tf_op jit(solution)/shard_map/ppermute | solution.py:118
  78.0 9.9 %collective-permute-start.19 = (bf16[128,1152]{1,0:T(8,128)(2,1)S(1)}, bf16[128,1152]{1,0:T(8,128)(2,1)S(1)}, u32[]{:S(2)}, u32[]{:S(2)}) collective-permute-start(bf16[128,1152]{1,0:T(8,128)(2,1)S(1)} %get-tuple-element.96), channel_id=1, source_target_pairs={{0,16},{8,24},{16,0},{24,8},{1,17},{9,25},{17,1},{25,9},{2,18},{10... | collective-permute-start | bytes 884744 | tf_op jit(solution)/shard_map/ppermute | solution.py:118
  79.6 24.2 %collective-permute-start.10 = (bf16[2,128,1152]{2,1,0:T(8,128)(2,1)S(1)}, bf16[2,128,1152]{2,1,0:T(8,128)(2,1)S(1)}, u32[]{:S(2)}, u32[]{:S(2)}) collective-permute-start(bf16[2,128,1152]{2,1,0:T(8,128)(2,1)S(1)} %get-tuple-element.78), channel_id=1, source_target_pairs={{0,8},{8,0},{16,24},{24,16},{1,9},{9,1},{17,25},{25,17},{2,10},{10... | collective-permute-start | bytes 1769480 | tf_op jit(solution)/shard_map/ppermute | solution.py:118
  80.1 23.7 %collective-permute-start.11 = (bf16[2,128,1152]{2,1,0:T(8,128)(2,1)S(1)}, bf16[2,128,1152]{2,1,0:T(8,128)(2,1)S(1)}, u32[]{:S(2)}, u32[]{:S(2)}) collective-permute-start(bf16[2,128,1152]{2,1,0:T(8,128)(2,1)S(1)} %get-tuple-element.79), channel_id=1, source_target_pairs={{0,16},{8,24},{16,0},{24,8},{1,17},{9,25},{17,1},{25,9},{2,18},{10... | collective-permute-start | bytes 1769480 | tf_op jit(solution)/shard_map/ppermute | solution.py:118
  81.2 21.6 %collective-permute-start.12 = (bf16[128,2048]{1,0:T(8,128)(2,1)S(1)}, bf16[128,2048]{1,0:T(8,128)(2,1)S(1)}, u32[]{:S(2)}, u32[]{:S(2)}) collective-permute-start(bf16[128,2048]{1,0:T(8,128)(2,1)S(1)} %get-tuple-element.83), channel_id=1, source_target_pairs={{0,1},{1,0},{2,3},{3,2},{4,5},{5,4},{6,7},{7,6},{8,9},{9,8},{10,11... | collective-permute-start | bytes 1572872 | tf_op jit(solution)/shard_map/ppermute | solution.py:118
  81.8 21.9 %collective-permute-start.16 = (bf16[128,2048]{1,0:T(8,128)(2,1)S(1)}, bf16[128,2048]{1,0:T(8,128)(2,1)S(1)}, u32[]{:S(2)}, u32[]{:S(2)}) collective-permute-start(bf16[128,2048]{1,0:T(8,128)(2,1)S(1)} %get-tuple-element.89), channel_id=1, source_target_pairs={{0,6},{1,7},{2,4},{3,5},{4,2},{5,3},{6,0},{7,1},{8,14},{9,15},{10,... | collective-permute-start | bytes 1572872 | tf_op jit(solution)/shard_map/ppermute | solution.py:118
  88.0 11.7 %collective-permute-start.20 = (bf16[128,1152]{1,0:T(8,128)(2,1)S(1)}, bf16[128,1152]{1,0:T(8,128)(2,1)S(1)}, u32[]{:S(2)}, u32[]{:S(2)}) collective-permute-start(bf16[128,1152]{1,0:T(8,128)(2,1)S(1)} %get-tuple-element.97), channel_id=1, source_target_pairs={{0,8},{8,0},{16,24},{24,16},{1,9},{9,1},{17,25},{25,17},{2,10},{10... | collective-permute-start | bytes 884744 | tf_op jit(solution)/shard_map/ppermute | solution.py:118
  100.8 26.6 %collective-permute-start.23 = (bf16[128,1152]{1,0:T(8,128)(2,1)S(1)}, bf16[128,1152]{1,0:T(8,128)(2,1)S(1)}, u32[]{:S(2)}, u32[]{:S(2)}) collective-permute-start(bf16[128,1152]{1,0:T(8,128)(2,1)S(1)} %get-tuple-element.104), channel_id=1, source_target_pairs={{0,4},{1,5},{2,6},{3,7},{4,0},{5,1},{6,2},{7,3},{8,12},{9,13},{10,... | collective-permute-start | bytes 884744 | tf_op jit(solution)/shard_map/ppermute | solution.py:118
  102.7 30.6 %collective-permute-start.24 = (bf16[128,1152]{1,0:T(8,128)(2,1)S(1)}, bf16[128,1152]{1,0:T(8,128)(2,1)S(1)}, u32[]{:S(2)}, u32[]{:S(2)}) collective-permute-start(bf16[128,1152]{1,0:T(8,128)(2,1)S(1)} %get-tuple-element.105), channel_id=1, source_target_pairs={{0,4},{1,5},{2,6},{3,7},{4,0},{5,1},{6,2},{7,3},{8,12},{9,13},{10,... | collective-permute-start | bytes 884744 | tf_op jit(solution)/shard_map/ppermute | solution.py:118
  105.4 28.0 %collective-permute-start.21 = (bf16[128,1152]{1,0:T(8,128)(2,1)S(1)}, bf16[128,1152]{1,0:T(8,128)(2,1)S(1)}, u32[]{:S(2)}, u32[]{:S(2)}) collective-permute-start(bf16[128,1152]{1,0:T(8,128)(2,1)S(1)} %get-tuple-element.102), channel_id=1, source_target_pairs={{0,16},{8,24},{16,0},{24,8},{1,17},{9,25},{17,1},{25,9},{2,18},{10... | collective-permute-start | bytes 884744 | tf_op jit(solution)/shard_map/ppermute | solution.py:118
  105.9 27.5 %collective-permute-start.22 = (bf16[128,1152]{1,0:T(8,128)(2,1)S(1)}, bf16[128,1152]{1,0:T(8,128)(2,1)S(1)}, u32[]{:S(2)}, u32[]{:S(2)}) collective-permute-start(bf16[128,1152]{1,0:T(8,128)(2,1)S(1)} %get-tuple-element.103), channel_id=1, source_target_pairs={{0,8},{8,0},{16,24},{24,16},{1,9},{9,1},{17,25},{25,17},{2,10},{10... | collective-permute-start | bytes 884744 | tf_op jit(solution)/shard_map/ppermute | solution.py:118
  (7 other events, 65.2 us)

commit v4 on v3

--- a/solution.py
+++ b/solution.py
@@ -294,38 +294,45 @@
     refs[-1][...] = jnp.where(at[4] == 1, middle[...], ends[...])
 
 
-def line_kernel(at, kept, other, *outs):
-    out = outs[-1]
-    out[...] = (kept[...].astype(jnp.float32) + other[...].astype(jnp.float32)).astype(out.dtype)
+def line_kernel(at, kept, other, *refs, passed, cuts):
+    value = kept[...].astype(jnp.float32) + other[...].astype(jnp.float32)
+    for ref in refs[:passed]:
+        value = value + jnp.where(at[4] == 1, ref[...].astype(jnp.float32), 0.0)
+    for i, out in enumerate(refs[-cuts:]):
+        out[...] = value[:, i * out.shape[1] : (i + 1) * out.shape[1]].astype(out.dtype)
 
 
 def pair_kernel(at, got_a, got_b, keep_a, keep_b, *refs):
     f32 = jnp.float32
-    more, results = refs[: (len(refs) - 3) * 5 // 7], refs[-2:]
-    end_a, end_b, own = refs[len(more) : len(more) + 3]
+    count = 6 if len(refs) > 6 else 0
+    more, results = refs[:count], refs[-2:]
+    end_a, end_b, own = refs[count : count + 3] if count else refs[-3:]
     for half, (got, keep, out) in enumerate(((got_a, keep_a, end_a), (got_b, keep_b, end_b))):
         out[...] = (keep[1].astype(f32) + got[1].astype(f32)).astype(out.dtype)
         own[half] = keep[0].astype(f32) + got[0].astype(f32)
     if more:
-        value = sum(ref[...].astype(f32) for ref in more).astype(results[0].dtype)
-        for i, ref in enumerate(results):
-            ref[...] = value[:, i * ref.shape[1] : (i + 1) * ref.shape[1]]
-
-
-def lead_kernel(at, end_a, end_b, own, done, sent_a, sent_b, first):
-    del done
-    for half, (end, sent) in enumerate(((end_a, sent_a), (end_b, sent_b))):
+        own_sum, other_sum, one, two = [ref[...].astype(f32) for ref in more[:4]]
+        value = own_sum + other_sum + one + jnp.where(at[4] == 1, 0.0, two)
+        for i, (ref, three) in enumerate(zip(results, more[4:])):
+            term = value[:, i * ref.shape[1] : (i + 1) * ref.shape[1]]
+            ref[...] = (term + three[...].astype(f32)).astype(ref.dtype)
+
+
+def lead_kernel(at, end_a, end_b, own, *refs):
+    sent, first = refs[-2:]
+    rows = own.shape[1]
+    for half, end in enumerate((end_a, end_b)):
         value = own[half] + end[...].astype(jnp.float32)
         first[half] = value
-        sent[...] = value.astype(sent.dtype)
-
-
-def finish_kernel(at, first, second, end_a, end_b, traded_a, traded_b, gu_ref, dn_ref):
+        sent[half * rows : (half + 1) * rows] = value.astype(sent.dtype)
+
+
+def finish_kernel(at, first, second, end_a, end_b, traded, gu_ref, dn_ref):
     columns = gu_ref.shape[2]
     rows = end_a.shape[0]
-    for half, (end, traded) in enumerate(((end_a, traded_a), (end_b, traded_b))):
+    for half, end in enumerate((end_a, end_b)):
         here = slice(half * rows, (half + 1) * rows)
-        lead = jnp.where(at[3] == 1, traded[...].astype(jnp.float32), first[half])
+        lead = jnp.where(at[3] == 1, traded[here].astype(jnp.float32), first[half])
         for slot, value in ((at[1], lead), (1 - at[1], second[half] + end[...].astype(jnp.float32))):
             gu_ref[slot, here, :] = value[:, :columns]
             dn_ref[slot, here, :] = value[:, columns:]
@@ -386,10 +393,13 @@
     )
     other = [swap_with(block, "expert", 1) for block in sent]
 
-    def line(k, *earlier):
-        operands = (kept[k], other[k], *earlier)
-        going, done = call(line_kernel, "line_terms", at, operands, outer_outs[:1], 0)
-        return swap_with(going, "expert", 2 * k), done
+    def line(k, *passed, cuts=1):
+        kernel = functools.partial(line_kernel, passed=len(passed), cuts=cuts)
+        outs = [((count_tokens, 2 * width // cuts), bf16)] * cuts
+        *going, done = call(kernel, "line_terms", at, (kept[k], other[k], *passed), outs, 0)
+        if k == 2:
+            return send(going[0], [(1, 3), (2, 0), (0, 1), (3, 2)]), done
+        return *(swap_with(piece, "expert", 2 * k) for piece in going), done
 
     (got_one, mark_one), (got_two, mark_two) = line(1), line(2)
 
@@ -402,9 +412,9 @@
         kernel = functools.partial(late_kernel, pieces=2, order=i)
         return call(kernel, "late_terms", at, (*far, p, h, sums[i], *earlier), part, 6 * flops)
 
-    def halves(send_a, send_b, keep_a, keep_b, more):
+    def halves(send_a, send_b, keep_a, keep_b, more, *earlier):
         got_a, got_b = swap_with(send_a, "dp", 1), swap_with(send_b, "dp", 2)
-        operands = (got_a, got_b, keep_a, keep_b, *more)
+        operands = (got_a, got_b, keep_a, keep_b, *earlier, *more)
         outs = [one_block, one_block, both] + [((count_tokens, width), bf16)] * (2 if more else 0)
         end_a, end_b, own, *results, _ = call(pair_kernel, "pair_terms", at, operands, outs, 0)
         return swap_with(end_a, "dp", 2), swap_with(end_b, "dp", 1), own, results
@@ -414,19 +424,18 @@
     k, s, _ = call(outer_kernel, "far_results", at, (h, p, *weights, done), outer_outs, 12 * flops)
     kept.append(k)
     other.append(swap_with(s, "expert", 1))
-    got_three, done = line(3, got_one, got_two)
-    end_a, end_b, own, _ = halves(*first, [])
-    *leading, head, _ = call(
-        lead_kernel, "lead_terms", at, (end_a, end_b, own, done), [one_block, one_block, both], 0
-    )
-    traded = [swap_with(half, "expert", n_expert // 2) for half in leading]
-    more = [kept[0], other[0], got_one, got_two, got_three]
+    three_mixed, three_grad, done = line(3, got_two, cuts=2)
+    end_a, end_b, own, _ = halves(*first, [], done)
+    outs = [((2 * rows, columns), bf16), both]
+    leading, head, _ = call(lead_kernel, "lead_terms", at, (end_a, end_b, own, three_mixed, three_grad, got_one), outs, 0)
+    traded = swap_with(leading, "expert", n_expert // 2)
+    more = [kept[0], other[0], got_one, got_two, three_mixed, three_grad]
     end_a, end_b, tail, (mixed, grad_tokens) = halves(*second, more)
     grad_gu, grad_dn, _ = call(
         finish_kernel,
         "finish",
         at,
-        (head, tail, end_a, end_b, *traded),
+        (head, tail, end_a, end_b, traded),
         [((2, 2 * rows, 2 * units), f32), ((2, 2 * rows, units), f32)],
         0,
     )

time: 136 us -> 132 us (0.971)
  waiting for transfers between devices: 66 us -> 58.9 us
  starting transfers between devices: 24.3 us -> 28 us
    ppermute x23 -> x22, waiting for transfers between devices: 65.4 us -> 58 us  [swap_with(): lax.ppermute(block, axis, [(i, i ^ mask) for i in range(lax.axis_size(axi...]
    ppermute x2 -> x3, starting transfers between devices: 2.16 us -> 4.46 us  [send(): lax.ppermute(block, 'expert', [(2 * a + c, 2 * b + c) for a, b in pairs f...]
    ppermute x23 -> x22, starting transfers between devices: 22.1 us -> 23.6 us  [swap_with(): lax.ppermute(block, axis, [(i, i ^ mask) for i in range(lax.axis_size(axi...]
  transfers between devices with their start and end apart: 25 -> 25, of which waited for: 10 -> 11; matrix products, arithmetic and copies ran while one was open for 2% -> 2% of each run, Pallas kernels for 23% -> 23%
where the time goes in v4:
time: 132 us
  waiting for transfers between devices  58.9 us (45%)
  Pallas kernels  36.6 us (28%)
  starting transfers between devices  28 us (21%)
  local copies, waits for them, and re-layouts  5.1 us (4%)
  between operations  2.06 us (2%)
  other arithmetic  1.48 us (1%)
    ppermute x22, waiting for transfers between devices, swap_with(): lax.ppermute(block, axis, [(i, i ^ mask) for i in range(lax.axis_size(axi...  58 us
    pallas_call x16, Pallas kernels, call(): pl.pallas_call(functools.partial(marked, kernel, 1 + len(operands) + len(...  34 us
    ppermute x22, starting transfers between devices, swap_with(): lax.ppermute(block, axis, [(i, i ^ mask) for i in range(lax.axis_size(axi...  23.6 us
    ppermute x3, starting transfers between devices, send(): lax.ppermute(block, 'expert', [(2 * a + c, 2 * b + c) for a, b in pairs f...  4.46 us
    unnamed x12, local copies, waits for them, and re-layouts  4.42 us
  transfers between devices with their start and end apart: 25, of which 11 were waited for; matrix products, arithmetic and copies ran while one was open for 2% of the time, Pallas kernels for 23%

profile of v4, /device:TPU:0, one launch (start us, length us, event | category | flops | bytes accessed | tf_op | source)
XLA Modules:
  0.0 132.1 jit_solution(15673752950581305680)
XLA Ops:
  0.6 2.6 %message.1 = (bf16[128,2176]{1,0:T(8,128)(2,1)}, bf16[128,2176]{1,0:T(8,128)(2,1)}) custom-call(bf16[128,1024]{1,0:T(8,128)(2,1)} %tokens_ref.1, bf16[128,1024]{1,0:T(8,128)(2,1)} %cotangent_ref.1, s32[8,128]{1,0:T(8,128)} %bitcast.6, f32[8,128]{1,0:T(8,128)} %bitcast.7), custom_call_target="tpu_custom_call" | custom-call | bytes 1048576 | tf_op jit(solution)/shard_map/message/pallas_call | solution.py:155
  3.7 2.6 %collective-permute-start.4 = (bf16[128,2176]{1,0:T(8,128)(2,1)}, bf16[128,2176]{1,0:T(8,128)(2,1)S(1)}, u32[]{:S(2)}, u32[]{:S(2)}) collective-permute-start(bf16[128,2176]{1,0:T(8,128)(2,1)} %get-tuple-element.57.refs_1_), channel_id=1, source_target_pairs={{0,2},{1,3},{2,0},{3,1},{4,6},{5,7},{6,4},{7,5},{8,10},{9,11},{10,... | collective-permute-start | bytes 1671176 | tf_op jit(solution)/shard_map/ppermute | solution.py:118
  6.2 2.6 %collective-permute-start = (bf16[128,2176]{1,0:T(8,128)(2,1)}, bf16[128,2176]{1,0:T(8,128)(2,1)S(1)}, u32[]{:S(2)}, u32[]{:S(2)}) collective-permute-start(bf16[128,2176]{1,0:T(8,128)(2,1)} %get-tuple-element.57.refs_1_), channel_id=1, source_target_pairs={{0,4},{1,5},{2,6},{3,7},{4,0},{5,1},{6,2},{7,3},{8,12},{9,13},{10,... | collective-permute-start | bytes 1671176 | tf_op jit(solution)/shard_map/ppermute | solution.py:118
  12.3 1.9 %copy-done.1 = bf16[2,1024,768]{2,1,0:T(8,128)(2,1)S(1)} copy-done((bf16[2,1024,768]{2,1,0:T(8,128)(2,1)S(1)}, bf16[2,1024,768]{2,1,0:T(8,128)(2,1)}, u32[]{:S(2)}) %copy-start.1) | copy-done | bytes 3145752
  16.7 3.6 %near_block.3 = (bf16[2,256,384]{2,1,0:T(8,128)(2,1)S(1)}, bf16[2,256,768]{2,1,0:T(8,128)(2,1)S(1)}, bf16[128,2048]{1,0:T(8,128)(2,1)S(1)}, bf16[128,2048]{1,0:T(8,128)(2,1)S(1)}, f32[8,128]{1,0:T(8,128)S(1)}) custom-call(s32[5]{0:T(128)S(1)} %stack.28.refs_0_, bf16[128,2176]{1,0:T(8,128)(2,1)S(1)} %copy-done.5, ...), custom_call_target="tpu_custom_call" | custom-call | flops 4831838208 | tf_op jit(solution)/shard_map/near_block/pallas_call | solution.py:178
  20.3 11.3 %collective-permute-done.4.refs_0_ = bf16[128,2176]{1,0:T(8,128)(2,1)S(1)} collective-permute-done((bf16[128,2176]{1,0:T(8,128)(2,1)}, bf16[128,2176]{1,0:T(8,128)(2,1)S(1)}, u32[]{:S(2)}, u32[]{:S(2)}) %collective-permute-start.4) | collective-permute-done | bytes 557088 | tf_op jit(solution)/shard_map/ppermute | solution.py:118
  31.5 2.6 %collective-permute-done.refs_1_.refs_5_ = bf16[128,2176]{1,0:T(8,128)(2,1)S(1)} collective-permute-done((bf16[128,2176]{1,0:T(8,128)(2,1)}, bf16[128,2176]{1,0:T(8,128)(2,1)S(1)}, u32[]{:S(2)}, u32[]{:S(2)}) %collective-permute-start) | collective-permute-done | bytes 557088 | tf_op jit(solution)/shard_map/ppermute | solution.py:118
  36.3 4.0 %near_block.4 = (bf16[2,256,384]{2,1,0:T(8,128)(2,1)S(1)}, bf16[2,256,768]{2,1,0:T(8,128)(2,1)S(1)}, bf16[128,2048]{1,0:T(8,128)(2,1)S(1)}, bf16[128,2048]{1,0:T(8,128)(2,1)S(1)}, f32[8,128]{1,0:T(8,128)}) custom-call(s32[5]{0:T(128)S(1)} %stack.28.refs_0_, bf16[128,2176]{1,0:T(8,128)(2,1)S(1)} %hold.3.refs_1_.refs_3_, ...), custom_call_target="tpu_custom_call" | custom-call | flops 4831838208 | tf_op jit(solution)/shard_map/near_block/pallas_call | solution.py:178
  40.8 4.0 %near_block.5 = (bf16[2,256,384]{2,1,0:T(8,128)(2,1)S(1)}, bf16[2,256,768]{2,1,0:T(8,128)(2,1)S(1)}, bf16[128,2048]{1,0:T(8,128)(2,1)S(1)}, bf16[128,2048]{1,0:T(8,128)(2,1)S(1)}, f32[8,128]{1,0:T(8,128)}) custom-call(s32[5]{0:T(128)S(1)} %stack.28.refs_0_, bf16[128,2176]{1,0:T(8,128)(2,1)S(1)} %collective-permute-done.refs_1_.refs_5_, ...), custom_call_target="tpu_custom_call" | custom-call | flops 6039797760 | tf_op jit(solution)/shard_map/near_block/pallas_call | solution.py:178
  44.8 4.9 %early_terms.1 = (f32[4,256,1152]{2,1,0:T(8,128)S(1)}, f32[4,256,1152]{2,1,0:T(8,128)S(1)}, f32[8,128]{1,0:T(8,128)S(1)}) custom-call(s32[5]{0:T(128)S(1)} %stack.28.refs_0_, bf16[128,2176]{1,0:T(8,128)(2,1)S(1)} %copy-done.5, bf16[128,2176]{1,0:T(8,128)(2,1)S(1)} %collective-permute-done.3.refs_2_, bf16[128,2176]{1,0:T(8,128)(2,1)S(1)} %hold.3.refs_1_.refs_3_, ...), custom_call_target="tpu_custom_call" | custom-call | flops 10871635968 | tf_op jit(solution)/shard_map/early_terms/pallas_call | solution.py:178
  52.9 2.3 %collective-permute-start.14 = (bf16[128,2048]{1,0:T(8,128)(2,1)S(1)}, bf16[128,2048]{1,0:T(8,128)(2,1)S(1)}, u32[]{:S(2)}, u32[]{:S(2)}) collective-permute-start(bf16[128,2048]{1,0:T(8,128)(2,1)S(1)} %get-tuple-element.85), channel_id=1, source_target_pairs={{2,6},{3,7},{4,0},{5,1},{0,2},{1,3},{6,4},{7,5},{10,14},{11,15},{1... | collective-permute-start | bytes 1572872 | tf_op jit(solution)/shard_map/ppermute | solution.py:122
  55.2 2.8 %far_hidden.1 = (bf16[2,256,384]{2,1,0:T(8,128)(2,1)S(1)}, bf16[2,256,768]{2,1,0:T(8,128)(2,1)S(1)}, f32[8,128]{1,0:T(8,128)}) custom-call(s32[5]{0:T(128)S(1)} %stack.28.refs_0_, bf16[128,2176]{1,0:T(8,128)(2,1)S(1)} %get-tuple-element.72.refs_1_, bf16[128,2176]{1,0:T(8,128)(2,1)S(1)} %collective-permute-done.9.refs_2_, ...), custom_call_target="tpu_custom_call" | custom-call | flops 4831838208 | tf_op jit(solution)/shard_map/far_hidden/pallas_call | solution.py:178
  60.8 2.5 %far_results.1 = (bf16[128,2048]{1,0:T(8,128)(2,1)S(1)}, bf16[128,2048]{1,0:T(8,128)(2,1)S(1)}, f32[8,128]{1,0:T(8,128)}) custom-call(s32[5]{0:T(128)S(1)} %stack.28.refs_0_, bf16[2,256,384]{2,1,0:T(8,128)(2,1)S(1)} %get-tuple-element.74.refs_4_.refs_1_, bf16[2,256,768]{2,1,0:T(8,128)(2,1)S(1)} %get-tuple-element.73.refs_3_.refs_2_, ...), custom_call_target="tpu_custom_call" | custom-call | flops 4831838208 | tf_op jit(solution)/shard_map/far_results/pallas_call | solution.py:178
  66.3 1.9 %collective-permute-start.13 = (bf16[128,2048]{1,0:T(8,128)(2,1)S(1)}, bf16[128,2048]{1,0:T(8,128)(2,1)S(1)}, u32[]{:S(2)}, u32[]{:S(2)}) collective-permute-start(bf16[128,2048]{1,0:T(8,128)(2,1)S(1)} %get-tuple-element.84), channel_id=1, source_target_pairs={{0,2},{1,3},{2,0},{3,1},{4,6},{5,7},{6,4},{7,5},{8,10},{9,11},{10,... | collective-permute-start | bytes 1572872 | tf_op jit(solution)/shard_map/ppermute | solution.py:118
  69.3 2.3 %collective-permute-start.16 = (bf16[128,1024]{1,0:T(8,128)(2,1)S(1)}, bf16[128,1024]{1,0:T(8,128)(2,1)S(1)}, u32[]{:S(2)}, u32[]{:S(2)}) collective-permute-start(bf16[128,1024]{1,0:T(8,128)(2,1)S(1)} %get-tuple-element.89), channel_id=1, source_target_pairs={{0,6},{1,7},{2,4},{3,5},{4,2},{5,3},{6,0},{7,1},{8,14},{9,15},{10,... | collective-permute-start | bytes 786440 | tf_op jit(solution)/shard_map/ppermute | solution.py:118
  73.2 5.9 %collective-permute-done.18.refs_1_ = bf16[2,128,1152]{2,1,0:T(8,128)(2,1)S(1)} collective-permute-done((bf16[2,128,1152]{2,1,0:T(8,128)(2,1)S(1)}, bf16[2,128,1152]{2,1,0:T(8,128)(2,1)S(1)}, u32[]{:S(2)}, u32[]{:S(2)}) %collective-permute-start.18) | collective-permute-done | bytes 589856 | tf_op jit(solution)/shard_map/ppermute | solution.py:118
  83.7 5.5 %collective-permute-done.16.refs_9_.refs_4_ = bf16[128,1024]{1,0:T(8,128)(2,1)S(1)} collective-permute-done((bf16[128,1024]{1,0:T(8,128)(2,1)S(1)}, bf16[128,1024]{1,0:T(8,128)(2,1)S(1)}, u32[]{:S(2)}, u32[]{:S(2)}) %collective-permute-start.16) | collective-permute-done | bytes 262176 | tf_op jit(solution)/shard_map/ppermute | solution.py:118
  89.8 3.8 %collective-permute-done.17.refs_10_.refs_5_ = bf16[128,1024]{1,0:T(8,128)(2,1)S(1)} collective-permute-done((bf16[128,1024]{1,0:T(8,128)(2,1)S(1)}, bf16[128,1024]{1,0:T(8,128)(2,1)S(1)}, u32[]{:S(2)}, u32[]{:S(2)}) %collective-permute-start.17) | collective-permute-done | bytes 262176 | tf_op jit(solution)/shard_map/ppermute | solution.py:118
  93.6 7.9 %collective-permute-done.20.refs_1_ = bf16[128,1152]{1,0:T(8,128)(2,1)S(1)} collective-permute-done((bf16[128,1152]{1,0:T(8,128)(2,1)S(1)}, bf16[128,1152]{1,0:T(8,128)(2,1)S(1)}, u32[]{:S(2)}, u32[]{:S(2)}) %collective-permute-start.20) | collective-permute-done | bytes 294944 | tf_op jit(solution)/shard_map/ppermute | solution.py:118
  102.7 2.5 %collective-permute-start.24 = (bf16[256,1152]{1,0:T(8,128)(2,1)S(1)}, bf16[256,1152]{1,0:T(8,128)(2,1)S(1)}, u32[]{:S(2)}, u32[]{:S(2)}) collective-permute-start(bf16[256,1152]{1,0:T(8,128)(2,1)S(1)} %get-tuple-element.105), channel_id=1, source_target_pairs={{0,4},{1,5},{2,6},{3,7},{4,0},{5,1},{6,2},{7,3},{8,12},{9,13},{10,... | collective-permute-start | bytes 1769480 | tf_op jit(solution)/shard_map/ppermute | solution.py:118
  105.2 1.7 %pair_terms.2 = (bf16[128,1152]{1,0:T(8,128)(2,1)S(1)}, bf16[128,1152]{1,0:T(8,128)(2,1)S(1)}, f32[2,128,1152]{2,1,0:T(8,128)S(1)}, bf16[128,1024]{1,0:T(8,128)(...) custom-call(s32[5]{0:T(128)S(1)} %stack.28.refs_0_, bf16[2,128,1152]{2,1,0:T(8,128)(2,1)S(1)} %collective-permute-done.10.refs_1_, ...), custom_call_target="tpu_custom_call" | custom-call | tf_op jit(solution)/shard_map/pair_terms/pallas_call | solution.py:178
  108.9 4.8 %collective-permute-done.22.refs_3_ = bf16[128,1152]{1,0:T(8,128)(2,1)S(1)} collective-permute-done((bf16[128,1152]{1,0:T(8,128)(2,1)S(1)}, bf16[128,1152]{1,0:T(8,128)(2,1)S(1)}, u32[]{:S(2)}, u32[]{:S(2)}) %collective-permute-start.22) | collective-permute-done | bytes 294944 | tf_op jit(solution)/shard_map/ppermute | solution.py:118
  115.1 14.8 %collective-permute-done.24.refs_5_ = bf16[256,1152]{1,0:T(8,128)(2,1)S(1)} collective-permute-done((bf16[256,1152]{1,0:T(8,128)(2,1)S(1)}, bf16[256,1152]{1,0:T(8,128)(2,1)S(1)}, u32[]{:S(2)}, u32[]{:S(2)}) %collective-permute-start.24) | collective-permute-done | bytes 589856 | tf_op jit(solution)/shard_map/ppermute | solution.py:118
  130.0 2.2 %finish.1 = (f32[2,256,768]{2,1,0:T(8,128)}, f32[2,256,384]{2,1,0:T(8,128)}, f32[8,128]{1,0:T(8,128)}) custom-call(s32[5]{0:T(128)S(1)} %stack.28.refs_0_, f32[2,128,1152]{2,1,0:T(8,128)S(1)} %get-tuple-element.101.refs_1_, f32[2,128,1152]{2,1,0:T(8,128)S(1)} %get-tuple-element.102.refs_2_, bf16[128,1152]{1,0:T(8,128)(2,1)S(1)} %collective-permute-done.22.refs_3_, ...), custom_call_target="tpu_custom_call" | custom-call | tf_op jit(solution)/shard_map/finish/pallas_call | solution.py:178
  (62 shorter events, 29.2 us)
Async XLA Ops:
  3.2 9.1 %collective-permute-start.3 = (bf16[128,2176]{1,0:T(8,128)(2,1)}, bf16[128,2176]{1,0:T(8,128)(2,1)S(1)}, u32[]{:S(2)}, u32[]{:S(2)}) collective-permute-start(bf16[128,2176]{1,0:T(8,128)(2,1)} %get-tuple-element.57.refs_1_), channel_id=1, source_target_pairs={{0,1},{1,0},{2,3},{3,2},{4,5},{5,4},{6,7},{7,6},{8,9},{9,8},{10,11... | collective-permute-start | bytes 1671176 | tf_op jit(solution)/shard_map/ppermute | solution.py:118
  3.7 27.9 %collective-permute-start.4 = (bf16[128,2176]{1,0:T(8,128)(2,1)}, bf16[128,2176]{1,0:T(8,128)(2,1)S(1)}, u32[]{:S(2)}, u32[]{:S(2)}) collective-permute-start(bf16[128,2176]{1,0:T(8,128)(2,1)} %get-tuple-element.57.refs_1_), channel_id=1, source_target_pairs={{0,2},{1,3},{2,0},{3,1},{4,6},{5,7},{6,4},{7,5},{8,10},{9,11},{10,... | collective-permute-start | bytes 1671176 | tf_op jit(solution)/shard_map/ppermute | solution.py:118
  6.2 27.9 %collective-permute-start = (bf16[128,2176]{1,0:T(8,128)(2,1)}, bf16[128,2176]{1,0:T(8,128)(2,1)S(1)}, u32[]{:S(2)}, u32[]{:S(2)}) collective-permute-start(bf16[128,2176]{1,0:T(8,128)(2,1)} %get-tuple-element.57.refs_1_), channel_id=1, source_target_pairs={{0,4},{1,5},{2,6},{3,7},{4,0},{5,1},{6,2},{7,3},{8,12},{9,13},{10,... | collective-permute-start | bytes 1671176 | tf_op jit(solution)/shard_map/ppermute | solution.py:118
  31.5 4.7 %collective-permute-start.5 = (bf16[128,2176]{1,0:T(8,128)(2,1)S(1)}, bf16[128,2176]{1,0:T(8,128)(2,1)S(1)}, u32[]{:S(2)}, u32[]{:S(2)}) collective-permute-start(bf16[128,2176]{1,0:T(8,128)(2,1)S(1)} %hold.3.refs_1_.refs_3_), channel_id=1, source_target_pairs={{0,1},{1,0},{2,3},{3,2},{4,5},{5,4},{6,7},{7,6},{8,9},{9,8},{10,11... | collective-permute-start | bytes 1671176 | tf_op jit(solution)/shard_map/ppermute | solution.py:118
  34.1 6.7 %collective-permute-start.6 = (bf16[128,2176]{1,0:T(8,128)(2,1)S(1)}, bf16[128,2176]{1,0:T(8,128)(2,1)S(1)}, u32[]{:S(2)}, u32[]{:S(2)}) collective-permute-start(bf16[128,2176]{1,0:T(8,128)(2,1)S(1)} %collective-permute-done.refs_1_.refs_5_), channel_id=1, source_target_pairs={{0,1},{1,0},{2,3},{3,2},{4,5},{5,4},{6,7},{7,6},{8,9},{9,8},{10,11... | collective-permute-start | bytes 1671176 | tf_op jit(solution)/shard_map/ppermute | solution.py:118
  34.1 17.0 %collective-permute-start.1 = (bf16[128,2176]{1,0:T(8,128)(2,1)S(1)}, bf16[128,2176]{1,0:T(8,128)(2,1)S(1)}, u32[]{:S(2)}, u32[]{:S(2)}) collective-permute-start(bf16[128,2176]{1,0:T(8,128)(2,1)S(1)} %hold.2), channel_id=1, source_target_pairs={{2,4},{3,5},{4,2},{5,3},{10,12},{11,13},{12,10},{13,11},{18,20},{1... | collective-permute-start | bytes 1671176 | tf_op jit(solution)/shard_map/ppermute | solution.py:122
  34.8 16.9 %collective-permute-start.2 = (bf16[128,2176]{1,0:T(8,128)(2,1)S(1)}, bf16[128,2176]{1,0:T(8,128)(2,1)S(1)}, u32[]{:S(2)}, u32[]{:S(2)}) collective-permute-start(bf16[128,2176]{1,0:T(8,128)(2,1)S(1)} %collective-permute-done.refs_1_.refs_5_), channel_id=1, source_target_pairs={{2,0},{3,1},{4,6},{5,7},{10,8},{11,9},{12,14},{13,15},{18,16},{19,... | collective-permute-start | bytes 1671176 | tf_op jit(solution)/shard_map/ppermute | solution.py:122
  40.3 9.5 %collective-permute-start.7 = (bf16[128,2048]{1,0:T(8,128)(2,1)S(1)}, bf16[128,2048]{1,0:T(8,128)(2,1)S(1)}, u32[]{:S(2)}, u32[]{:S(2)}) collective-permute-start(bf16[128,2048]{1,0:T(8,128)(2,1)S(1)} %get-tuple-element.67), channel_id=1, source_target_pairs={{0,1},{1,0},{2,3},{3,2},{4,5},{5,4},{6,7},{7,6},{8,9},{9,8},{10,11... | collective-permute-start | bytes 1572872 | tf_op jit(solution)/shard_map/ppermute | solution.py:118
  44.8 5.6 %collective-permute-start.8 = (bf16[128,2048]{1,0:T(8,128)(2,1)S(1)}, bf16[128,2048]{1,0:T(8,128)(2,1)S(1)}, u32[]{:S(2)}, u32[]{:S(2)}) collective-permute-start(bf16[128,2048]{1,0:T(8,128)(2,1)S(1)} %get-tuple-element.70), channel_id=1, source_target_pairs={{0,1},{1,0},{2,3},{3,2},{4,5},{5,4},{6,7},{7,6},{8,9},{9,8},{10,11... | collective-permute-start | bytes 1572872 | tf_op jit(solution)/shard_map/ppermute | solution.py:118
  52.9 15.7 %collective-permute-start.14 = (bf16[128,2048]{1,0:T(8,128)(2,1)S(1)}, bf16[128,2048]{1,0:T(8,128)(2,1)S(1)}, u32[]{:S(2)}, u32[]{:S(2)}) collective-permute-start(bf16[128,2048]{1,0:T(8,128)(2,1)S(1)} %get-tuple-element.85), channel_id=1, source_target_pairs={{2,6},{3,7},{4,0},{5,1},{0,2},{1,3},{6,4},{7,5},{10,14},{11,15},{1... | collective-permute-start | bytes 1572872 | tf_op jit(solution)/shard_map/ppermute | solution.py:122
  63.3 5.2 %collective-permute-start.15 = (bf16[128,2048]{1,0:T(8,128)(2,1)S(1)}, bf16[128,2048]{1,0:T(8,128)(2,1)S(1)}, u32[]{:S(2)}, u32[]{:S(2)}) collective-permute-start(bf16[128,2048]{1,0:T(8,128)(2,1)S(1)} %get-tuple-element.88), channel_id=1, source_target_pairs={{0,1},{1,0},{2,3},{3,2},{4,5},{5,4},{6,7},{7,6},{8,9},{9,8},{10,11... | collective-permute-start | bytes 1572872 | tf_op jit(solution)/shard_map/ppermute | solution.py:118
  63.3 15.7 %collective-permute-start.18 = (bf16[2,128,1152]{2,1,0:T(8,128)(2,1)S(1)}, bf16[2,128,1152]{2,1,0:T(8,128)(2,1)S(1)}, u32[]{:S(2)}, u32[]{:S(2)}) collective-permute-start(bf16[2,128,1152]{2,1,0:T(8,128)(2,1)S(1)} %get-tuple-element.93), channel_id=1, source_target_pairs={{0,8},{8,0},{16,24},{24,16},{1,9},{9,1},{17,25},{25,17},{2,10},{10... | collective-permute-start | bytes 1769480 | tf_op jit(solution)/shard_map/ppermute | solution.py:118
  64.8 15.7 %collective-permute-start.19 = (bf16[2,128,1152]{2,1,0:T(8,128)(2,1)S(1)}, bf16[2,128,1152]{2,1,0:T(8,128)(2,1)S(1)}, u32[]{:S(2)}, u32[]{:S(2)}) collective-permute-start(bf16[2,128,1152]{2,1,0:T(8,128)(2,1)S(1)} %get-tuple-element.94), channel_id=1, source_target_pairs={{0,16},{8,24},{16,0},{24,8},{1,17},{9,25},{17,1},{25,9},{2,18},{10... | collective-permute-start | bytes 1769480 | tf_op jit(solution)/shard_map/ppermute | solution.py:118
  66.3 16.9 %collective-permute-start.13 = (bf16[128,2048]{1,0:T(8,128)(2,1)S(1)}, bf16[128,2048]{1,0:T(8,128)(2,1)S(1)}, u32[]{:S(2)}, u32[]{:S(2)}) collective-permute-start(bf16[128,2048]{1,0:T(8,128)(2,1)S(1)} %get-tuple-element.84), channel_id=1, source_target_pairs={{0,2},{1,3},{2,0},{3,1},{4,6},{5,7},{6,4},{7,5},{8,10},{9,11},{10,... | collective-permute-start | bytes 1572872 | tf_op jit(solution)/shard_map/ppermute | solution.py:118
  69.3 19.9 %collective-permute-start.16 = (bf16[128,1024]{1,0:T(8,128)(2,1)S(1)}, bf16[128,1024]{1,0:T(8,128)(2,1)S(1)}, u32[]{:S(2)}, u32[]{:S(2)}) collective-permute-start(bf16[128,1024]{1,0:T(8,128)(2,1)S(1)} %get-tuple-element.89), channel_id=1, source_target_pairs={{0,6},{1,7},{2,4},{3,5},{4,2},{5,3},{6,0},{7,1},{8,14},{9,15},{10,... | collective-permute-start | bytes 786440 | tf_op jit(solution)/shard_map/ppermute | solution.py:118
  71.6 22.0 %collective-permute-start.17 = (bf16[128,1024]{1,0:T(8,128)(2,1)S(1)}, bf16[128,1024]{1,0:T(8,128)(2,1)S(1)}, u32[]{:S(2)}, u32[]{:S(2)}) collective-permute-start(bf16[128,1024]{1,0:T(8,128)(2,1)S(1)} %get-tuple-element.90), channel_id=1, source_target_pairs={{0,6},{1,7},{2,4},{3,5},{4,2},{5,3},{6,0},{7,1},{8,14},{9,15},{10,... | collective-permute-start | bytes 786440 | tf_op jit(solution)/shard_map/ppermute | solution.py:118
  79.1 26.1 %collective-permute-start.10 = (bf16[2,128,1152]{2,1,0:T(8,128)(2,1)S(1)}, bf16[2,128,1152]{2,1,0:T(8,128)(2,1)S(1)}, u32[]{:S(2)}, u32[]{:S(2)}) collective-permute-start(bf16[2,128,1152]{2,1,0:T(8,128)(2,1)S(1)} %get-tuple-element.78), channel_id=1, source_target_pairs={{0,8},{8,0},{16,24},{24,16},{1,9},{9,1},{17,25},{25,17},{2,10},{10... | collective-permute-start | bytes 1769480 | tf_op jit(solution)/shard_map/ppermute | solution.py:118
  80.6 24.6 %collective-permute-start.11 = (bf16[2,128,1152]{2,1,0:T(8,128)(2,1)S(1)}, bf16[2,128,1152]{2,1,0:T(8,128)(2,1)S(1)}, u32[]{:S(2)}, u32[]{:S(2)}) collective-permute-start(bf16[2,128,1152]{2,1,0:T(8,128)(2,1)S(1)} %get-tuple-element.79), channel_id=1, source_target_pairs={{0,16},{8,24},{16,0},{24,8},{1,17},{9,25},{17,1},{25,9},{2,18},{10... | collective-permute-start | bytes 1769480 | tf_op jit(solution)/shard_map/ppermute | solution.py:118
  83.2 18.3 %collective-permute-start.20 = (bf16[128,1152]{1,0:T(8,128)(2,1)S(1)}, bf16[128,1152]{1,0:T(8,128)(2,1)S(1)}, u32[]{:S(2)}, u32[]{:S(2)}) collective-permute-start(bf16[128,1152]{1,0:T(8,128)(2,1)S(1)} %get-tuple-element.98), channel_id=1, source_target_pairs={{0,16},{8,24},{16,0},{24,8},{1,17},{9,25},{17,1},{25,9},{2,18},{10... | collective-permute-start | bytes 884744 | tf_op jit(solution)/shard_map/ppermute | solution.py:118
  89.3 12.3 %collective-permute-start.21 = (bf16[128,1152]{1,0:T(8,128)(2,1)S(1)}, bf16[128,1152]{1,0:T(8,128)(2,1)S(1)}, u32[]{:S(2)}, u32[]{:S(2)}) collective-permute-start(bf16[128,1152]{1,0:T(8,128)(2,1)S(1)} %get-tuple-element.99), channel_id=1, source_target_pairs={{0,8},{8,0},{16,24},{24,16},{1,9},{9,1},{17,25},{25,17},{2,10},{10... | collective-permute-start | bytes 884744 | tf_op jit(solution)/shard_map/ppermute | solution.py:118
  93.6 11.5 %collective-permute-start.12 = (bf16[128,2048]{1,0:T(8,128)(2,1)S(1)}, bf16[128,2048]{1,0:T(8,128)(2,1)S(1)}, u32[]{:S(2)}, u32[]{:S(2)}) collective-permute-start(bf16[128,2048]{1,0:T(8,128)(2,1)S(1)} %get-tuple-element.83), channel_id=1, source_target_pairs={{0,1},{1,0},{2,3},{3,2},{4,5},{5,4},{6,7},{7,6},{8,9},{9,8},{10,11... | collective-permute-start | bytes 1572872 | tf_op jit(solution)/shard_map/ppermute | solution.py:118
  102.7 27.3 %collective-permute-start.24 = (bf16[256,1152]{1,0:T(8,128)(2,1)S(1)}, bf16[256,1152]{1,0:T(8,128)(2,1)S(1)}, u32[]{:S(2)}, u32[]{:S(2)}) collective-permute-start(bf16[256,1152]{1,0:T(8,128)(2,1)S(1)} %get-tuple-element.105), channel_id=1, source_target_pairs={{0,4},{1,5},{2,6},{3,7},{4,0},{5,1},{6,2},{7,3},{8,12},{9,13},{10,... | collective-permute-start | bytes 1769480 | tf_op jit(solution)/shard_map/ppermute | solution.py:118
  106.9 6.9 %collective-permute-start.22 = (bf16[128,1152]{1,0:T(8,128)(2,1)S(1)}, bf16[128,1152]{1,0:T(8,128)(2,1)S(1)}, u32[]{:S(2)}, u32[]{:S(2)}) collective-permute-start(bf16[128,1152]{1,0:T(8,128)(2,1)S(1)} %get-tuple-element.103), channel_id=1, source_target_pairs={{0,16},{8,24},{16,0},{24,8},{1,17},{9,25},{17,1},{25,9},{2,18},{10... | collective-permute-start | bytes 884744 | tf_op jit(solution)/shard_map/ppermute | solution.py:118
  108.4 6.7 %collective-permute-start.23 = (bf16[128,1152]{1,0:T(8,128)(2,1)S(1)}, bf16[128,1152]{1,0:T(8,128)(2,1)S(1)}, u32[]{:S(2)}, u32[]{:S(2)}) collective-permute-start(bf16[128,1152]{1,0:T(8,128)(2,1)S(1)} %get-tuple-element.104), channel_id=1, source_target_pairs={{0,8},{8,0},{16,24},{24,16},{1,9},{9,1},{17,25},{25,17},{2,10},{10... | collective-permute-start | bytes 884744 | tf_op jit(solution)/shard_map/ppermute | solution.py:118
  (7 other events, 64.2 us)

commit v5 on v4

--- a/solution.py
+++ b/solution.py
@@ -427,7 +427,7 @@
     three_mixed, three_grad, done = line(3, got_two, cuts=2)
     end_a, end_b, own, _ = halves(*first, [], done)
     outs = [((2 * rows, columns), bf16), both]
-    leading, head, _ = call(lead_kernel, "lead_terms", at, (end_a, end_b, own, three_mixed, three_grad, got_one), outs, 0)
+    leading, head, _ = call(lead_kernel, "lead_terms", at, (end_a, end_b, own, three_mixed, three_grad), outs, 0)
     traded = swap_with(leading, "expert", n_expert // 2)
     more = [kept[0], other[0], got_one, got_two, three_mixed, three_grad]
     end_a, end_b, tail, (mixed, grad_tokens) = halves(*second, more)

time: 132 us -> 131 us (level)
  waiting for transfers between devices: 58.9 us -> 50.6 us
  starting transfers between devices: 28 us -> 34.6 us
    ppermute x22, waiting for transfers between devices: 58 us -> 47.8 us  [swap_with(): lax.ppermute(block, axis, [(i, i ^ mask) for i in range(lax.axis_size(axi...]
    ppermute x22, starting transfers between devices: 23.6 us -> 30.1 us  [swap_with(): lax.ppermute(block, axis, [(i, i ^ mask) for i in range(lax.axis_size(axi...]
    ppermute x3, waiting for transfers between devices: 0.85 us -> 2.74 us  [send(): lax.ppermute(block, 'expert', [(2 * a + c, 2 * b + c) for a, b in pairs f...]
  transfers between devices with their start and end apart: 25 -> 25, of which waited for: 11 -> 12; matrix products, arithmetic and copies ran while one was open for 2% -> 2% of each run, Pallas kernels for 23% -> 24%
where the time goes in v5:
time: 131 us; the launch traced here: 130 us
  waiting for transfers between devices  50.6 us (39%)
  Pallas kernels  36.6 us (28%)
  starting transfers between devices  34.6 us (26%)
  local copies, waits for them, and re-layouts  5.1 us (4%)
  between operations  2.06 us (2%)
  other arithmetic  1.48 us (1%)
    ppermute x22, waiting for transfers between devices, swap_with(): lax.ppermute(block, axis, [(i, i ^ mask) for i in range(lax.axis_size(axi...  47.8 us
    pallas_call x16, Pallas kernels, call(): pl.pallas_call(functools.partial(marked, kernel, 1 + len(operands) + len(...  34 us
    ppermute x22, starting transfers between devices, swap_with(): lax.ppermute(block, axis, [(i, i ^ mask) for i in range(lax.axis_size(axi...  30.1 us
    ppermute x3, starting transfers between devices, send(): lax.ppermute(block, 'expert', [(2 * a + c, 2 * b + c) for a, b in pairs f...  4.46 us
    unnamed x12, local copies, waits for them, and re-layouts  4.42 us
    ppermute x3, waiting for transfers between devices, send(): lax.ppermute(block, 'expert', [(2 * a + c, 2 * b + c) for a, b in pairs f...  2.74 us
  transfers between devices with their start and end apart: 25, of which 12 were waited for; matrix products, arithmetic and copies ran while one was open for 2% of the time, Pallas kernels for 24%

profile of v5, /device:TPU:0, one launch (start us, length us, event | category | flops | bytes accessed | tf_op | source)
XLA Modules:
  0.0 130.3 jit_solution(5094026226946843305)
XLA Ops:
  0.6 2.6 %message.1 = (bf16[128,2176]{1,0:T(8,128)(2,1)}, bf16[128,2176]{1,0:T(8,128)(2,1)}) custom-call(bf16[128,1024]{1,0:T(8,128)(2,1)} %tokens_ref.1, bf16[128,1024]{1,0:T(8,128)(2,1)} %cotangent_ref.1, s32[8,128]{1,0:T(8,128)} %bitcast.6, f32[8,128]{1,0:T(8,128)} %bitcast.7), custom_call_target="tpu_custom_call" | custom-call | bytes 1048576 | tf_op jit(solution)/shard_map/message/pallas_call | solution.py:155
  3.7 2.6 %collective-permute-start.4 = (bf16[128,2176]{1,0:T(8,128)(2,1)}, bf16[128,2176]{1,0:T(8,128)(2,1)S(1)}, u32[]{:S(2)}, u32[]{:S(2)}) collective-permute-start(bf16[128,2176]{1,0:T(8,128)(2,1)} %get-tuple-element.57.refs_1_), channel_id=1, source_target_pairs={{0,2},{1,3},{2,0},{3,1},{4,6},{5,7},{6,4},{7,5},{8,10},{9,11},{10,... | collective-permute-start | bytes 1671176 | tf_op jit(solution)/shard_map/ppermute | solution.py:118
  6.2 2.6 %collective-permute-start = (bf16[128,2176]{1,0:T(8,128)(2,1)}, bf16[128,2176]{1,0:T(8,128)(2,1)S(1)}, u32[]{:S(2)}, u32[]{:S(2)}) collective-permute-start(bf16[128,2176]{1,0:T(8,128)(2,1)} %get-tuple-element.57.refs_1_), channel_id=1, source_target_pairs={{0,4},{1,5},{2,6},{3,7},{4,0},{5,1},{6,2},{7,3},{8,12},{9,13},{10,... | collective-permute-start | bytes 1671176 | tf_op jit(solution)/shard_map/ppermute | solution.py:118
  12.3 1.9 %copy-done.1 = bf16[2,1024,768]{2,1,0:T(8,128)(2,1)S(1)} copy-done((bf16[2,1024,768]{2,1,0:T(8,128)(2,1)S(1)}, bf16[2,1024,768]{2,1,0:T(8,128)(2,1)}, u32[]{:S(2)}) %copy-start.1) | copy-done | bytes 3145752
  16.7 3.6 %near_block.3 = (bf16[2,256,384]{2,1,0:T(8,128)(2,1)S(1)}, bf16[2,256,768]{2,1,0:T(8,128)(2,1)S(1)}, bf16[128,2048]{1,0:T(8,128)(2,1)S(1)}, bf16[128,2048]{1,0:T(8,128)(2,1)S(1)}, f32[8,128]{1,0:T(8,128)S(1)}) custom-call(s32[5]{0:T(128)S(1)} %stack.28.refs_0_, bf16[128,2176]{1,0:T(8,128)(2,1)S(1)} %copy-done.5, ...), custom_call_target="tpu_custom_call" | custom-call | flops 4831838208 | tf_op jit(solution)/shard_map/near_block/pallas_call | solution.py:178
  20.3 11.3 %collective-permute-done.4.refs_0_ = bf16[128,2176]{1,0:T(8,128)(2,1)S(1)} collective-permute-done((bf16[128,2176]{1,0:T(8,128)(2,1)}, bf16[128,2176]{1,0:T(8,128)(2,1)S(1)}, u32[]{:S(2)}, u32[]{:S(2)}) %collective-permute-start.4) | collective-permute-done | bytes 557088 | tf_op jit(solution)/shard_map/ppermute | solution.py:118
  31.5 2.6 %collective-permute-done.refs_1_.refs_5_ = bf16[128,2176]{1,0:T(8,128)(2,1)S(1)} collective-permute-done((bf16[128,2176]{1,0:T(8,128)(2,1)}, bf16[128,2176]{1,0:T(8,128)(2,1)S(1)}, u32[]{:S(2)}, u32[]{:S(2)}) %collective-permute-start) | collective-permute-done | bytes 557088 | tf_op jit(solution)/shard_map/ppermute | solution.py:118
  36.3 4.0 %near_block.4 = (bf16[2,256,384]{2,1,0:T(8,128)(2,1)S(1)}, bf16[2,256,768]{2,1,0:T(8,128)(2,1)S(1)}, bf16[128,2048]{1,0:T(8,128)(2,1)S(1)}, bf16[128,2048]{1,0:T(8,128)(2,1)S(1)}, f32[8,128]{1,0:T(8,128)}) custom-call(s32[5]{0:T(128)S(1)} %stack.28.refs_0_, bf16[128,2176]{1,0:T(8,128)(2,1)S(1)} %hold.3.refs_1_.refs_3_, ...), custom_call_target="tpu_custom_call" | custom-call | flops 4831838208 | tf_op jit(solution)/shard_map/near_block/pallas_call | solution.py:178
  40.8 4.0 %near_block.5 = (bf16[2,256,384]{2,1,0:T(8,128)(2,1)S(1)}, bf16[2,256,768]{2,1,0:T(8,128)(2,1)S(1)}, bf16[128,2048]{1,0:T(8,128)(2,1)S(1)}, bf16[128,2048]{1,0:T(8,128)(2,1)S(1)}, f32[8,128]{1,0:T(8,128)}) custom-call(s32[5]{0:T(128)S(1)} %stack.28.refs_0_, bf16[128,2176]{1,0:T(8,128)(2,1)S(1)} %collective-permute-done.refs_1_.refs_5_, ...), custom_call_target="tpu_custom_call" | custom-call | flops 6039797760 | tf_op jit(solution)/shard_map/near_block/pallas_call | solution.py:178
  44.8 4.9 %early_terms.1 = (f32[4,256,1152]{2,1,0:T(8,128)S(1)}, f32[4,256,1152]{2,1,0:T(8,128)S(1)}, f32[8,128]{1,0:T(8,128)S(1)}) custom-call(s32[5]{0:T(128)S(1)} %stack.28.refs_0_, bf16[128,2176]{1,0:T(8,128)(2,1)S(1)} %copy-done.5, bf16[128,2176]{1,0:T(8,128)(2,1)S(1)} %collective-permute-done.3.refs_2_, bf16[128,2176]{1,0:T(8,128)(2,1)S(1)} %hold.3.refs_1_.refs_3_, ...), custom_call_target="tpu_custom_call" | custom-call | flops 10871635968 | tf_op jit(solution)/shard_map/early_terms/pallas_call | solution.py:178
  52.9 2.3 %collective-permute-start.14 = (bf16[128,2048]{1,0:T(8,128)(2,1)S(1)}, bf16[128,2048]{1,0:T(8,128)(2,1)S(1)}, u32[]{:S(2)}, u32[]{:S(2)}) collective-permute-start(bf16[128,2048]{1,0:T(8,128)(2,1)S(1)} %get-tuple-element.85), channel_id=1, source_target_pairs={{2,6},{3,7},{4,0},{5,1},{0,2},{1,3},{6,4},{7,5},{10,14},{11,15},{1... | collective-permute-start | bytes 1572872 | tf_op jit(solution)/shard_map/ppermute | solution.py:122
  55.2 2.8 %far_hidden.1 = (bf16[2,256,384]{2,1,0:T(8,128)(2,1)S(1)}, bf16[2,256,768]{2,1,0:T(8,128)(2,1)S(1)}, f32[8,128]{1,0:T(8,128)}) custom-call(s32[5]{0:T(128)S(1)} %stack.28.refs_0_, bf16[128,2176]{1,0:T(8,128)(2,1)S(1)} %get-tuple-element.72.refs_1_, bf16[128,2176]{1,0:T(8,128)(2,1)S(1)} %collective-permute-done.9.refs_2_, ...), custom_call_target="tpu_custom_call" | custom-call | flops 4831838208 | tf_op jit(solution)/shard_map/far_hidden/pallas_call | solution.py:178
  63.9 2.5 %far_results.1 = (bf16[128,2048]{1,0:T(8,128)(2,1)S(1)}, bf16[128,2048]{1,0:T(8,128)(2,1)S(1)}, f32[8,128]{1,0:T(8,128)}) custom-call(s32[5]{0:T(128)S(1)} %stack.28.refs_0_, bf16[2,256,384]{2,1,0:T(8,128)(2,1)S(1)} %get-tuple-element.74.refs_4_.refs_1_, bf16[2,256,768]{2,1,0:T(8,128)(2,1)S(1)} %get-tuple-element.73.refs_3_.refs_2_, ...), custom_call_target="tpu_custom_call" | custom-call | flops 4831838208 | tf_op jit(solution)/shard_map/far_results/pallas_call | solution.py:178
  66.4 2.1 %collective-permute-done.14.refs_3_.refs_8_ = bf16[128,2048]{1,0:T(8,128)(2,1)S(1)} collective-permute-done((bf16[128,2048]{1,0:T(8,128)(2,1)S(1)}, bf16[128,2048]{1,0:T(8,128)(2,1)S(1)}, u32[]{:S(2)}, u32[]{:S(2)}) %collective-permute-start.14) | collective-permute-done | bytes 524320 | tf_op jit(solution)/shard_map/ppermute | solution.py:122
  69.3 2.3 %collective-permute-start.16 = (bf16[128,1024]{1,0:T(8,128)(2,1)S(1)}, bf16[128,1024]{1,0:T(8,128)(2,1)S(1)}, u32[]{:S(2)}, u32[]{:S(2)}) collective-permute-start(bf16[128,1024]{1,0:T(8,128)(2,1)S(1)} %get-tuple-element.89), channel_id=1, source_target_pairs={{0,6},{1,7},{2,4},{3,5},{4,2},{5,3},{6,0},{7,1},{8,14},{9,15},{10,... | collective-permute-start | bytes 786440 | tf_op jit(solution)/shard_map/ppermute | solution.py:118
  71.6 3.1 %collective-permute-done.18.refs_1_ = bf16[2,128,1152]{2,1,0:T(8,128)(2,1)S(1)} collective-permute-done((bf16[2,128,1152]{2,1,0:T(8,128)(2,1)S(1)}, bf16[2,128,1152]{2,1,0:T(8,128)(2,1)S(1)}, u32[]{:S(2)}, u32[]{:S(2)}) %collective-permute-start.18) | collective-permute-done | bytes 589856 | tf_op jit(solution)/shard_map/ppermute | solution.py:118
  78.5 2.5 %collective-permute-start.17 = (bf16[128,1024]{1,0:T(8,128)(2,1)S(1)}, bf16[128,1024]{1,0:T(8,128)(2,1)S(1)}, u32[]{:S(2)}, u32[]{:S(2)}) collective-permute-start(bf16[128,1024]{1,0:T(8,128)(2,1)S(1)} %get-tuple-element.90), channel_id=1, source_target_pairs={{0,6},{1,7},{2,4},{3,5},{4,2},{5,3},{6,0},{7,1},{8,14},{9,15},{10,... | collective-permute-start | bytes 786440 | tf_op jit(solution)/shard_map/ppermute | solution.py:118
  83.5 3.7 %collective-permute-done.17.refs_10_.refs_5_ = bf16[128,1024]{1,0:T(8,128)(2,1)S(1)} collective-permute-done((bf16[128,1024]{1,0:T(8,128)(2,1)S(1)}, bf16[128,1024]{1,0:T(8,128)(2,1)S(1)}, u32[]{:S(2)}, u32[]{:S(2)}) %collective-permute-start.17) | collective-permute-done | bytes 262176 | tf_op jit(solution)/shard_map/ppermute | solution.py:118
  87.2 8.9 %collective-permute-start.13 = (bf16[128,2048]{1,0:T(8,128)(2,1)S(1)}, bf16[128,2048]{1,0:T(8,128)(2,1)S(1)}, u32[]{:S(2)}, u32[]{:S(2)}) collective-permute-start(bf16[128,2048]{1,0:T(8,128)(2,1)S(1)} %get-tuple-element.84), channel_id=1, source_target_pairs={{0,2},{1,3},{2,0},{3,1},{4,6},{5,7},{6,4},{7,5},{8,10},{9,11},{10,... | collective-permute-start | bytes 1572872 | tf_op jit(solution)/shard_map/ppermute | solution.py:118
  96.1 4.8 %collective-permute-done.21.refs_2_ = bf16[128,1152]{1,0:T(8,128)(2,1)S(1)} collective-permute-done((bf16[128,1152]{1,0:T(8,128)(2,1)S(1)}, bf16[128,1152]{1,0:T(8,128)(2,1)S(1)}, u32[]{:S(2)}, u32[]{:S(2)}) %collective-permute-start.21) | collective-permute-done | bytes 294944 | tf_op jit(solution)/shard_map/ppermute | solution.py:118
  103.2 13.6 %collective-permute-done.13.refs_7_ = bf16[128,2048]{1,0:T(8,128)(2,1)S(1)} collective-permute-done((bf16[128,2048]{1,0:T(8,128)(2,1)S(1)}, bf16[128,2048]{1,0:T(8,128)(2,1)S(1)}, u32[]{:S(2)}, u32[]{:S(2)}) %collective-permute-start.13) | collective-permute-done | bytes 524320 | tf_op jit(solution)/shard_map/ppermute | solution.py:118
  116.8 1.7 %pair_terms.2 = (bf16[128,1152]{1,0:T(8,128)(2,1)S(1)}, bf16[128,1152]{1,0:T(8,128)(2,1)S(1)}, f32[2,128,1152]{2,1,0:T(8,128)S(1)}, bf16[128,1024]{1,0:T(8,128)(...) custom-call(s32[5]{0:T(128)S(1)} %stack.28.refs_0_, bf16[2,128,1152]{2,1,0:T(8,128)(2,1)S(1)} %collective-permute-done.10.refs_1_, ...), custom_call_target="tpu_custom_call" | custom-call | tf_op jit(solution)/shard_map/pair_terms/pallas_call | solution.py:178
  120.5 6.8 %collective-permute-done.22.refs_3_ = bf16[128,1152]{1,0:T(8,128)(2,1)S(1)} collective-permute-done((bf16[128,1152]{1,0:T(8,128)(2,1)S(1)}, bf16[128,1152]{1,0:T(8,128)(2,1)S(1)}, u32[]{:S(2)}, u32[]{:S(2)}) %collective-permute-start.22) | collective-permute-done | bytes 294944 | tf_op jit(solution)/shard_map/ppermute | solution.py:118
  128.2 2.2 %finish.1 = (f32[2,256,768]{2,1,0:T(8,128)}, f32[2,256,384]{2,1,0:T(8,128)}, f32[8,128]{1,0:T(8,128)}) custom-call(s32[5]{0:T(128)S(1)} %stack.28.refs_0_, f32[2,128,1152]{2,1,0:T(8,128)S(1)} %get-tuple-element.101.refs_1_, f32[2,128,1152]{2,1,0:T(8,128)S(1)} %get-tuple-element.102.refs_2_, bf16[128,1152]{1,0:T(8,128)(2,1)S(1)} %collective-permute-done.22.refs_3_, ...), custom_call_target="tpu_custom_call" | custom-call | tf_op jit(solution)/shard_map/finish/pallas_call | solution.py:178
  (62 shorter events, 29.3 us)
Async XLA Ops:
  3.2 9.1 %collective-permute-start.3 = (bf16[128,2176]{1,0:T(8,128)(2,1)}, bf16[128,2176]{1,0:T(8,128)(2,1)S(1)}, u32[]{:S(2)}, u32[]{:S(2)}) collective-permute-start(bf16[128,2176]{1,0:T(8,128)(2,1)} %get-tuple-element.57.refs_1_), channel_id=1, source_target_pairs={{0,1},{1,0},{2,3},{3,2},{4,5},{5,4},{6,7},{7,6},{8,9},{9,8},{10,11... | collective-permute-start | bytes 1671176 | tf_op jit(solution)/shard_map/ppermute | solution.py:118
  3.7 27.9 %collective-permute-start.4 = (bf16[128,2176]{1,0:T(8,128)(2,1)}, bf16[128,2176]{1,0:T(8,128)(2,1)S(1)}, u32[]{:S(2)}, u32[]{:S(2)}) collective-permute-start(bf16[128,2176]{1,0:T(8,128)(2,1)} %get-tuple-element.57.refs_1_), channel_id=1, source_target_pairs={{0,2},{1,3},{2,0},{3,1},{4,6},{5,7},{6,4},{7,5},{8,10},{9,11},{10,... | collective-permute-start | bytes 1671176 | tf_op jit(solution)/shard_map/ppermute | solution.py:118
  6.2 27.9 %collective-permute-start = (bf16[128,2176]{1,0:T(8,128)(2,1)}, bf16[128,2176]{1,0:T(8,128)(2,1)S(1)}, u32[]{:S(2)}, u32[]{:S(2)}) collective-permute-start(bf16[128,2176]{1,0:T(8,128)(2,1)} %get-tuple-element.57.refs_1_), channel_id=1, source_target_pairs={{0,4},{1,5},{2,6},{3,7},{4,0},{5,1},{6,2},{7,3},{8,12},{9,13},{10,... | collective-permute-start | bytes 1671176 | tf_op jit(solution)/shard_map/ppermute | solution.py:118
  31.5 4.7 %collective-permute-start.5 = (bf16[128,2176]{1,0:T(8,128)(2,1)S(1)}, bf16[128,2176]{1,0:T(8,128)(2,1)S(1)}, u32[]{:S(2)}, u32[]{:S(2)}) collective-permute-start(bf16[128,2176]{1,0:T(8,128)(2,1)S(1)} %hold.3.refs_1_.refs_3_), channel_id=1, source_target_pairs={{0,1},{1,0},{2,3},{3,2},{4,5},{5,4},{6,7},{7,6},{8,9},{9,8},{10,11... | collective-permute-start | bytes 1671176 | tf_op jit(solution)/shard_map/ppermute | solution.py:118
  34.1 6.7 %collective-permute-start.6 = (bf16[128,2176]{1,0:T(8,128)(2,1)S(1)}, bf16[128,2176]{1,0:T(8,128)(2,1)S(1)}, u32[]{:S(2)}, u32[]{:S(2)}) collective-permute-start(bf16[128,2176]{1,0:T(8,128)(2,1)S(1)} %collective-permute-done.refs_1_.refs_5_), channel_id=1, source_target_pairs={{0,1},{1,0},{2,3},{3,2},{4,5},{5,4},{6,7},{7,6},{8,9},{9,8},{10,11... | collective-permute-start | bytes 1671176 | tf_op jit(solution)/shard_map/ppermute | solution.py:118
  34.1 17.0 %collective-permute-start.1 = (bf16[128,2176]{1,0:T(8,128)(2,1)S(1)}, bf16[128,2176]{1,0:T(8,128)(2,1)S(1)}, u32[]{:S(2)}, u32[]{:S(2)}) collective-permute-start(bf16[128,2176]{1,0:T(8,128)(2,1)S(1)} %hold.2), channel_id=1, source_target_pairs={{2,4},{3,5},{4,2},{5,3},{10,12},{11,13},{12,10},{13,11},{18,20},{1... | collective-permute-start | bytes 1671176 | tf_op jit(solution)/shard_map/ppermute | solution.py:122
  34.8 16.9 %collective-permute-start.2 = (bf16[128,2176]{1,0:T(8,128)(2,1)S(1)}, bf16[128,2176]{1,0:T(8,128)(2,1)S(1)}, u32[]{:S(2)}, u32[]{:S(2)}) collective-permute-start(bf16[128,2176]{1,0:T(8,128)(2,1)S(1)} %collective-permute-done.refs_1_.refs_5_), channel_id=1, source_target_pairs={{2,0},{3,1},{4,6},{5,7},{10,8},{11,9},{12,14},{13,15},{18,16},{19,... | collective-permute-start | bytes 1671176 | tf_op jit(solution)/shard_map/ppermute | solution.py:122
  40.3 9.5 %collective-permute-start.7 = (bf16[128,2048]{1,0:T(8,128)(2,1)S(1)}, bf16[128,2048]{1,0:T(8,128)(2,1)S(1)}, u32[]{:S(2)}, u32[]{:S(2)}) collective-permute-start(bf16[128,2048]{1,0:T(8,128)(2,1)S(1)} %get-tuple-element.67), channel_id=1, source_target_pairs={{0,1},{1,0},{2,3},{3,2},{4,5},{5,4},{6,7},{7,6},{8,9},{9,8},{10,11... | collective-permute-start | bytes 1572872 | tf_op jit(solution)/shard_map/ppermute | solution.py:118
  44.8 5.6 %collective-permute-start.8 = (bf16[128,2048]{1,0:T(8,128)(2,1)S(1)}, bf16[128,2048]{1,0:T(8,128)(2,1)S(1)}, u32[]{:S(2)}, u32[]{:S(2)}) collective-permute-start(bf16[128,2048]{1,0:T(8,128)(2,1)S(1)} %get-tuple-element.70), channel_id=1, source_target_pairs={{0,1},{1,0},{2,3},{3,2},{4,5},{5,4},{6,7},{7,6},{8,9},{9,8},{10,11... | collective-permute-start | bytes 1572872 | tf_op jit(solution)/shard_map/ppermute | solution.py:118
  52.9 2.3 %collective-permute-start.9 = (bf16[128,2176]{1,0:T(8,128)(2,1)S(1)}, bf16[128,2176]{1,0:T(8,128)(2,1)S(1)}, u32[]{:S(2)}, u32[]{:S(2)}) collective-permute-start(bf16[128,2176]{1,0:T(8,128)(2,1)S(1)} %get-tuple-element.72.refs_1_), channel_id=1, source_target_pairs={{0,1},{1,0},{2,3},{3,2},{4,5},{5,4},{6,7},{7,6},{8,9},{9,8},{10,11... | collective-permute-start | bytes 1671176 | tf_op jit(solution)/shard_map/ppermute | solution.py:118
  52.9 15.7 %collective-permute-start.14 = (bf16[128,2048]{1,0:T(8,128)(2,1)S(1)}, bf16[128,2048]{1,0:T(8,128)(2,1)S(1)}, u32[]{:S(2)}, u32[]{:S(2)}) collective-permute-start(bf16[128,2048]{1,0:T(8,128)(2,1)S(1)} %get-tuple-element.85), channel_id=1, source_target_pairs={{2,6},{3,7},{4,0},{5,1},{0,2},{1,3},{6,4},{7,5},{10,14},{11,15},{1... | collective-permute-start | bytes 1572872 | tf_op jit(solution)/shard_map/ppermute | solution.py:122
  59.4 15.3 %collective-permute-start.18 = (bf16[2,128,1152]{2,1,0:T(8,128)(2,1)S(1)}, bf16[2,128,1152]{2,1,0:T(8,128)(2,1)S(1)}, u32[]{:S(2)}, u32[]{:S(2)}) collective-permute-start(bf16[2,128,1152]{2,1,0:T(8,128)(2,1)S(1)} %get-tuple-element.93), channel_id=1, source_target_pairs={{0,8},{8,0},{16,24},{24,16},{1,9},{9,1},{17,25},{25,17},{2,10},{10... | collective-permute-start | bytes 1769480 | tf_op jit(solution)/shard_map/ppermute | solution.py:118
  60.9 15.0 %collective-permute-start.19 = (bf16[2,128,1152]{2,1,0:T(8,128)(2,1)S(1)}, bf16[2,128,1152]{2,1,0:T(8,128)(2,1)S(1)}, u32[]{:S(2)}, u32[]{:S(2)}) collective-permute-start(bf16[2,128,1152]{2,1,0:T(8,128)(2,1)S(1)} %get-tuple-element.94), channel_id=1, source_target_pairs={{0,16},{8,24},{16,0},{24,8},{1,17},{9,25},{17,1},{25,9},{2,18},{10... | collective-permute-start | bytes 1769480 | tf_op jit(solution)/shard_map/ppermute | solution.py:118
  69.3 12.7 %collective-permute-start.16 = (bf16[128,1024]{1,0:T(8,128)(2,1)S(1)}, bf16[128,1024]{1,0:T(8,128)(2,1)S(1)}, u32[]{:S(2)}, u32[]{:S(2)}) collective-permute-start(bf16[128,1024]{1,0:T(8,128)(2,1)S(1)} %get-tuple-element.89), channel_id=1, source_target_pairs={{0,6},{1,7},{2,4},{3,5},{4,2},{5,3},{6,0},{7,1},{8,14},{9,15},{10,... | collective-permute-start | bytes 786440 | tf_op jit(solution)/shard_map/ppermute | solution.py:118
  77.0 10.2 %collective-permute-start.20 = (bf16[128,1152]{1,0:T(8,128)(2,1)S(1)}, bf16[128,1152]{1,0:T(8,128)(2,1)S(1)}, u32[]{:S(2)}, u32[]{:S(2)}) collective-permute-start(bf16[128,1152]{1,0:T(8,128)(2,1)S(1)} %get-tuple-element.98), channel_id=1, source_target_pairs={{0,16},{8,24},{16,0},{24,8},{1,17},{9,25},{17,1},{25,9},{2,18},{10... | collective-permute-start | bytes 884744 | tf_op jit(solution)/shard_map/ppermute | solution.py:118
  78.5 8.7 %collective-permute-start.17 = (bf16[128,1024]{1,0:T(8,128)(2,1)S(1)}, bf16[128,1024]{1,0:T(8,128)(2,1)S(1)}, u32[]{:S(2)}, u32[]{:S(2)}) collective-permute-start(bf16[128,1024]{1,0:T(8,128)(2,1)S(1)} %get-tuple-element.90), channel_id=1, source_target_pairs={{0,6},{1,7},{2,4},{3,5},{4,2},{5,3},{6,0},{7,1},{8,14},{9,15},{10,... | collective-permute-start | bytes 786440 | tf_op jit(solution)/shard_map/ppermute | solution.py:118
  81.0 35.8 %collective-permute-start.10 = (bf16[2,128,1152]{2,1,0:T(8,128)(2,1)S(1)}, bf16[2,128,1152]{2,1,0:T(8,128)(2,1)S(1)}, u32[]{:S(2)}, u32[]{:S(2)}) collective-permute-start(bf16[2,128,1152]{2,1,0:T(8,128)(2,1)S(1)} %get-tuple-element.78), channel_id=1, source_target_pairs={{0,8},{8,0},{16,24},{24,16},{1,9},{9,1},{17,25},{25,17},{2,10},{10... | collective-permute-start | bytes 1769480 | tf_op jit(solution)/shard_map/ppermute | solution.py:118
  81.5 35.2 %collective-permute-start.11 = (bf16[2,128,1152]{2,1,0:T(8,128)(2,1)S(1)}, bf16[2,128,1152]{2,1,0:T(8,128)(2,1)S(1)}, u32[]{:S(2)}, u32[]{:S(2)}) collective-permute-start(bf16[2,128,1152]{2,1,0:T(8,128)(2,1)S(1)} %get-tuple-element.79), channel_id=1, source_target_pairs={{0,16},{8,24},{16,0},{24,8},{1,17},{9,25},{17,1},{25,9},{2,18},{10... | collective-permute-start | bytes 1769480 | tf_op jit(solution)/shard_map/ppermute | solution.py:118
  82.1 18.8 %collective-permute-start.21 = (bf16[128,1152]{1,0:T(8,128)(2,1)S(1)}, bf16[128,1152]{1,0:T(8,128)(2,1)S(1)}, u32[]{:S(2)}, u32[]{:S(2)}) collective-permute-start(bf16[128,1152]{1,0:T(8,128)(2,1)S(1)} %get-tuple-element.99), channel_id=1, source_target_pairs={{0,8},{8,0},{16,24},{24,16},{1,9},{9,1},{17,25},{25,17},{2,10},{10... | collective-permute-start | bytes 884744 | tf_op jit(solution)/shard_map/ppermute | solution.py:118
  87.2 16.0 %collective-permute-start.12 = (bf16[128,2048]{1,0:T(8,128)(2,1)S(1)}, bf16[128,2048]{1,0:T(8,128)(2,1)S(1)}, u32[]{:S(2)}, u32[]{:S(2)}) collective-permute-start(bf16[128,2048]{1,0:T(8,128)(2,1)S(1)} %get-tuple-element.83), channel_id=1, source_target_pairs={{0,1},{1,0},{2,3},{3,2},{4,5},{5,4},{6,7},{7,6},{8,9},{9,8},{10,11... | collective-permute-start | bytes 1572872 | tf_op jit(solution)/shard_map/ppermute | solution.py:118
  87.2 29.6 %collective-permute-start.13 = (bf16[128,2048]{1,0:T(8,128)(2,1)S(1)}, bf16[128,2048]{1,0:T(8,128)(2,1)S(1)}, u32[]{:S(2)}, u32[]{:S(2)}) collective-permute-start(bf16[128,2048]{1,0:T(8,128)(2,1)S(1)} %get-tuple-element.84), channel_id=1, source_target_pairs={{0,2},{1,3},{2,0},{3,1},{4,6},{5,7},{6,4},{7,5},{8,10},{9,11},{10,... | collective-permute-start | bytes 1572872 | tf_op jit(solution)/shard_map/ppermute | solution.py:118
  102.0 26.2 %collective-permute-start.24 = (bf16[256,1152]{1,0:T(8,128)(2,1)S(1)}, bf16[256,1152]{1,0:T(8,128)(2,1)S(1)}, u32[]{:S(2)}, u32[]{:S(2)}) collective-permute-start(bf16[256,1152]{1,0:T(8,128)(2,1)S(1)} %get-tuple-element.105), channel_id=1, source_target_pairs={{0,4},{1,5},{2,6},{3,7},{4,0},{5,1},{6,2},{7,3},{8,12},{9,13},{10,... | collective-permute-start | bytes 1769480 | tf_op jit(solution)/shard_map/ppermute | solution.py:118
  118.4 8.8 %collective-permute-start.22 = (bf16[128,1152]{1,0:T(8,128)(2,1)S(1)}, bf16[128,1152]{1,0:T(8,128)(2,1)S(1)}, u32[]{:S(2)}, u32[]{:S(2)}) collective-permute-start(bf16[128,1152]{1,0:T(8,128)(2,1)S(1)} %get-tuple-element.103), channel_id=1, source_target_pairs={{0,16},{8,24},{16,0},{24,8},{1,17},{9,25},{17,1},{25,9},{2,18},{10... | collective-permute-start | bytes 884744 | tf_op jit(solution)/shard_map/ppermute | solution.py:118
  119.0 8.6 %collective-permute-start.23 = (bf16[128,1152]{1,0:T(8,128)(2,1)S(1)}, bf16[128,1152]{1,0:T(8,128)(2,1)S(1)}, u32[]{:S(2)}, u32[]{:S(2)}) collective-permute-start(bf16[128,1152]{1,0:T(8,128)(2,1)S(1)} %get-tuple-element.104), channel_id=1, source_target_pairs={{0,8},{8,0},{16,24},{24,16},{1,9},{9,1},{17,25},{25,17},{2,10},{10... | collective-permute-start | bytes 884744 | tf_op jit(solution)/shard_map/ppermute | solution.py:118
  (7 other events, 64.1 us)
